TPU v7x, 32 devices: a whole 2x2x4 slice. The times are simulated.
32 devices in a mesh: gx: 4 (over x, core), gy: 8 (over z, y).
Axes of the slice: x: 2, y: 2, z: 4, core: 2. Of those that a mesh axis runs over, the one named last changes fastest.
Arguments:
- fine_latent: bfloat16 [128, 1024, 256], P('gx', 'gy'), may hold values from -6 to 6
- nbr_dir: int32 [128, 6, 1024], P('gx', None, 'gy'), may hold values from 0 to 7
- nbr_mask: int32 [128, 6, 1024], P('gx', None, 'gy'), may hold values 0 or 1
- dir_embed: bfloat16 [8, 256], replicated, may hold values from -6 to 6
- w_center: bfloat16 [256, 256], replicated, may hold values from -0.375 to 0.375
- w_neighbour: bfloat16 [256, 256], replicated, may hold values from -0.375 to 0.375
- w_msg: bfloat16 [256, 256], replicated, may hold values from -0.375 to 0.375
- w_node_in: bfloat16 [512, 256], replicated, may hold values from -0.25 to 0.25
- w_node_out: bfloat16 [256, 256], replicated, may hold values from -0.375 to 0.375
- restrict_weight: bfloat16 [8, 128, 32, 128], P('gy', 'gx'), may hold values from -0.25 to 0.25
- cluster_host: int32 [8, 128, 1], P('gy', 'gx'), may hold values from 0 to 7; in each aligned block of 32 rows (0 to 31, 32 to 63, ..., all dimensions but the last counted through in order) at most 8 rows name the same one
- cluster_slot: int32 [8, 128], P('gy', 'gx'), may hold values from 0 to 7
- coarse_src: int32 [8192, 6], P(('gx', 'gy')), may hold values from 0 to 8191, as said below
- a_src: bfloat16 [256, 256], replicated, may hold values from -0.375 to 0.375
- a_dst: bfloat16 [256, 256], replicated, may hold values from -0.375 to 0.375
- a_msg: bfloat16 [256, 256], replicated, may hold values from -0.375 to 0.375
- b_in: bfloat16 [512, 256], replicated, may hold values from -0.25 to 0.25
- b_out: bfloat16 [256, 256], replicated, may hold values from -0.375 to 0.375
Outputs:
- fine_out: bfloat16 [128, 1024, 256], P('gx', 'gy')
Inputs may be any that keep to these rules, and one draw needn't show every extreme that they name: `cluster_host`: among the 32 blocks of one device at most 8 name the same host; some device's blocks name one host exactly 8 times. coarse_src[n, j] lies in the strip of 2048 coarse rows that holds n, or in the next strip; rows of the last of the 4 strips take sources from their own strip only.
All inputs are finite; a program needn't handle non-finite values. No bound on the sum of `nbr_mask` on one device may be relied on, other than what follows from the above.
Results may differ from a plain program's by a relative error of at most 0.009.
Values may be sent and summed in bfloat16 or wider, within the bound.
No kernel may reach another device: no remote copies, remote signals or barrier semaphores. Data moves between devices by JAX's collectives and lax.ppermute only.
A program may use at most 64 MiB of HBM per device.

v0:
```python
import jax
import jax.numpy as jnp
from jax import lax
from jax.sharding import PartitionSpec as P

STEP_X = (-1, -1, -1, 0, 0, 1, 1, 1)
STEP_Y = (-1, 0, 1, -1, 1, -1, 0, 1)


def padded(block, sides, width):
    for axis, dim in sides:
        count = lax.axis_size(axis)
        forward = [(i, i + 1) for i in range(count - 1)]
        backward = [(target, source) for source, target in forward]
        low = lax.ppermute(
            lax.slice_in_dim(block, block.shape[dim] - width, None, axis=dim), axis, forward
        )
        high = lax.ppermute(lax.slice_in_dim(block, 0, width, axis=dim), axis, backward)
        block = jnp.concatenate([low, block, high], axis=dim)
    return block


def passed_along(value, axis, steps):
    count = lax.axis_size(axis)
    initial, last = (max(0, -steps), min(count, count - steps))
    return lax.ppermute(value, axis, [(source, source + steps) for source in range(initial, last)])


def coarse_update(coarse_rows, sources, source_table, strip_base, a_dst, a_msg, b_in, b_out):
    row_total, feature_width = coarse_rows.shape
    degree = sources.shape[1]
    dest_proj = jnp.dot(coarse_rows, a_dst, preferred_element_type=jnp.float32)
    local_index = (sources - strip_base).reshape(-1)
    gathered = jnp.take(source_table, local_index, axis=0, mode="clip").reshape(
        row_total, degree, feature_width
    )
    hidden = jax.nn.relu(gathered.astype(jnp.float32) + dest_proj[:, None, :]).astype(jnp.bfloat16)
    messages = jnp.dot(
        hidden.reshape(row_total * degree, feature_width), a_msg, preferred_element_type=jnp.float32
    )
    summed = jnp.sum(messages.reshape(row_total, degree, feature_width), axis=1).astype(
        jnp.bfloat16
    )
    joined = jnp.concatenate([coarse_rows, summed], axis=1)
    node_hidden = jax.nn.relu(jnp.dot(joined, b_in, preferred_element_type=jnp.float32)).astype(
        jnp.bfloat16
    )
    return (
        coarse_rows.astype(jnp.float32)
        + jnp.dot(node_hidden, b_out, preferred_element_type=jnp.float32)
    ).astype(jnp.bfloat16)


def per_device(
    fine_latent,
    nbr_dir,
    nbr_mask,
    dir_embed,
    w_center,
    w_neighbour,
    w_msg,
    w_node_in,
    w_node_out,
    restrict_weight,
    cluster_host,
    cluster_slot,
    coarse_src,
    a_src,
    a_dst,
    a_msg,
    b_in,
    b_out,
):
    cells_x, cells_y, feature_width = fine_latent.shape
    flattened = fine_latent.reshape(cells_x * cells_y, feature_width)
    center = jnp.dot(flattened, w_center, preferred_element_type=jnp.float32).reshape(
        cells_x, cells_y, feature_width
    )
    neighbour_proj = jnp.dot(flattened, w_neighbour, preferred_element_type=jnp.float32).astype(
        jnp.bfloat16
    )
    extended = padded(
        neighbour_proj.reshape(cells_x, cells_y, feature_width), (("gx", 0), ("gy", 1)), 1
    )
    live_slots = nbr_mask.astype(jnp.float32)
    embedding = dir_embed.astype(jnp.float32)
    aggregate = jnp.zeros((cells_x, cells_y, feature_width), jnp.float32)
    for direction in range(8):
        counts = jnp.sum(jnp.where(nbr_dir == direction, live_slots, 0.0), axis=1)
        low_x = 1 + STEP_X[direction]
        low_y = 1 + STEP_Y[direction]
        shifted = lax.slice(
            extended, (low_x, low_y, 0), (low_x + cells_x, low_y + cells_y, feature_width)
        )
        hidden = jax.nn.relu(center + shifted.astype(jnp.float32) + embedding[direction]).astype(
            jnp.bfloat16
        )
        message = jnp.dot(
            hidden.reshape(-1, feature_width), w_msg, preferred_element_type=jnp.float32
        )
        aggregate = aggregate + counts[:, :, None] * message.reshape(
            cells_x, cells_y, feature_width
        )
    joined = jnp.concatenate(
        [flattened, aggregate.reshape(-1, feature_width).astype(jnp.bfloat16)], axis=1
    )
    node_hidden = jax.nn.relu(
        jnp.dot(joined, w_node_in, preferred_element_type=jnp.float32)
    ).astype(jnp.bfloat16)
    refined = (
        flattened.astype(jnp.float32)
        + jnp.dot(node_hidden, w_node_out, preferred_element_type=jnp.float32)
    ).astype(jnp.bfloat16)
    blocks = refined.reshape(cells_x, cells_y, feature_width)
    weights = restrict_weight[0]
    restricted = jnp.einsum("brc,bcl->brl", weights, blocks, preferred_element_type=jnp.float32)
    block_count, cluster_rows, _ = restricted.shape
    flat_restricted = restricted.reshape(block_count, cluster_rows * feature_width)
    host_count = lax.axis_size("gy")
    per_host = block_count // 4
    host_rows = per_host * cluster_rows
    block_hosts = cluster_host[0, :, 0]
    block_slots = cluster_slot[0]
    cluster = block_hosts * per_host + block_slots
    number = lax.axis_size("gy") * host_rows // cluster_rows
    wanted = jnp.arange(number, dtype=jnp.int32)[:, None]
    selector = (cluster[None, :] == wanted).astype(jnp.float32)
    partial_term = jnp.dot(
        selector,
        flat_restricted,
        preferred_element_type=jnp.float32,
        precision=lax.Precision.HIGHEST,
    )
    coarse_in = lax.psum_scatter(
        partial_term.reshape(lax.axis_size("gy") * host_rows, feature_width),
        "gy",
        scatter_dimension=0,
        tiled=True,
    ).astype(jnp.bfloat16)
    source_proj = jnp.dot(coarse_in, a_src, preferred_element_type=jnp.float32).astype(jnp.bfloat16)
    strip_rows = lax.all_gather(source_proj, "gy", axis=0, tiled=True)
    next_rows = passed_along(strip_rows, "gx", -1)
    source_table = jnp.concatenate([strip_rows, next_rows], axis=0)
    strip_base = lax.axis_index("gx") * strip_rows.shape[0]
    group_place = lax.axis_index("gy") % 4
    group_rows = [coarse_in]
    group_sources = [coarse_src]
    for member in range(1, 4):
        member_rows, member_sources = passed_along((coarse_in, coarse_src), "gy", -member)
        group_rows.append(member_rows)
        group_sources.append(member_sources)
    group_out = coarse_update(
        jnp.concatenate(group_rows, axis=0),
        jnp.concatenate(group_sources, axis=0),
        source_table,
        strip_base,
        a_dst,
        a_msg,
        b_in,
        b_out,
    )
    coarse_out = group_out[:host_rows]
    for member in range(1, 4):
        returned_rows = passed_along(
            group_out[member * host_rows : (member + 1) * host_rows], "gy", member
        )
        coarse_out = jnp.where(group_place == member, returned_rows, coarse_out)
    strip_out = lax.all_gather(coarse_out, "gy", axis=0, tiled=True)
    selector = (
        cluster[:, None] == jnp.arange(host_count * per_host, dtype=jnp.int32)[None, :]
    ).astype(jnp.bfloat16)
    chosen = jnp.dot(
        selector, strip_out.reshape(host_count * per_host, -1), preferred_element_type=jnp.float32
    ).astype(jnp.bfloat16)
    chosen = chosen.reshape(block_count, cluster_rows, feature_width)
    prolonged = jnp.einsum("brc,brl->bcl", weights, chosen, preferred_element_type=jnp.float32)
    return (blocks.astype(jnp.float32) + prolonged).astype(jnp.bfloat16)


def solution(mesh):
    in_specs = (
        P("gx", "gy", None),
        P("gx", None, "gy"),
        P("gx", None, "gy"),
        P(),
        P(),
        P(),
        P(),
        P(),
        P(),
        P("gy", "gx", None, None),
        P("gy", "gx", None),
        P("gy", "gx"),
        P(("gx", "gy"), None),
        P(),
        P(),
        P(),
        P(),
        P(),
    )
    out_specs = P("gx", "gy", None)
    return jax.shard_map(
        per_device, mesh=mesh, in_specs=in_specs, out_specs=out_specs, check_vma=False
    )
```

profile of v0, /device:TPU:1, one launch (start us, length us, event | category | flops | bytes accessed | tf_op | source)
XLA Modules:
  0.0 306.9 jit_solution(8759754886147584759)
XLA Ops:
  6.5 2.4 convolution_convert_fusion.1
  9.1 4.6 %collective-permute-start = (bf16[1,128,256]{2,1,0:T(8,128)(2,1)S(1)}, bf16[1,128,256]{2,1,0:T(8,128)(2,1)S(1)}, u32[]{:S(2)}, u32[]{:S(2)}) collective-permute-start(bf16[1,128,256]{2,1,0:T(8,128)(2,1)S(1)} %get-tuple-element.17), channel_id=1, source_target_pairs={{0,8},{8,16},{16,24},{1,9},{9,17},{17,25},{2,10},{10,18},{18,26},{... | collective-permute-start | bytes 196616 | tf_op jit(solution)/shard_map/ppermute | solution.py:15
  13.7 2.1 collective-permute-start.1
  15.8 0.7 fusion.81
  16.5 0.6 fusion.106
  17.1 0.6 fusion.87
  17.7 0.7 select_reduce_fusion.7
  18.4 1.0 collective-permute-done.1
  19.5 3.1 %collective-permute-start.2 = (bf16[34,1,256]{2,1,0:T(2,128)(2,1)S(1)}, bf16[34,1,256]{2,1,0:T(2,128)(2,1)S(1)}, u32[]{:S(2)}, u32[]{:S(2)}) collective-permute-start(bf16[34,1,256]{2,1,0:T(2,128)(2,1)S(1)} %get-tuple-element.16), channel_id=1, source_target_pairs={{0,1},{1,2},{2,3},{3,4},{4,5},{5,6},{6,7},{8,9},{9,10},{10,11},{11... | collective-permute-start | bytes 52232 | tf_op jit(solution)/shard_map/ppermute | solution.py:15
  22.7 1.3 collective-permute-start.3
  24.0 0.8 fusion.9
  24.8 0.8 fusion.14
  25.6 1.7 collective-permute-done.3
  27.4 1.2 pad_maximum_fusion
  28.6 0.8 fusion.11
  29.4 0.8 fusion.8
  30.3 1.0 fusion.10
  31.3 1.1 fusion.12
  32.4 2.8 fusion.13
  35.2 8.7 %add_convert_fusion = bf16[32,128,256]{2,1,0:T(8,128)(2,1)} fusion(f32[32,128,256]{2,1,0:T(8,128)S(1)} %fusion.14, f32[32,128,256]{2,1,0:T(8,128)} %fusion.13, f32[32,128,256]{2,1,0:T(8,128)S(1)} %fusion.12, f32[32,128,256]{2,1,0:T(8,128)S(1)} %fusion.11, f32[32,128,256]{2,1,0:T(8,128)S(1)} %fusion.10, f32[32,128,256]{2,1,0:T(8,128)S(1)} %fusion.9, ...), kind=kOutput, calls=%fused_computation.13 | convolution fusion | flops 558891008 | bytes 38011904 | tf_op jit(solution)/shard_map/dot_general | solution.py:98
  43.9 4.9 %fusion.1 = bf16[4096,256]{1,0:T(8,128)(2,1)S(1)} fusion(bf16[256,256]{1,0:T(8,128)(2,1)} %param.26, bf16[4096,256]{1,0:T(8,128)(2,1)} %bitcast.82, bf16[512,256]{1,0:T(8,128)(2,1)} %param.25, bf16[4096,256]{1,0:T(8,128)(2,1)} %bitcast.87), kind=kOutput, calls=%fused_computation.6 | convolution fusion | flops 1624244224 | bytes 6684672 | tf_op jit(solution)/shard_map/dot_general | solution.py:112
  48.8 0.4 fusion.68
  49.2 0.6 copy.28
  49.9 2.3 fusion.84
  52.2 2.7 reshape.127
  55.0 67.5 %reduce-scatter.2.cloned.1.call-done = f32[256,256]{1,0:T(8,128)} async-done(((f32[2048,256]{1,0:T(8,128)}), f32[256,256]{1,0:T(8,128)}) %reduce-scatter.2.cloned.1.call-update) | async-done | bytes 262160 | tf_op jit(solution)/shard_map/reduce_scatter | solution.py:134
  122.5 1.0 convert_element_type.139
  123.4 0.9 convolution_convert_fusion.2
  124.4 40.2 %all-gather.3.cloned.1.call-done = bf16[2048,256]{1,0:T(8,128)(2,1)} async-done(((bf16[256,256]{1,0:T(8,128)(2,1)}), bf16[2048,256]{1,0:T(8,128)(2,1)}) %all-gather.3.cloned.1.call-update) | async-done | bytes 1048592 | tf_op jit(solution)/shard_map/all_gather | solution.py:141
  164.6 3.6 %collective-permute-start.7 = (bf16[2048,256]{1,0:T(8,128)(2,1)}, bf16[2048,256]{1,0:T(8,128)(2,1)S(1)}, u32[]{:S(2)}, u32[]{:S(2)}) collective-permute-start(bf16[2048,256]{1,0:T(8,128)(2,1)} %all-gather.3.cloned.1.call-done), channel_id=1, source_target_pairs={{8,0},{16,8},{24,16},{9,1},{17,9},{25,17},{10,2},{18,10},{26,18},{... | collective-permute-start | bytes 3145736 | tf_op jit(solution)/shard_map/ppermute | solution.py:26
  168.2 1.3 collective-permute-start.10
  169.5 1.3 collective-permute-start.8
  170.8 1.5 collective-permute-start.9
  172.3 1.3 collective-permute-done.10
  173.6 0.4 collective-permute-done.8
  174.0 1.9 collective-permute-done.9
  176.0 0.2 copy.25
  176.2 0.3 reshape.133
  176.5 1.3 collective-permute-start.4
  177.8 1.3 collective-permute-start.5
  179.1 1.3 collective-permute-start.6
  180.4 0.6 broadcast_clamp_fusion
  181.0 2.8 collective-permute-done.4
  183.8 3.7 %collective-permute-done.5 = bf16[256,256]{1,0:T(8,128)(2,1)S(1)} collective-permute-done((bf16[256,256]{1,0:T(8,128)(2,1)S(1)}, bf16[256,256]{1,0:T(8,128)(2,1)S(1)}, u32[]{:S(2)}, u32[]{:S(2)}) %collective-permute-start.5) | collective-permute-done | bytes 131104 | tf_op jit(solution)/shard_map/ppermute | solution.py:26
  187.5 2.9 collective-permute-done.6
  190.3 1.3 fusion.83
  191.6 1.4 pad_maximum_fusion.5
  193.0 27.1 %gather_fusion = bf16[6144,256]{1,0:T(8,128)(2,1)} fusion(bf16[4096,256]{1,0:T(8,128)(2,1)S(1)} %pad_maximum_fusion.5, s32[6144]{0:T(1024)} %broadcast_clamp_fusion), kind=kCustom, calls=%fused_computation | custom fusion | bytes 6316032 | tf_op jit(solution)/shard_map/jit(_take)/gather | solution.py:34
  220.1 6.9 %reshape.130 = f32[1024,6,256]{2,1,0:T(8,128)} reshape(bf16[6144,256]{1,0:T(8,128)(2,1)} %gather_fusion) | data formatting | bytes 9437184 | tf_op jit(solution)/shard_map/convert_element_type | solution.py:37
  226.9 4.2 %maximum_convert_fusion = bf16[1024,6,256]{2,1,0:T(8,128)(2,1)S(1)} fusion(f32[1024,6,256]{2,1,0:T(8,128)} %reshape.130, f32[1024,256]{1,0:T(8,128)S(1)} %copy-done.6), kind=kLoop, calls=%fused_computation.2 | loop fusion | flops 4718592 | bytes 10485760 | tf_op jit(solution)/shard_map/convert_element_type | solution.py:37
  231.2 1.8 fusion.39
  233.0 2.1 add_convert_fusion.1
  235.1 0.7 fusion.105
  235.8 5.3 %collective-permute-start.11 = (bf16[256,256]{1,0:T(8,128)(2,1)}, bf16[256,256]{1,0:T(8,128)(2,1)S(1)}, u32[]{:S(2)}, u32[]{:S(2)}) collective-permute-start(bf16[256,256]{1,0:T(8,128)(2,1)} %get-tuple-element.21), channel_id=1, source_target_pairs={{0,3},{1,4},{2,5},{3,6},{4,7},{8,11},{9,12},{10,13},{11,14},{12,15... | collective-permute-start | bytes 393224 | tf_op jit(solution)/shard_map/ppermute | solution.py:26
  241.1 1.3 collective-permute-start.12
  242.4 3.0 collective-permute-start.13
  245.4 1.9 collective-permute-done.13
  247.3 0.7 fusion.71
  248.0 2.9 copy.24
  250.9 41.1 %all-gather.5.cloned.1.call-done = bf16[2048,256]{1,0:T(8,128)(2,1)} async-done(((bf16[256,256]{1,0:T(8,128)(2,1)}), bf16[2048,256]{1,0:T(8,128)(2,1)}) %all-gather.5.cloned.1.call-update) | async-done | bytes 1048592 | tf_op jit(solution)/shard_map/all_gather | solution.py:168
  292.0 1.6 reshape.128
  293.6 0.4 convolution_convert_fusion
  294.1 2.2 fusion.5
  296.3 4.1 %copy.27 = bf16[32,128,256]{2,1,0:T(8,128)(2,1)} copy(bf16[32,128,256]{1,2,0:T(8,128)(2,1)} %fusion.5) | data formatting | bytes 4194304 | tf_op jit(solution)/shard_map/convert_element_type | solution.py:177
  (66 shorter events, 0.5 us)
Async XLA Ops:
  6.5 42.3 %copy-start = (bf16[1,32,32,128]{3,2,1,0:T(8,128)(2,1)S(1)}, bf16[1,32,32,128]{3,2,1,0:T(8,128)(2,1)}, u32[]{:S(2)}) copy-start(bf16[1,32,32,128]{3,2,1,0:T(8,128)(2,1)} %param.27) | copy-start | bytes 786436
  6.5 9.3 %copy-start.1 = (bf16[32,128,256]{2,1,0:T(8,128)(2,1)S(1)}, bf16[32,128,256]{2,1,0:T(8,128)(2,1)}, u32[]{:S(2)}) copy-start(bf16[32,128,256]{2,1,0:T(8,128)(2,1)} %param.18) | copy-start | bytes 6291460
  6.5 9.3 %copy-start.7 = (bf16[256,256]{1,0:T(8,128)(2,1)S(1)}, bf16[256,256]{1,0:T(8,128)(2,1)}, u32[]{:S(2)}) copy-start(bf16[256,256]{1,0:T(8,128)(2,1)} %param.22) | copy-start | bytes 393220
  6.5 115.9 %reduce-scatter.2.cloned.1.call-start = ((), (), s32[]{:S(2)}) async-start(), calls=%async_computation.1 | async-start | bytes 2359296 | tf_op jit(solution)/shard_map/reduce_scatter | solution.py:134
  9.0 7.5 %copy-start.11 = (bf16[8,256]{1,0:T(8,128)(2,1)S(1)}, bf16[8,256]{1,0:T(8,128)(2,1)}, u32[]{:S(2)}) copy-start(bf16[8,256]{1,0:T(8,128)(2,1)} %param.21) | copy-start | bytes 12292
  9.0 8.1 %copy-start.21 = (s32[1,32]{1,0:T(1,128)S(1)}, s32[1,32]{1,0:T(1,128)}, u32[]{:S(2)}) copy-start(s32[1,32]{1,0:T(1,128)} %param.29) | copy-start | bytes 388
  9.0 8.1 %copy-start.23 = (s32[1,32,1]{1,2,0:T(1,128)S(1)}, s32[1,32,1]{1,2,0:T(1,128)}, u32[]{:S(2)}) copy-start(s32[1,32,1]{1,2,0:T(1,128)} %param.28) | copy-start | bytes 388
  9.0 8.7 %copy-start.9 = (s32[32,6,128]{2,0,1:T(8,128)S(1)}, s32[32,6,128]{2,0,1:T(8,128)}, u32[]{:S(2)}) copy-start(s32[32,6,128]{2,0,1:T(8,128)} %param.20) | copy-start | bytes 294916
  9.0 8.7 %copy-start.10 = (s32[32,6,128]{2,0,1:T(8,128)S(1)}, s32[32,6,128]{2,0,1:T(8,128)}, u32[]{:S(2)}) copy-start(s32[32,6,128]{2,0,1:T(8,128)} %param.19) | copy-start | bytes 294916
  9.1 9.4 %collective-permute-start = (bf16[1,128,256]{2,1,0:T(8,128)(2,1)S(1)}, bf16[1,128,256]{2,1,0:T(8,128)(2,1)S(1)}, u32[]{:S(2)}, u32[]{:S(2)}) collective-permute-start(bf16[1,128,256]{2,1,0:T(8,128)(2,1)S(1)} %get-tuple-element.17), channel_id=1, source_target_pairs={{0,8},{8,16},{16,24},{1,9},{9,17},{17,25},{2,10},{10,18},{18,26},{... | collective-permute-start | bytes 196616 | tf_op jit(solution)/shard_map/ppermute | solution.py:15
  13.7 10.2 %copy-start.2 = (bf16[256,256]{1,0:T(8,128)(2,1)S(1)}, bf16[256,256]{1,0:T(8,128)(2,1)}, u32[]{:S(2)}) copy-start(bf16[256,256]{1,0:T(8,128)(2,1)} %param.24) | copy-start | bytes 393220
  13.7 5.7 %collective-permute-start.1 = (bf16[1,128,256]{2,1,0:T(8,128)(2,1)S(1)}, bf16[1,128,256]{2,1,0:T(8,128)(2,1)S(1)}, u32[]{:S(2)}, u32[]{:S(2)}) collective-permute-start(bf16[1,128,256]{2,1,0:T(8,128)(2,1)S(1)} %get-tuple-element.18), channel_id=1, source_target_pairs={{8,0},{16,8},{24,16},{9,1},{17,9},{25,17},{10,2},{18,10},{26,18},{... | collective-permute-start | bytes 196616 | tf_op jit(solution)/shard_map/ppermute | solution.py:18
  19.5 6.1 %collective-permute-start.2 = (bf16[34,1,256]{2,1,0:T(2,128)(2,1)S(1)}, bf16[34,1,256]{2,1,0:T(2,128)(2,1)S(1)}, u32[]{:S(2)}, u32[]{:S(2)}) collective-permute-start(bf16[34,1,256]{2,1,0:T(2,128)(2,1)S(1)} %get-tuple-element.16), channel_id=1, source_target_pairs={{0,1},{1,2},{2,3},{3,4},{4,5},{5,6},{6,7},{8,9},{9,10},{10,11},{11... | collective-permute-start | bytes 52232 | tf_op jit(solution)/shard_map/ppermute | solution.py:15
  22.7 4.7 %collective-permute-start.3 = (bf16[34,1,256]{2,1,0:T(2,128)(2,1)S(1)}, bf16[34,1,256]{2,1,0:T(2,128)(2,1)S(1)}, u32[]{:S(2)}, u32[]{:S(2)}) collective-permute-start(bf16[34,1,256]{2,1,0:T(2,128)(2,1)S(1)} %get-tuple-element.15), channel_id=1, source_target_pairs={{1,0},{2,1},{3,2},{4,3},{5,4},{6,5},{7,6},{9,8},{10,9},{11,10},{12... | collective-permute-start | bytes 52232 | tf_op jit(solution)/shard_map/ppermute | solution.py:18
  48.8 3.4 %copy-start.3 = (bf16[4096,256]{1,0:T(8,128)(2,1)}, bf16[4096,256]{1,0:T(8,128)(2,1)S(1)}, u32[]{:S(2)}) copy-start(bf16[4096,256]{1,0:T(8,128)(2,1)S(1)} %fusion.1) | copy-start | bytes 6291460
  48.8 1.1 copy-start.13
  49.9 73.6 %copy-start.8 = (bf16[256,256]{1,0:T(8,128)(2,1)S(1)}, bf16[256,256]{1,0:T(8,128)(2,1)}, u32[]{:S(2)}) copy-start(bf16[256,256]{1,0:T(8,128)(2,1)} %param.31) | copy-start | bytes 393220
  52.2 116.0 %copy-start.12 = (s32[256,6]{0,1:T(8,128)S(1)}, s32[256,6]{0,1:T(8,128)}, u32[]{:S(2)}) copy-start(s32[256,6]{0,1:T(8,128)} %param.30) | copy-start | bytes 18436
  54.9 135.4 %copy-start.15 = (bf16[256,256]{1,0:T(8,128)(2,1)S(1)}, bf16[256,256]{1,0:T(8,128)(2,1)}, u32[]{:S(2)}) copy-start(bf16[256,256]{1,0:T(8,128)(2,1)} %param.32) | copy-start | bytes 393220
  54.9 109.7 %all-gather.3.cloned.1.call-start = ((), (), s32[]{:S(2)}) async-start(), calls=%async_computation.2 | async-start | bytes 1179648 | tf_op jit(solution)/shard_map/all_gather | solution.py:141
  124.3 167.7 %all-gather.5.cloned.1.call-start = ((), (), s32[]{:S(2)}) async-start(), calls=%async_computation.3 | async-start | bytes 1179648 | tf_op jit(solution)/shard_map/all_gather | solution.py:168
  164.6 27.0 %collective-permute-start.7 = (bf16[2048,256]{1,0:T(8,128)(2,1)}, bf16[2048,256]{1,0:T(8,128)(2,1)S(1)}, u32[]{:S(2)}, u32[]{:S(2)}) collective-permute-start(bf16[2048,256]{1,0:T(8,128)(2,1)} %all-gather.3.cloned.1.call-done), channel_id=1, source_target_pairs={{8,0},{16,8},{24,16},{9,1},{17,9},{25,17},{10,2},{18,10},{26,18},{... | collective-permute-start | bytes 3145736 | tf_op jit(solution)/shard_map/ppermute | solution.py:26
  168.2 5.4 %collective-permute-start.10 = (s32[256,6]{0,1:T(8,128)S(1)}, s32[256,6]{0,1:T(8,128)S(1)}, u32[]{:S(2)}, u32[]{:S(2)}) collective-permute-start(s32[256,6]{0,1:T(8,128)S(1)} %copy-done.12), channel_id=1, source_target_pairs={{3,0},{4,1},{5,2},{6,3},{7,4},{11,8},{12,9},{13,10},{14,11},{15,12... | collective-permute-start | bytes 18440 | tf_op jit(solution)/shard_map/ppermute | solution.py:26
  169.5 4.5 %collective-permute-start.8 = (s32[256,6]{0,1:T(8,128)S(1)}, s32[256,6]{0,1:T(8,128)S(1)}, u32[]{:S(2)}, u32[]{:S(2)}) collective-permute-start(s32[256,6]{0,1:T(8,128)S(1)} %copy-done.12), channel_id=1, source_target_pairs={{1,0},{2,1},{3,2},{4,3},{5,4},{6,5},{7,6},{9,8},{10,9},{11,10},{12... | collective-permute-start | bytes 18440 | tf_op jit(solution)/shard_map/ppermute | solution.py:26
  170.8 5.2 %collective-permute-start.9 = (s32[256,6]{0,1:T(8,128)S(1)}, s32[256,6]{0,1:T(8,128)S(1)}, u32[]{:S(2)}, u32[]{:S(2)}) collective-permute-start(s32[256,6]{0,1:T(8,128)S(1)} %copy-done.12), channel_id=1, source_target_pairs={{2,0},{3,1},{4,2},{5,3},{6,4},{7,5},{10,8},{11,9},{12,10},{13,11},... | collective-permute-start | bytes 18440 | tf_op jit(solution)/shard_map/ppermute | solution.py:26
  176.5 7.3 %collective-permute-start.4 = (bf16[256,256]{1,0:T(8,128)(2,1)S(1)}, bf16[256,256]{1,0:T(8,128)(2,1)S(1)}, u32[]{:S(2)}, u32[]{:S(2)}) collective-permute-start(bf16[256,256]{1,0:T(8,128)(2,1)S(1)} %convert_element_type.139), channel_id=1, source_target_pairs={{1,0},{2,1},{3,2},{4,3},{5,4},{6,5},{7,6},{9,8},{10,9},{11,10},{12... | collective-permute-start | bytes 393224 | tf_op jit(solution)/shard_map/ppermute | solution.py:26
  177.8 9.6 %collective-permute-start.5 = (bf16[256,256]{1,0:T(8,128)(2,1)S(1)}, bf16[256,256]{1,0:T(8,128)(2,1)S(1)}, u32[]{:S(2)}, u32[]{:S(2)}) collective-permute-start(bf16[256,256]{1,0:T(8,128)(2,1)S(1)} %convert_element_type.139), channel_id=1, source_target_pairs={{2,0},{3,1},{4,2},{5,3},{6,4},{7,5},{10,8},{11,9},{12,10},{13,11},... | collective-permute-start | bytes 393224 | tf_op jit(solution)/shard_map/ppermute | solution.py:26
  179.1 11.2 %collective-permute-start.6 = (bf16[256,256]{1,0:T(8,128)(2,1)S(1)}, bf16[256,256]{1,0:T(8,128)(2,1)S(1)}, u32[]{:S(2)}, u32[]{:S(2)}) collective-permute-start(bf16[256,256]{1,0:T(8,128)(2,1)S(1)} %convert_element_type.139), channel_id=1, source_target_pairs={{3,0},{4,1},{5,2},{6,3},{7,4},{11,8},{12,9},{13,10},{14,11},{15,12... | collective-permute-start | bytes 393224 | tf_op jit(solution)/shard_map/ppermute | solution.py:26
  183.8 7.8 %copy-start.18 = (bf16[256,256]{1,0:T(8,128)(2,1)}, bf16[256,256]{1,0:T(8,128)(2,1)S(1)}, u32[]{:S(2)}) copy-start(bf16[256,256]{1,0:T(8,128)(2,1)S(1)} %collective-permute-done.4) | copy-start | bytes 393220
  187.5 4.2 %copy-start.19 = (bf16[256,256]{1,0:T(8,128)(2,1)}, bf16[256,256]{1,0:T(8,128)(2,1)S(1)}, u32[]{:S(2)}) copy-start(bf16[256,256]{1,0:T(8,128)(2,1)S(1)} %collective-permute-done.5) | copy-start | bytes 393220
  190.3 1.3 copy-start.20
  220.1 6.9 %copy-start.6 = (f32[1024,256]{1,0:T(8,128)S(1)}, f32[1024,256]{1,0:T(8,128)}, u32[]{:S(2)}) copy-start(f32[1024,256]{1,0:T(8,128)} %fusion.83) | copy-start | bytes 3145732
  226.9 4.2 %copy-start.16 = (bf16[256,256]{1,0:T(8,128)(2,1)S(1)}, bf16[256,256]{1,0:T(8,128)(2,1)}, u32[]{:S(2)}) copy-start(bf16[256,256]{1,0:T(8,128)(2,1)} %param.33) | copy-start | bytes 393220
  231.1 1.9 copy-start.14
  231.1 1.9 copy-start.17
  233.0 15.0 %copy-start.22 = (s32[1,32]{1,0:T(1,128)S(1)}, s32[1,32]{1,0:T(1,128)}, u32[]{:S(2)}) copy-start(s32[1,32]{1,0:T(1,128)} %param.29) | copy-start | bytes 388
  233.0 15.0 %copy-start.24 = (s32[1,32,1]{1,2,0:T(1,128)S(1)}, s32[1,32,1]{1,2,0:T(1,128)}, u32[]{:S(2)}) copy-start(s32[1,32,1]{1,2,0:T(1,128)} %param.28) | copy-start | bytes 388
  233.0 15.0 %copy-start.4 = (bf16[4096,256]{1,0:T(8,128)(2,1)S(1)}, bf16[4096,256]{1,0:T(8,128)(2,1)}, u32[]{:S(2)}) copy-start(bf16[4096,256]{1,0:T(8,128)(2,1)} %copy-done.3) | copy-start | bytes 6291460
  235.8 9.6 %collective-permute-start.11 = (bf16[256,256]{1,0:T(8,128)(2,1)}, bf16[256,256]{1,0:T(8,128)(2,1)S(1)}, u32[]{:S(2)}, u32[]{:S(2)}) collective-permute-start(bf16[256,256]{1,0:T(8,128)(2,1)} %get-tuple-element.21), channel_id=1, source_target_pairs={{0,3},{1,4},{2,5},{3,6},{4,7},{8,11},{9,12},{10,13},{11,14},{12,15... | collective-permute-start | bytes 393224 | tf_op jit(solution)/shard_map/ppermute | solution.py:26
  241.1 4.3 %collective-permute-start.12 = (bf16[256,256]{1,0:T(8,128)(2,1)S(1)}, bf16[256,256]{1,0:T(8,128)(2,1)S(1)}, u32[]{:S(2)}, u32[]{:S(2)}) collective-permute-start(bf16[256,256]{1,0:T(8,128)(2,1)S(1)} %get-tuple-element.20), channel_id=1, source_target_pairs={{0,2},{1,3},{2,4},{3,5},{4,6},{5,7},{8,10},{9,11},{10,12},{11,13},... | collective-permute-start | bytes 393224 | tf_op jit(solution)/shard_map/ppermute | solution.py:26
  242.4 4.9 %collective-permute-start.13 = (bf16[256,256]{1,0:T(8,128)(2,1)S(1)}, bf16[256,256]{1,0:T(8,128)(2,1)S(1)}, u32[]{:S(2)}, u32[]{:S(2)}) collective-permute-start(bf16[256,256]{1,0:T(8,128)(2,1)S(1)} %get-tuple-element.19), channel_id=1, source_target_pairs={{0,1},{1,2},{2,3},{3,4},{4,5},{5,6},{6,7},{8,9},{9,10},{10,11},{11... | collective-permute-start | bytes 393224 | tf_op jit(solution)/shard_map/ppermute | solution.py:26
  250.9 43.2 %copy-start.5 = (bf16[32,128,256]{1,2,0:T(8,128)(2,1)S(1)}, bf16[32,128,256]{1,2,0:T(8,128)(2,1)}, u32[]{:S(2)}) copy-start(bf16[32,128,256]{1,2,0:T(8,128)(2,1)} %copy.24) | copy-start | bytes 6291460
Sparse Core Ops, SparseCore 0:
  55.0 67.3 reduce-scatter.1
  124.6 39.9 all-gather.2
  248.1 43.8 all-gather.4
where the time goes:
time: 310 us; the launch traced here: 307 us
  waiting for transfers between devices  166 us (54%)
  local copies, waits for them, and re-layouts  47.8 us (15%)
  matrix products  36.3 us (12%)
  starting transfers between devices  32.2 us (10%)
  between operations  13.6 us (4%)
  other arithmetic  10.4 us (3%)
    reduce_scatter x1, waiting for transfers between devices, per_device(): lax.psum_scatter(partial_term.reshape(lax.axis_size('gy') * host_rows, fe...  67.5 us
    all_gather x1, waiting for transfers between devices, per_device(): strip_out = lax.all_gather(coarse_out, 'gy', axis=0, tiled=True)  41.1 us
    all_gather x1, waiting for transfers between devices, per_device(): strip_rows = lax.all_gather(source_proj, 'gy', axis=0, tiled=True)  40.2 us
    gather x1, local copies, waits for them, and re-layouts, coarse_update(): jnp.take(source_table, local_index, axis=0, mode='clip')  27.1 us
    ppermute x10, starting transfers between devices, passed_along(): lax.ppermute(value, axis, [(source, source + steps) for source in range(i...  21 us
    dot_general x8, matrix products, per_device(): jnp.dot(hidden.reshape(-1, feature_width), w_msg, preferred_element_type=...  16.9 us
    ppermute x10, waiting for transfers between devices, passed_along(): lax.ppermute(value, axis, [(source, source + steps) for source in range(i...  14.8 us
    ppermute x2, starting transfers between devices, padded(): lax.ppermute(lax.slice_in_dim(block, block.shape[dim] - width, None, axis...  7.79 us
  transfers between devices with their start and end apart: 17, of which 12 were waited for; matrix products, arithmetic and copies ran while one was open for 3% of the time, Pallas kernels for 0%

commit v1 on v0

v1 whole, which is shorter than its diff:
```python
import functools

import jax
import jax.numpy as jnp
from jax import lax
from jax.experimental import pallas as pl
from jax.experimental.pallas import tpu as pltpu
from jax.sharding import PartitionSpec as P

STEP_X = (-1, -1, -1, 0, 0, 1, 1, 1)
STEP_Y = (-1, 0, 1, -1, 1, -1, 0, 1)
F32 = jnp.float32
BF16 = jnp.bfloat16
VMEM_LIMIT = 56 << 20


def dot(a, b):
    return jnp.dot(a, b, preferred_element_type=F32)


def fine_kernel(
    hosts,
    rows_per_chunk,
    offset_ref,
    latent_ref,
    ends_ref,
    sides_ref,
    counts_ref,
    embed_ref,
    wc_ref,
    wn_ref,
    wm_ref,
    wi_ref,
    wo_ref,
    weight_ref,
    refined_ref,
    *rest,
):
    partial_refs = rest[:hosts]
    proj_ref, center_ref, summed_ref, side_ref, total_ref = rest[hosts:]
    cells_x, cells_y, width = latent_ref.shape
    total_ref[...] = jnp.zeros_like(total_ref)
    place = lax.broadcasted_iota(jnp.int32, (cells_y, width), 0)

    padded = sides_ref.shape[1]
    side_ref[0] = dot(sides_ref[0], wn_ref[...]).astype(BF16).astype(F32)
    side_ref[1] = dot(sides_ref[1], wn_ref[...]).astype(BF16).astype(F32)

    def store_row(row, proj):
        low = side_ref[0, pl.ds(row, 1), :]
        high = side_ref[1, pl.ds(row, 1), :]
        proj_ref[1, row] = proj
        proj_ref[0, row] = jnp.where(place == 0, low, pltpu.roll(proj, 1, 0))
        proj_ref[2, row] = jnp.where(
            place == cells_y - 1, high, pltpu.roll(proj, cells_y - 1, 0)
        )

    for end, row in ((0, 0), (1, cells_x + 1)):
        store_row(row, dot(ends_ref[end], wn_ref[...]).astype(BF16).astype(F32))

    def project(chunk, carry):
        first = chunk * rows_per_chunk
        cells = latent_ref[pl.ds(first, rows_per_chunk)].reshape(-1, width)
        proj = dot(cells, wn_ref[...]).astype(BF16).astype(F32)
        for row in range(rows_per_chunk):
            store_row(first + row + 1, proj[row * cells_y : (row + 1) * cells_y])
        return carry

    lax.fori_loop(0, cells_x // rows_per_chunk, project, 0)

    tile = 32

    def refine(chunk, carry):
        first = chunk * rows_per_chunk
        cells = latent_ref[pl.ds(first, rows_per_chunk)].reshape(-1, width)
        center_ref[...] = dot(cells, wc_ref[...]).reshape(rows_per_chunk, cells_y, width)

        def gather(row, inner):
            x = first + row
            live = counts_ref[x].T
            for start in range(0, cells_y, tile):
                span = slice(start, start + tile)
                center = center_ref[row, span, :]
                total = None
                for d in range(8):
                    near = proj_ref[1 + STEP_Y[d], x + 1 + STEP_X[d], span, :]
                    hidden = jnp.maximum(center + near + embed_ref[d : d + 1, :], 0.0)
                    term = live[span, d : d + 1] * hidden
                    total = term if total is None else total + term
                summed_ref[row, span, :] = total.astype(BF16)
            return inner

        lax.fori_loop(0, rows_per_chunk, gather, 0)
        aggregate = dot(summed_ref[...].reshape(-1, width), wm_ref[...]).astype(BF16)
        hidden = dot(cells, wi_ref[:width]) + dot(aggregate, wi_ref[width:])
        hidden = jnp.maximum(hidden, 0.0).astype(BF16)
        refined = (cells.astype(F32) + dot(hidden, wo_ref[...])).astype(BF16)
        refined_ref[pl.ds(first, rows_per_chunk)] = refined.reshape(
            rows_per_chunk, cells_y, width
        )
        for row in range(rows_per_chunk):
            x = first + row
            block = refined[row * cells_y : (row + 1) * cells_y]
            rows = weight_ref.shape[1]
            part = dot(weight_ref[x], block)
            base = pl.multiple_of(offset_ref[x], rows)
            total_ref[pl.ds(base, rows), :] += part
        return carry

    lax.fori_loop(0, cells_x // rows_per_chunk, refine, 0)
    size = partial_refs[0].shape[0]
    for host in range(hosts):
        partial_refs[host][...] = total_ref[host * size : (host + 1) * size, :].astype(BF16)


def coarse_kernel(
    hosts,
    place_ref,
    source_ref,
    edge_ref,
    refined_ref,
    weight_ref,
    as_ref,
    ad_ref,
    am_ref,
    bi_ref,
    bo_ref,
    *rest,
):
    own_refs = rest[:hosts]
    next_refs = rest[hosts : 2 * hosts]
    out_ref, strip_ref, table_ref, rows_ref, dest_ref, summed_ref = rest[2 * hosts :]
    blocks, rows, _ = weight_ref.shape
    size, width = own_refs[0].shape
    half = width // 2
    degree = source_ref.shape[0] // (hosts * size)

    def split_store(ref, first, value):
        count = value.shape[0]
        ref[pl.ds(2 * first, count, stride=2), :] = value[:, :half]
        ref[pl.ds(2 * first + 1, count, stride=2), :] = value[:, half:]

    for number, ref in enumerate(own_refs + next_refs):
        proj = dot(ref[...], as_ref[...]).astype(BF16).astype(F32)
        split_store(table_ref, number * size, proj)
    for number, ref in enumerate(own_refs):
        strip_ref[pl.ds(number * size, size), :] = ref[...]

    def pick(block, carry):
        base = pl.multiple_of(place_ref[block], rows)
        rows_ref[pl.ds(pl.multiple_of(block * rows, rows), rows), :] = strip_ref[
            pl.ds(base, rows), :
        ]
        return carry

    lax.fori_loop(0, blocks, pick, 0)
    for first in range(0, blocks * rows, 256):
        split_store(dest_ref, first, dot(rows_ref[first : first + 256, :], ad_ref[...]))

    def gather(block, carry):
        edge = edge_ref[block]
        for row in range(rows):
            at = pl.ds(pl.multiple_of(2 * (block * rows + row), 2), 2)
            dest = dest_ref[at, :]
            total = None
            for slot in range(degree):
                source = source_ref[edge + row * degree + slot]
                near = table_ref[pl.ds(pl.multiple_of(2 * source, 2), 2), :]
                hidden = jnp.maximum(near + dest, 0.0)
                total = hidden if total is None else total + hidden
            summed_ref[at, :] = total
        return carry

    lax.fori_loop(0, blocks, gather, 0)
    step = 8

    def update(group, carry):
        first = pl.multiple_of(group * step * rows, step * rows)
        base = rows_ref[pl.ds(first, step * rows), :]
        summed = jnp.concatenate(
            [summed_ref[pl.ds(2 * first + part, step * rows, stride=2), :] for part in (0, 1)],
            axis=1,
        ).astype(BF16)
        aggregate = dot(summed, am_ref[...]).astype(BF16)
        hidden = dot(base, bi_ref[:width]) + dot(aggregate, bi_ref[width:])
        hidden = jnp.maximum(hidden, 0.0).astype(BF16)
        result = (base.astype(F32) + dot(hidden, bo_ref[...])).astype(BF16)
        for part in range(step):
            block = group * step + part
            raised = lax.dot_general(
                weight_ref[block],
                result[part * rows : (part + 1) * rows],
                (((0,), (0,)), ((), ())),
                preferred_element_type=F32,
            )
            out_ref[block] = (refined_ref[block].astype(F32) + raised).astype(BF16)
        return carry

    lax.fori_loop(0, blocks // step, update, 0)


def shifted(value, axis, step):
    count = lax.axis_size(axis)
    pairs = [(i, i + step) for i in range(count) if 0 <= i + step < count]
    return lax.ppermute(value, axis, pairs)


def swapped(value, axis, distance):
    count = lax.axis_size(axis)
    return lax.ppermute(value, axis, [(i, i ^ distance) for i in range(count)])


def per_device(
    fine_latent,
    nbr_dir,
    nbr_mask,
    dir_embed,
    w_center,
    w_neighbour,
    w_msg,
    w_node_in,
    w_node_out,
    restrict_weight,
    cluster_host,
    cluster_slot,
    coarse_src,
    a_src,
    a_dst,
    a_msg,
    b_in,
    b_out,
):
    cells_x, cells_y, width = fine_latent.shape
    hosts = lax.axis_size("gy")
    outer = 4
    inner = hosts // outer
    me = lax.axis_index("gy")
    weights = restrict_weight[0]
    blocks, rows, _ = weights.shape
    per_host = blocks // 4
    size = per_host * rows
    degree = coarse_src.shape[1]

    strip_src = lax.all_gather(coarse_src.reshape(-1), "gy", axis=0, tiled=True)

    low = shifted(fine_latent[:, -1, :], "gy", 1)
    high = shifted(fine_latent[:, 0, :], "gy", -1)
    first_row = jnp.concatenate([fine_latent[0], low[:1], high[:1]], axis=0)
    last_row = jnp.concatenate([fine_latent[-1], low[-1:], high[-1:]], axis=0)
    above = shifted(last_row, "gx", 1)
    below = shifted(first_row, "gx", -1)
    ends = jnp.stack([above[:cells_y], below[:cells_y]])
    extra = -(cells_x + 2) % 16
    fill = jnp.zeros((extra, width), BF16)
    sides = jnp.stack(
        [
            jnp.concatenate([above[cells_y : cells_y + 1], low, below[cells_y : cells_y + 1], fill]),
            jnp.concatenate([above[cells_y + 1 :], high, below[cells_y + 1 :], fill]),
        ]
    )
    padded = cells_x + 2 + extra

    live = nbr_mask.astype(F32)
    counts = jnp.stack(
        [jnp.sum(jnp.where(nbr_dir == d, live, 0.0), axis=1) for d in range(8)], axis=1
    )

    relative = cluster_host[0, :, 0] ^ me
    offsets = (relative * per_host + cluster_slot[0]) * rows
    edges = (cluster_host[0, :, 0] * per_host + cluster_slot[0]) * (rows * degree)

    vmem = pl.BlockSpec(memory_space=pltpu.VMEM)
    smem = pl.BlockSpec(memory_space=pltpu.SMEM)
    chunk = 8
    fine = pl.pallas_call(
        functools.partial(fine_kernel, hosts, chunk),
        out_shape=[jax.ShapeDtypeStruct(fine_latent.shape, BF16)]
        + [jax.ShapeDtypeStruct((size, width), BF16)] * hosts,
        in_specs=[smem] + [vmem] * 11,
        out_specs=[vmem] * (1 + hosts),
        scratch_shapes=[
            pltpu.VMEM((3, cells_x + 2, cells_y, width), F32),
            pltpu.VMEM((chunk, cells_y, width), F32),
            pltpu.VMEM((chunk, cells_y, width), BF16),
            pltpu.VMEM((2, padded, width), F32),
            pltpu.VMEM((hosts * size, width), F32),
        ],
        compiler_params=pltpu.CompilerParams(vmem_limit_bytes=VMEM_LIMIT),
        name="fine_cells",
    )(
        offsets,
        fine_latent,
        ends,
        sides,
        counts,
        dir_embed.astype(F32),
        w_center,
        w_neighbour,
        w_msg,
        w_node_in,
        w_node_out,
        weights,
    )
    refined, partial = fine[0], fine[1:]

    parts = {}
    for far in reversed(range(outer)):
        total = partial[far * inner].astype(F32)
        for near in range(1, inner):
            total = total + swapped(partial[far * inner + near], "gy", near).astype(F32)
        parts[far] = total
    coarse_in = parts[0]
    for far in reversed(range(1, outer)):
        coarse_in = coarse_in + swapped(parts[far].astype(BF16), "gy", far * inner).astype(F32)
    coarse_in = coarse_in.astype(BF16)

    own = [None] * hosts
    own[0] = coarse_in
    for far in range(1, outer):
        own[far * inner] = swapped(coarse_in, "gy", far * inner)
    for far in range(outer):
        for near in range(1, inner):
            own[far * inner + near] = swapped(own[far * inner], "gy", near)
    following = [shifted(value, "gx", -1) for value in own]

    strip_rows = hosts * size
    local = strip_src - lax.axis_index("gx") * strip_rows
    local = jnp.clip(local, 0, 2 * strip_rows - 1) ^ (me * size)

    return pl.pallas_call(
        functools.partial(coarse_kernel, hosts),
        out_shape=jax.ShapeDtypeStruct(fine_latent.shape, BF16),
        in_specs=[smem] * 3 + [vmem] * (7 + 2 * hosts),
        out_specs=vmem,
        scratch_shapes=[
            pltpu.VMEM((strip_rows, width), BF16),
            pltpu.VMEM((4 * strip_rows, width // 2), F32),
            pltpu.VMEM((blocks * rows, width), BF16),
            pltpu.VMEM((2 * blocks * rows, width // 2), F32),
            pltpu.VMEM((2 * blocks * rows, width // 2), F32),
        ],
        compiler_params=pltpu.CompilerParams(vmem_limit_bytes=VMEM_LIMIT),
        name="coarse_rows",
    )(offsets, local, edges, refined, weights, a_src, a_dst, a_msg, b_in, b_out, *own, *following)


def solution(mesh):
    in_specs = (
        P("gx", "gy", None),
        P("gx", None, "gy"),
        P("gx", None, "gy"),
        P(),
        P(),
        P(),
        P(),
        P(),
        P(),
        P("gy", "gx", None, None),
        P("gy", "gx", None),
        P("gy", "gx"),
        P(("gx", "gy"), None),
        P(),
        P(),
        P(),
        P(),
        P(),
    )
    out_specs = P("gx", "gy", None)
    return jax.shard_map(
        per_device, mesh=mesh, in_specs=in_specs, out_specs=out_specs, check_vma=False
    )
```

time: 310 us -> 147 us (0.47)
  waiting for transfers between devices: 166 us -> 16.5 us
  local copies, waits for them, and re-layouts: 47.8 us -> 3.73 us
  Pallas kernels: 0 us -> 37.6 us
  matrix products: 36.3 us -> 0 us
  blocking collectives: 0 us -> 24.7 us
  starting transfers between devices: 32.2 us -> 53.9 us
  between operations: 13.6 us -> 0.45 us
    all_gather x2 -> x0, waiting for transfers between devices: 81.4 us -> none  [the longest x1 41.1 us: per_device(): strip_out = lax.all_gather(coarse_out, 'gy', axis=0, tiled=True)]
    reduce_scatter x1 -> x0, waiting for transfers between devices: 67.5 us -> none  [per_device(): lax.psum_scatter(partial_term.reshape(lax.axis_size('gy') * host_rows, fe...]
    pallas_call x0 -> x2, Pallas kernels: none -> 37.6 us  [the longest x1 22.7 us: per_device(): pl.pallas_call(functools.partial(fine_kernel, hosts, chunk), out_shape=[j...]
    dot_general x19 -> x0, matrix products: 36.3 us -> none  [the longest x8 16.9 us: per_device(): jnp.dot(hidden.reshape(-1, feature_width), w_msg, preferred_element_type=...]
    gather x1 -> x0, local copies, waits for them, and re-layouts: 27.1 us -> none  [coarse_update(): jnp.take(source_table, local_index, axis=0, mode='clip')]
    all_gather x0 -> x1, blocking collectives: none -> 24.7 us  [per_device(): strip_src = lax.all_gather(coarse_src.reshape(-1), 'gy', axis=0, tiled=True)]
    ppermute x14 -> x26, starting transfers between devices: 32.1 us -> 53.9 us  [the longest x12 35.2 us: shifted(): return lax.ppermute(value, axis, pairs)]
    convert_element_type x2 -> x0, local copies, waits for them, and re-layouts: 10.9 us -> none  [the longest x1 6.88 us: coarse_update(): gathered.astype(jnp.float32) + dest_proj[:, None, :]]
  transfers between devices with their start and end apart: 17 -> 26, of which waited for: 12 -> 8; matrix products, arithmetic and copies ran while one was open for 3% -> 6% of each run, Pallas kernels for 0% -> 0%
where the time goes in v1:
time: 147 us; the launch traced here: 146 us
  starting transfers between devices  53.9 us (37%)
  Pallas kernels  37.6 us (26%)
  blocking collectives  24.7 us (17%)
  waiting for transfers between devices  16.5 us (11%)
  other arithmetic  9.48 us (6%)
  local copies, waits for them, and re-layouts  3.73 us (3%)
    ppermute x12, starting transfers between devices, shifted(): return lax.ppermute(value, axis, pairs)  35.2 us
    all_gather x1, blocking collectives, per_device(): strip_src = lax.all_gather(coarse_src.reshape(-1), 'gy', axis=0, tiled=True)  24.7 us
    pallas_call x1, Pallas kernels, per_device(): pl.pallas_call(functools.partial(fine_kernel, hosts, chunk), out_shape=[j...  22.7 us
    ppermute x14, starting transfers between devices, swapped(): return lax.ppermute(value, axis, [(i, i ^ distance) for i in range(count)])  18.7 us
    pallas_call x1, Pallas kernels, per_device(): pl.pallas_call(functools.partial(coarse_kernel, hosts), out_shape=jax.Sha...  14.9 us
    ppermute x14, waiting for transfers between devices, swapped(): return lax.ppermute(value, axis, [(i, i ^ distance) for i in range(count)])  11.5 us
    ppermute x12, waiting for transfers between devices, shifted(): return lax.ppermute(value, axis, pairs)  5.02 us
  transfers between devices with their start and end apart: 26, of which 8 were waited for; matrix products, arithmetic and copies ran while one was open for 6% of the time, Pallas kernels for 0%

profile of v1, /device:TPU:1, one launch (start us, length us, event | category | flops | bytes accessed | tf_op | source)
XLA Modules:
  0.0 146.4 jit_solution(3343718881988398358)
XLA Ops:
  0.0 1.0 fusion.2
  1.0 1.3 collective-permute-start.1
  2.4 4.6 %collective-permute-start = (bf16[32,256]{1,0:T(8,128)(2,1)S(1)}, bf16[32,256]{1,0:T(8,128)(2,1)S(1)}, u32[]{:S(2)}, u32[]{:S(2)}) collective-permute-start(bf16[32,256]{1,0:T(8,128)(2,1)S(1)} %bitcast.51), channel_id=1, source_target_pairs={{0,1},{1,2},{2,3},{3,4},{4,5},{5,6},{6,7},{8,9},{9,10},{10,11},{11... | collective-permute-start | bytes 49160 | tf_op jit(solution)/shard_map/ppermute | solution.py:205
  7.0 0.9 slice_bitcast_fusion.3
  7.9 1.3 fusion
  9.1 1.0 select_reduce_fusion
  10.2 1.3 convert_element_type.52.embed_ref
  11.4 0.1 pad.9.clone
  11.5 0.8 stack.59.counts_ref
  12.3 0.0 collective-permute-done
  12.4 2.9 %collective-permute-start.3 = (bf16[130,256]{1,0:T(8,128)(2,1)S(1)}, bf16[130,256]{1,0:T(8,128)(2,1)S(1)}, u32[]{:S(2)}, u32[]{:S(2)}) collective-permute-start(bf16[130,256]{1,0:T(8,128)(2,1)S(1)} %pad_maximum_fusion.2), channel_id=1, source_target_pairs={{8,0},{16,8},{24,16},{9,1},{17,9},{25,17},{10,2},{18,10},{26,18},{... | collective-permute-start | bytes 199688 | tf_op jit(solution)/shard_map/ppermute | solution.py:205
  15.3 3.5 %collective-permute-start.2 = (bf16[130,256]{1,0:T(8,128)(2,1)S(1)}, bf16[130,256]{1,0:T(8,128)(2,1)S(1)}, u32[]{:S(2)}, u32[]{:S(2)}) collective-permute-start(bf16[130,256]{1,0:T(8,128)(2,1)S(1)} %pad_maximum_fusion.1), channel_id=1, source_target_pairs={{0,8},{8,16},{16,24},{1,9},{9,17},{17,25},{2,10},{10,18},{18,26},{... | collective-permute-start | bytes 199688 | tf_op jit(solution)/shard_map/ppermute | solution.py:205
  18.8 0.0 collective-permute-done.3
  18.8 1.3 collective-permute-done.2
  20.2 0.7 pad_maximum_fusion.ends_ref
  20.8 0.1 maximum_bitcast_fusion
  20.9 0.6 pad_maximum_fusion.3.sides_ref
  21.5 22.7 %fine_cells.1 = (bf16[32,128,256]{2,1,0:T(8,128)(2,1)}, bf16[256,256]{1,0:T(8,128)(2,1)}, bf16[256,256]{1,0:T(8,128)(2,1)}, bf16[256,256]{1,0:T(8,128)(2,1)}, bf...) custom-call(s32[32]{0:T(128)} %get-tuple-element.44.offset_ref.place, ...), custom_call_target="tpu_custom_call" | custom-call | tf_op jit(solution)/shard_map/fine_cells/pallas_call | solution.py:275
  44.3 2.1 %collective-permute-start.5 = (bf16[256,256]{1,0:T(8,128)(2,1)}, bf16[256,256]{1,0:T(8,128)(2,1)S(1)}, u32[]{:S(2)}, u32[]{:S(2)}) collective-permute-start(bf16[256,256]{1,0:T(8,128)(2,1)} %get-tuple-element.18), channel_id=1, source_target_pairs={{0,1},{1,0},{2,3},{3,2},{4,5},{5,4},{6,7},{7,6},{8,9},{9,8},{10,11... | collective-permute-start | bytes 393224 | tf_op jit(solution)/shard_map/ppermute | solution.py:210
  46.4 0.1 collective-permute-start.4
  46.5 1.4 collective-permute-start.7
  47.9 0.1 collective-permute-start.9
  47.9 2.6 %collective-permute-done.5 = bf16[256,256]{1,0:T(8,128)(2,1)S(1)} collective-permute-done((bf16[256,256]{1,0:T(8,128)(2,1)}, bf16[256,256]{1,0:T(8,128)(2,1)S(1)}, u32[]{:S(2)}, u32[]{:S(2)}) %collective-permute-start.5) | collective-permute-done | bytes 131104 | tf_op jit(solution)/shard_map/ppermute | solution.py:210
  50.6 0.9 add_convert_fusion.3
  51.5 2.8 %collective-permute-start.6 = (bf16[256,256]{1,0:T(8,128)(2,1)S(1)}, bf16[256,256]{1,0:T(8,128)(2,1)S(1)}, u32[]{:S(2)}, u32[]{:S(2)}) collective-permute-start(bf16[256,256]{1,0:T(8,128)(2,1)S(1)} %add_convert_fusion.3), channel_id=1, source_target_pairs={{0,6},{1,7},{2,4},{3,5},{4,2},{5,3},{6,0},{7,1},{8,14},{9,15},{10,... | collective-permute-start | bytes 393224 | tf_op jit(solution)/shard_map/ppermute | solution.py:210
  54.3 1.9 %collective-permute-done.7 = bf16[256,256]{1,0:T(8,128)(2,1)S(1)} collective-permute-done((bf16[256,256]{1,0:T(8,128)(2,1)}, bf16[256,256]{1,0:T(8,128)(2,1)S(1)}, u32[]{:S(2)}, u32[]{:S(2)}) %collective-permute-start.7) | collective-permute-done | bytes 131104 | tf_op jit(solution)/shard_map/ppermute | solution.py:210
  56.2 0.9 add_convert_fusion.2
  57.1 2.4 %collective-permute-start.8 = (bf16[256,256]{1,0:T(8,128)(2,1)S(1)}, bf16[256,256]{1,0:T(8,128)(2,1)S(1)}, u32[]{:S(2)}, u32[]{:S(2)}) collective-permute-start(bf16[256,256]{1,0:T(8,128)(2,1)S(1)} %add_convert_fusion.2), channel_id=1, source_target_pairs={{0,4},{1,5},{2,6},{3,7},{4,0},{5,1},{6,2},{7,3},{8,12},{9,13},{10,... | collective-permute-start | bytes 393224 | tf_op jit(solution)/shard_map/ppermute | solution.py:210
  59.5 0.9 add_convert_fusion.1
  60.4 0.7 collective-permute-start.10
  61.2 0.0 collective-permute-done.6
  61.2 4.4 %collective-permute-done.8 = bf16[256,256]{1,0:T(8,128)(2,1)S(1)} collective-permute-done((bf16[256,256]{1,0:T(8,128)(2,1)S(1)}, bf16[256,256]{1,0:T(8,128)(2,1)S(1)}, u32[]{:S(2)}, u32[]{:S(2)}) %collective-permute-start.8) | collective-permute-done | bytes 131104 | tf_op jit(solution)/shard_map/ppermute | solution.py:210
  65.5 1.5 %collective-permute-done.10 = bf16[256,256]{1,0:T(8,128)(2,1)S(1)} collective-permute-done((bf16[256,256]{1,0:T(8,128)(2,1)S(1)}, bf16[256,256]{1,0:T(8,128)(2,1)S(1)}, u32[]{:S(2)}, u32[]{:S(2)}) %collective-permute-start.10) | collective-permute-done | bytes 131104 | tf_op jit(solution)/shard_map/ppermute | solution.py:210
  67.0 1.0 add_convert_fusion.rest_0_
  68.0 3.0 %collective-permute-start.16 = (bf16[256,256]{1,0:T(8,128)(2,1)S(1)}, bf16[256,256]{1,0:T(8,128)(2,1)S(1)}, u32[]{:S(2)}, u32[]{:S(2)}) collective-permute-start(bf16[256,256]{1,0:T(8,128)(2,1)S(1)} %add_convert_fusion.rest_0_), channel_id=1, source_target_pairs={{0,6},{1,7},{2,4},{3,5},{4,2},{5,3},{6,0},{7,1},{8,14},{9,15},{10,... | collective-permute-start | bytes 393224 | tf_op jit(solution)/shard_map/ppermute | solution.py:210
  71.1 2.9 %collective-permute-start.18 = (bf16[256,256]{1,0:T(8,128)(2,1)S(1)}, bf16[256,256]{1,0:T(8,128)(2,1)S(1)}, u32[]{:S(2)}, u32[]{:S(2)}) collective-permute-start(bf16[256,256]{1,0:T(8,128)(2,1)S(1)} %add_convert_fusion.rest_0_), channel_id=1, source_target_pairs={{8,0},{16,8},{24,16},{9,1},{17,9},{25,17},{10,2},{18,10},{26,18},{... | collective-permute-start | bytes 393224 | tf_op jit(solution)/shard_map/ppermute | solution.py:205
  74.0 0.1 collective-permute-start.14
  74.1 0.2 collective-permute-start.12
  74.3 2.3 %collective-permute-start.11 = (bf16[256,256]{1,0:T(8,128)(2,1)S(1)}, bf16[256,256]{1,0:T(8,128)(2,1)S(1)}, u32[]{:S(2)}, u32[]{:S(2)}) collective-permute-start(bf16[256,256]{1,0:T(8,128)(2,1)S(1)} %add_convert_fusion.rest_0_), channel_id=1, source_target_pairs={{0,1},{1,0},{2,3},{3,2},{4,5},{5,4},{6,7},{7,6},{8,9},{9,8},{10,11... | collective-permute-start | bytes 393224 | tf_op jit(solution)/shard_map/ppermute | solution.py:210
  76.6 0.0 collective-permute-done.16.rest_6_
  76.6 2.1 %collective-permute-start.24 = (bf16[256,256]{1,0:T(8,128)(2,1)S(1)}, bf16[256,256]{1,0:T(8,128)(2,1)S(1)}, u32[]{:S(2)}, u32[]{:S(2)}) collective-permute-start(bf16[256,256]{1,0:T(8,128)(2,1)S(1)} %collective-permute-done.16.rest_6_), channel_id=1, source_target_pairs={{8,0},{16,8},{24,16},{9,1},{17,9},{25,17},{10,2},{18,10},{26,18},{... | collective-permute-start | bytes 393224 | tf_op jit(solution)/shard_map/ppermute | solution.py:205
  78.7 0.0 collective-permute-done.18.rest_8_
  78.8 1.5 %collective-permute-start.17 = (bf16[256,256]{1,0:T(8,128)(2,1)S(1)}, bf16[256,256]{1,0:T(8,128)(2,1)S(1)}, u32[]{:S(2)}, u32[]{:S(2)}) collective-permute-start(bf16[256,256]{1,0:T(8,128)(2,1)S(1)} %collective-permute-done.16.rest_6_), channel_id=1, source_target_pairs={{0,1},{1,0},{2,3},{3,2},{4,5},{5,4},{6,7},{7,6},{8,9},{9,8},{10,11... | collective-permute-start | bytes 393224 | tf_op jit(solution)/shard_map/ppermute | solution.py:210
  80.2 1.1 collective-permute-done.14.rest_4_
  81.4 2.7 %collective-permute-start.22 = (bf16[256,256]{1,0:T(8,128)(2,1)S(1)}, bf16[256,256]{1,0:T(8,128)(2,1)S(1)}, u32[]{:S(2)}, u32[]{:S(2)}) collective-permute-start(bf16[256,256]{1,0:T(8,128)(2,1)S(1)} %collective-permute-done.14.rest_4_), channel_id=1, source_target_pairs={{8,0},{16,8},{24,16},{9,1},{17,9},{25,17},{10,2},{18,10},{26,18},{... | collective-permute-start | bytes 393224 | tf_op jit(solution)/shard_map/ppermute | solution.py:205
  84.1 0.0 collective-permute-done.12.rest_2_
  84.1 2.0 %collective-permute-start.15 = (bf16[256,256]{1,0:T(8,128)(2,1)S(1)}, bf16[256,256]{1,0:T(8,128)(2,1)S(1)}, u32[]{:S(2)}, u32[]{:S(2)}) collective-permute-start(bf16[256,256]{1,0:T(8,128)(2,1)S(1)} %collective-permute-done.14.rest_4_), channel_id=1, source_target_pairs={{0,1},{1,0},{2,3},{3,2},{4,5},{5,4},{6,7},{7,6},{8,9},{9,8},{10,11... | collective-permute-start | bytes 393224 | tf_op jit(solution)/shard_map/ppermute | solution.py:210
  86.0 0.0 collective-permute-done.11.rest_1_
  86.0 0.1 collective-permute-start.13
  86.1 0.1 copy.24
  86.3 0.1 reshape.10
  86.4 24.7 %all-gather = s32[8,1,1536]{2,1,0:T(1,128)S(1)} all-gather(s32[1,1,1536]{2,1,0:T(1,128)S(1)} %reshape.10), channel_id=1, replica_groups=mesh['gx'=4,'gy'=8] {'gy'}, dimensions={0}, use_global_device_ids=true | all-gather | bytes 55296 | tf_op jit(solution)/shard_map/all_gather | solution.py:244
  111.2 7.5 %collective-permute-start.20 = (bf16[256,256]{1,0:T(8,128)(2,1)S(1)}, bf16[256,256]{1,0:T(8,128)(2,1)S(1)}, u32[]{:S(2)}, u32[]{:S(2)}) collective-permute-start(bf16[256,256]{1,0:T(8,128)(2,1)S(1)} %collective-permute-done.12.rest_2_), channel_id=1, source_target_pairs={{8,0},{16,8},{24,16},{9,1},{17,9},{25,17},{10,2},{18,10},{26,18},{... | collective-permute-start | bytes 393224 | tf_op jit(solution)/shard_map/ppermute | solution.py:205
  118.7 1.9 %collective-permute-start.19 = (bf16[256,256]{1,0:T(8,128)(2,1)S(1)}, bf16[256,256]{1,0:T(8,128)(2,1)S(1)}, u32[]{:S(2)}, u32[]{:S(2)}) collective-permute-start(bf16[256,256]{1,0:T(8,128)(2,1)S(1)} %collective-permute-done.11.rest_1_), channel_id=1, source_target_pairs={{8,0},{16,8},{24,16},{9,1},{17,9},{25,17},{10,2},{18,10},{26,18},{... | collective-permute-start | bytes 393224 | tf_op jit(solution)/shard_map/ppermute | solution.py:205
  120.6 0.0 collective-permute-done.22.rest_12_
  120.7 1.9 %collective-permute-start.25 = (bf16[256,256]{1,0:T(8,128)(2,1)S(1)}, bf16[256,256]{1,0:T(8,128)(2,1)S(1)}, u32[]{:S(2)}, u32[]{:S(2)}) collective-permute-start(bf16[256,256]{1,0:T(8,128)(2,1)S(1)} %collective-permute-done.17.rest_7_), channel_id=1, source_target_pairs={{8,0},{16,8},{24,16},{9,1},{17,9},{25,17},{10,2},{18,10},{26,18},{... | collective-permute-start | bytes 393224 | tf_op jit(solution)/shard_map/ppermute | solution.py:205
  122.6 0.0 collective-permute-done.15.rest_5_
  122.6 1.9 %collective-permute-start.23 = (bf16[256,256]{1,0:T(8,128)(2,1)S(1)}, bf16[256,256]{1,0:T(8,128)(2,1)S(1)}, u32[]{:S(2)}, u32[]{:S(2)}) collective-permute-start(bf16[256,256]{1,0:T(8,128)(2,1)S(1)} %collective-permute-done.15.rest_5_), channel_id=1, source_target_pairs={{8,0},{16,8},{24,16},{9,1},{17,9},{25,17},{10,2},{18,10},{26,18},{... | collective-permute-start | bytes 393224 | tf_op jit(solution)/shard_map/ppermute | solution.py:205
  124.6 1.9 %collective-permute-start.21 = (bf16[256,256]{1,0:T(8,128)(2,1)S(1)}, bf16[256,256]{1,0:T(8,128)(2,1)S(1)}, u32[]{:S(2)}, u32[]{:S(2)}) collective-permute-start(bf16[256,256]{1,0:T(8,128)(2,1)S(1)} %collective-permute-done.13.rest_3_), channel_id=1, source_target_pairs={{8,0},{16,8},{24,16},{9,1},{17,9},{25,17},{10,2},{18,10},{26,18},{... | collective-permute-start | bytes 393224 | tf_op jit(solution)/shard_map/ppermute | solution.py:205
  126.5 0.7 clamp_xor_fusion
  127.2 1.7 %collective-permute-done.23.rest_13_ = bf16[256,256]{1,0:T(8,128)(2,1)S(1)} collective-permute-done((bf16[256,256]{1,0:T(8,128)(2,1)S(1)}, bf16[256,256]{1,0:T(8,128)(2,1)S(1)}, u32[]{:S(2)}, u32[]{:S(2)}) %collective-permute-start.23) | collective-permute-done | bytes 131104 | tf_op jit(solution)/shard_map/ppermute | solution.py:205
  128.9 1.9 %collective-permute-done.21.rest_11_ = bf16[256,256]{1,0:T(8,128)(2,1)S(1)} collective-permute-done((bf16[256,256]{1,0:T(8,128)(2,1)S(1)}, bf16[256,256]{1,0:T(8,128)(2,1)S(1)}, u32[]{:S(2)}, u32[]{:S(2)}) %collective-permute-start.21) | collective-permute-done | bytes 131104 | tf_op jit(solution)/shard_map/ppermute | solution.py:205
  131.0 0.5 copy-done.15
  131.5 14.9 %coarse_rows.1 = bf16[32,128,256]{2,1,0:T(8,128)(2,1)} custom-call(s32[32]{0:T(128)} %get-tuple-element.44.offset_ref.place_ref, s32[12288]{0:T(1024)} %bitcast.41, s32[32]{0:T(128)} %get-tuple-element.43.edge_ref, bf16[32,128,256]{2,1,0:T(8,128)(2,1)} %get-tuple-element.14.refined_ref, bf16[32,32,128]{2,1,0:T(8,128)(2,1)} %bitcast.40, ...), custom_call_target="tpu_custom_call" | custom-call | tf_op jit(solution)/shard_map/coarse_rows/pallas_call | solution.py:330
  (53 shorter events, 0.2 us)
Async XLA Ops:
  1.0 11.3 %collective-permute-start.1 = (bf16[32,256]{1,0:T(8,128)(2,1)S(1)}, bf16[32,256]{1,0:T(8,128)(2,1)S(1)}, u32[]{:S(2)}, u32[]{:S(2)}) collective-permute-start(bf16[32,256]{1,0:T(8,128)(2,1)S(1)} %bitcast.50), channel_id=1, source_target_pairs={{1,0},{2,1},{3,2},{4,3},{5,4},{6,5},{7,6},{9,8},{10,9},{11,10},{12... | collective-permute-start | bytes 49160 | tf_op jit(solution)/shard_map/ppermute | solution.py:205
  2.4 10.0 %collective-permute-start = (bf16[32,256]{1,0:T(8,128)(2,1)S(1)}, bf16[32,256]{1,0:T(8,128)(2,1)S(1)}, u32[]{:S(2)}, u32[]{:S(2)}) collective-permute-start(bf16[32,256]{1,0:T(8,128)(2,1)S(1)} %bitcast.51), channel_id=1, source_target_pairs={{0,1},{1,2},{2,3},{3,4},{4,5},{5,6},{6,7},{8,9},{9,10},{10,11},{11... | collective-permute-start | bytes 49160 | tf_op jit(solution)/shard_map/ppermute | solution.py:205
  12.4 6.4 %collective-permute-start.3 = (bf16[130,256]{1,0:T(8,128)(2,1)S(1)}, bf16[130,256]{1,0:T(8,128)(2,1)S(1)}, u32[]{:S(2)}, u32[]{:S(2)}) collective-permute-start(bf16[130,256]{1,0:T(8,128)(2,1)S(1)} %pad_maximum_fusion.2), channel_id=1, source_target_pairs={{8,0},{16,8},{24,16},{9,1},{17,9},{25,17},{10,2},{18,10},{26,18},{... | collective-permute-start | bytes 199688 | tf_op jit(solution)/shard_map/ppermute | solution.py:205
  15.3 4.9 %collective-permute-start.2 = (bf16[130,256]{1,0:T(8,128)(2,1)S(1)}, bf16[130,256]{1,0:T(8,128)(2,1)S(1)}, u32[]{:S(2)}, u32[]{:S(2)}) collective-permute-start(bf16[130,256]{1,0:T(8,128)(2,1)S(1)} %pad_maximum_fusion.1), channel_id=1, source_target_pairs={{0,8},{8,16},{16,24},{1,9},{9,17},{17,25},{2,10},{10,18},{18,26},{... | collective-permute-start | bytes 199688 | tf_op jit(solution)/shard_map/ppermute | solution.py:205
  21.5 64.6 %copy-start.16 = (s32[256,6]{0,1:T(8,128)S(1)}, s32[256,6]{0,1:T(8,128)}, u32[]{:S(2)}) copy-start(s32[256,6]{0,1:T(8,128)} %param.30) | copy-start | bytes 18436
  44.3 6.3 %collective-permute-start.5 = (bf16[256,256]{1,0:T(8,128)(2,1)}, bf16[256,256]{1,0:T(8,128)(2,1)S(1)}, u32[]{:S(2)}, u32[]{:S(2)}) collective-permute-start(bf16[256,256]{1,0:T(8,128)(2,1)} %get-tuple-element.18), channel_id=1, source_target_pairs={{0,1},{1,0},{2,3},{3,2},{4,5},{5,4},{6,7},{7,6},{8,9},{9,8},{10,11... | collective-permute-start | bytes 393224 | tf_op jit(solution)/shard_map/ppermute | solution.py:210
  46.4 14.8 %collective-permute-start.4 = (bf16[256,256]{1,0:T(8,128)(2,1)}, bf16[256,256]{1,0:T(8,128)(2,1)S(1)}, u32[]{:S(2)}, u32[]{:S(2)}) collective-permute-start(bf16[256,256]{1,0:T(8,128)(2,1)} %get-tuple-element.16), channel_id=1, source_target_pairs={{0,1},{1,0},{2,3},{3,2},{4,5},{5,4},{6,7},{7,6},{8,9},{9,8},{10,11... | collective-permute-start | bytes 393224 | tf_op jit(solution)/shard_map/ppermute | solution.py:210
  46.5 9.7 %collective-permute-start.7 = (bf16[256,256]{1,0:T(8,128)(2,1)}, bf16[256,256]{1,0:T(8,128)(2,1)S(1)}, u32[]{:S(2)}, u32[]{:S(2)}) collective-permute-start(bf16[256,256]{1,0:T(8,128)(2,1)} %get-tuple-element.20), channel_id=1, source_target_pairs={{0,1},{1,0},{2,3},{3,2},{4,5},{5,4},{6,7},{7,6},{8,9},{9,8},{10,11... | collective-permute-start | bytes 393224 | tf_op jit(solution)/shard_map/ppermute | solution.py:210
  47.9 11.6 %collective-permute-start.9 = (bf16[256,256]{1,0:T(8,128)(2,1)}, bf16[256,256]{1,0:T(8,128)(2,1)S(1)}, u32[]{:S(2)}, u32[]{:S(2)}) collective-permute-start(bf16[256,256]{1,0:T(8,128)(2,1)} %get-tuple-element.22), channel_id=1, source_target_pairs={{0,1},{1,0},{2,3},{3,2},{4,5},{5,4},{6,7},{7,6},{8,9},{9,8},{10,11... | collective-permute-start | bytes 393224 | tf_op jit(solution)/shard_map/ppermute | solution.py:210
  51.5 9.7 %collective-permute-start.6 = (bf16[256,256]{1,0:T(8,128)(2,1)S(1)}, bf16[256,256]{1,0:T(8,128)(2,1)S(1)}, u32[]{:S(2)}, u32[]{:S(2)}) collective-permute-start(bf16[256,256]{1,0:T(8,128)(2,1)S(1)} %add_convert_fusion.3), channel_id=1, source_target_pairs={{0,6},{1,7},{2,4},{3,5},{4,2},{5,3},{6,0},{7,1},{8,14},{9,15},{10,... | collective-permute-start | bytes 393224 | tf_op jit(solution)/shard_map/ppermute | solution.py:210
  57.1 8.4 %collective-permute-start.8 = (bf16[256,256]{1,0:T(8,128)(2,1)S(1)}, bf16[256,256]{1,0:T(8,128)(2,1)S(1)}, u32[]{:S(2)}, u32[]{:S(2)}) collective-permute-start(bf16[256,256]{1,0:T(8,128)(2,1)S(1)} %add_convert_fusion.2), channel_id=1, source_target_pairs={{0,4},{1,5},{2,6},{3,7},{4,0},{5,1},{6,2},{7,3},{8,12},{9,13},{10,... | collective-permute-start | bytes 393224 | tf_op jit(solution)/shard_map/ppermute | solution.py:210
  60.4 6.6 %collective-permute-start.10 = (bf16[256,256]{1,0:T(8,128)(2,1)S(1)}, bf16[256,256]{1,0:T(8,128)(2,1)S(1)}, u32[]{:S(2)}, u32[]{:S(2)}) collective-permute-start(bf16[256,256]{1,0:T(8,128)(2,1)S(1)} %add_convert_fusion.1), channel_id=1, source_target_pairs={{0,2},{1,3},{2,0},{3,1},{4,6},{5,7},{6,4},{7,5},{8,10},{9,11},{10,... | collective-permute-start | bytes 393224 | tf_op jit(solution)/shard_map/ppermute | solution.py:210
  68.0 62.9 %copy-start = (bf16[256,256]{1,0:T(8,128)(2,1)}, bf16[256,256]{1,0:T(8,128)(2,1)S(1)}, u32[]{:S(2)}) copy-start(bf16[256,256]{1,0:T(8,128)(2,1)S(1)} %add_convert_fusion.rest_0_) | copy-start | bytes 393220
  68.0 8.6 %collective-permute-start.16 = (bf16[256,256]{1,0:T(8,128)(2,1)S(1)}, bf16[256,256]{1,0:T(8,128)(2,1)S(1)}, u32[]{:S(2)}, u32[]{:S(2)}) collective-permute-start(bf16[256,256]{1,0:T(8,128)(2,1)S(1)} %add_convert_fusion.rest_0_), channel_id=1, source_target_pairs={{0,6},{1,7},{2,4},{3,5},{4,2},{5,3},{6,0},{7,1},{8,14},{9,15},{10,... | collective-permute-start | bytes 393224 | tf_op jit(solution)/shard_map/ppermute | solution.py:210
  71.1 7.7 %collective-permute-start.18 = (bf16[256,256]{1,0:T(8,128)(2,1)S(1)}, bf16[256,256]{1,0:T(8,128)(2,1)S(1)}, u32[]{:S(2)}, u32[]{:S(2)}) collective-permute-start(bf16[256,256]{1,0:T(8,128)(2,1)S(1)} %add_convert_fusion.rest_0_), channel_id=1, source_target_pairs={{8,0},{16,8},{24,16},{9,1},{17,9},{25,17},{10,2},{18,10},{26,18},{... | collective-permute-start | bytes 393224 | tf_op jit(solution)/shard_map/ppermute | solution.py:205
  74.0 7.4 %collective-permute-start.14 = (bf16[256,256]{1,0:T(8,128)(2,1)S(1)}, bf16[256,256]{1,0:T(8,128)(2,1)S(1)}, u32[]{:S(2)}, u32[]{:S(2)}) collective-permute-start(bf16[256,256]{1,0:T(8,128)(2,1)S(1)} %add_convert_fusion.rest_0_), channel_id=1, source_target_pairs={{0,4},{1,5},{2,6},{3,7},{4,0},{5,1},{6,2},{7,3},{8,12},{9,13},{10,... | collective-permute-start | bytes 393224 | tf_op jit(solution)/shard_map/ppermute | solution.py:210
  74.1 10.0 %collective-permute-start.12 = (bf16[256,256]{1,0:T(8,128)(2,1)S(1)}, bf16[256,256]{1,0:T(8,128)(2,1)S(1)}, u32[]{:S(2)}, u32[]{:S(2)}) collective-permute-start(bf16[256,256]{1,0:T(8,128)(2,1)S(1)} %add_convert_fusion.rest_0_), channel_id=1, source_target_pairs={{0,2},{1,3},{2,0},{3,1},{4,6},{5,7},{6,4},{7,5},{8,10},{9,11},{10,... | collective-permute-start | bytes 393224 | tf_op jit(solution)/shard_map/ppermute | solution.py:210
  74.3 11.8 %collective-permute-start.11 = (bf16[256,256]{1,0:T(8,128)(2,1)S(1)}, bf16[256,256]{1,0:T(8,128)(2,1)S(1)}, u32[]{:S(2)}, u32[]{:S(2)}) collective-permute-start(bf16[256,256]{1,0:T(8,128)(2,1)S(1)} %add_convert_fusion.rest_0_), channel_id=1, source_target_pairs={{0,1},{1,0},{2,3},{3,2},{4,5},{5,4},{6,7},{7,6},{8,9},{9,8},{10,11... | collective-permute-start | bytes 393224 | tf_op jit(solution)/shard_map/ppermute | solution.py:210
  76.6 54.3 %copy-start.1 = (bf16[256,256]{1,0:T(8,128)(2,1)}, bf16[256,256]{1,0:T(8,128)(2,1)S(1)}, u32[]{:S(2)}) copy-start(bf16[256,256]{1,0:T(8,128)(2,1)S(1)} %collective-permute-done.16.rest_6_) | copy-start | bytes 393220
  76.6 34.5 %collective-permute-start.24 = (bf16[256,256]{1,0:T(8,128)(2,1)S(1)}, bf16[256,256]{1,0:T(8,128)(2,1)S(1)}, u32[]{:S(2)}, u32[]{:S(2)}) collective-permute-start(bf16[256,256]{1,0:T(8,128)(2,1)S(1)} %collective-permute-done.16.rest_6_), channel_id=1, source_target_pairs={{8,0},{16,8},{24,16},{9,1},{17,9},{25,17},{10,2},{18,10},{26,18},{... | collective-permute-start | bytes 393224 | tf_op jit(solution)/shard_map/ppermute | solution.py:205
  78.8 52.1 %copy-start.2 = (bf16[256,256]{1,0:T(8,128)(2,1)}, bf16[256,256]{1,0:T(8,128)(2,1)S(1)}, u32[]{:S(2)}) copy-start(bf16[256,256]{1,0:T(8,128)(2,1)S(1)} %collective-permute-done.18.rest_8_) | copy-start | bytes 393220
  78.8 39.9 %collective-permute-start.17 = (bf16[256,256]{1,0:T(8,128)(2,1)S(1)}, bf16[256,256]{1,0:T(8,128)(2,1)S(1)}, u32[]{:S(2)}, u32[]{:S(2)}) collective-permute-start(bf16[256,256]{1,0:T(8,128)(2,1)S(1)} %collective-permute-done.16.rest_6_), channel_id=1, source_target_pairs={{0,1},{1,0},{2,3},{3,2},{4,5},{5,4},{6,7},{7,6},{8,9},{9,8},{10,11... | collective-permute-start | bytes 393224 | tf_op jit(solution)/shard_map/ppermute | solution.py:210
  81.4 49.5 %copy-start.3 = (bf16[256,256]{1,0:T(8,128)(2,1)}, bf16[256,256]{1,0:T(8,128)(2,1)S(1)}, u32[]{:S(2)}) copy-start(bf16[256,256]{1,0:T(8,128)(2,1)S(1)} %collective-permute-done.14.rest_4_) | copy-start | bytes 393220
  81.4 39.3 %collective-permute-start.22 = (bf16[256,256]{1,0:T(8,128)(2,1)S(1)}, bf16[256,256]{1,0:T(8,128)(2,1)S(1)}, u32[]{:S(2)}, u32[]{:S(2)}) collective-permute-start(bf16[256,256]{1,0:T(8,128)(2,1)S(1)} %collective-permute-done.14.rest_4_), channel_id=1, source_target_pairs={{8,0},{16,8},{24,16},{9,1},{17,9},{25,17},{10,2},{18,10},{26,18},{... | collective-permute-start | bytes 393224 | tf_op jit(solution)/shard_map/ppermute | solution.py:205
  84.1 46.8 %copy-start.4 = (bf16[256,256]{1,0:T(8,128)(2,1)}, bf16[256,256]{1,0:T(8,128)(2,1)S(1)}, u32[]{:S(2)}) copy-start(bf16[256,256]{1,0:T(8,128)(2,1)S(1)} %collective-permute-done.12.rest_2_) | copy-start | bytes 393220
  84.1 38.5 %collective-permute-start.15 = (bf16[256,256]{1,0:T(8,128)(2,1)S(1)}, bf16[256,256]{1,0:T(8,128)(2,1)S(1)}, u32[]{:S(2)}, u32[]{:S(2)}) collective-permute-start(bf16[256,256]{1,0:T(8,128)(2,1)S(1)} %collective-permute-done.14.rest_4_), channel_id=1, source_target_pairs={{0,1},{1,0},{2,3},{3,2},{4,5},{5,4},{6,7},{7,6},{8,9},{9,8},{10,11... | collective-permute-start | bytes 393224 | tf_op jit(solution)/shard_map/ppermute | solution.py:210
  86.0 44.9 %copy-start.5 = (bf16[256,256]{1,0:T(8,128)(2,1)}, bf16[256,256]{1,0:T(8,128)(2,1)S(1)}, u32[]{:S(2)}) copy-start(bf16[256,256]{1,0:T(8,128)(2,1)S(1)} %collective-permute-done.11.rest_1_) | copy-start | bytes 393220
  86.0 38.5 %collective-permute-start.13 = (bf16[256,256]{1,0:T(8,128)(2,1)S(1)}, bf16[256,256]{1,0:T(8,128)(2,1)S(1)}, u32[]{:S(2)}, u32[]{:S(2)}) collective-permute-start(bf16[256,256]{1,0:T(8,128)(2,1)S(1)} %collective-permute-done.12.rest_2_), channel_id=1, source_target_pairs={{0,1},{1,0},{2,3},{3,2},{4,5},{5,4},{6,7},{7,6},{8,9},{9,8},{10,11... | collective-permute-start | bytes 393224 | tf_op jit(solution)/shard_map/ppermute | solution.py:210
  111.2 19.8 %copy-start.6 = (bf16[256,256]{1,0:T(8,128)(2,1)}, bf16[256,256]{1,0:T(8,128)(2,1)S(1)}, u32[]{:S(2)}) copy-start(bf16[256,256]{1,0:T(8,128)(2,1)S(1)} %collective-permute-done.24.rest_14_) | copy-start | bytes 393220
  111.2 16.0 %collective-permute-start.20 = (bf16[256,256]{1,0:T(8,128)(2,1)S(1)}, bf16[256,256]{1,0:T(8,128)(2,1)S(1)}, u32[]{:S(2)}, u32[]{:S(2)}) collective-permute-start(bf16[256,256]{1,0:T(8,128)(2,1)S(1)} %collective-permute-done.12.rest_2_), channel_id=1, source_target_pairs={{8,0},{16,8},{24,16},{9,1},{17,9},{25,17},{10,2},{18,10},{26,18},{... | collective-permute-start | bytes 393224 | tf_op jit(solution)/shard_map/ppermute | solution.py:205
  118.7 12.2 %copy-start.7 = (bf16[256,256]{1,0:T(8,128)(2,1)}, bf16[256,256]{1,0:T(8,128)(2,1)S(1)}, u32[]{:S(2)}) copy-start(bf16[256,256]{1,0:T(8,128)(2,1)S(1)} %collective-permute-done.17.rest_7_) | copy-start | bytes 393220
  118.7 8.5 %collective-permute-start.19 = (bf16[256,256]{1,0:T(8,128)(2,1)S(1)}, bf16[256,256]{1,0:T(8,128)(2,1)S(1)}, u32[]{:S(2)}, u32[]{:S(2)}) collective-permute-start(bf16[256,256]{1,0:T(8,128)(2,1)S(1)} %collective-permute-done.11.rest_1_), channel_id=1, source_target_pairs={{8,0},{16,8},{24,16},{9,1},{17,9},{25,17},{10,2},{18,10},{26,18},{... | collective-permute-start | bytes 393224 | tf_op jit(solution)/shard_map/ppermute | solution.py:205
  120.6 10.3 %copy-start.8 = (bf16[256,256]{1,0:T(8,128)(2,1)}, bf16[256,256]{1,0:T(8,128)(2,1)S(1)}, u32[]{:S(2)}) copy-start(bf16[256,256]{1,0:T(8,128)(2,1)S(1)} %collective-permute-done.22.rest_12_) | copy-start | bytes 393220
  120.7 6.5 %collective-permute-start.25 = (bf16[256,256]{1,0:T(8,128)(2,1)S(1)}, bf16[256,256]{1,0:T(8,128)(2,1)S(1)}, u32[]{:S(2)}, u32[]{:S(2)}) collective-permute-start(bf16[256,256]{1,0:T(8,128)(2,1)S(1)} %collective-permute-done.17.rest_7_), channel_id=1, source_target_pairs={{8,0},{16,8},{24,16},{9,1},{17,9},{25,17},{10,2},{18,10},{26,18},{... | collective-permute-start | bytes 393224 | tf_op jit(solution)/shard_map/ppermute | solution.py:205
  122.6 8.4 %copy-start.9 = (bf16[256,256]{1,0:T(8,128)(2,1)}, bf16[256,256]{1,0:T(8,128)(2,1)S(1)}, u32[]{:S(2)}) copy-start(bf16[256,256]{1,0:T(8,128)(2,1)S(1)} %collective-permute-done.15.rest_5_) | copy-start | bytes 393220
  122.6 6.3 %collective-permute-start.23 = (bf16[256,256]{1,0:T(8,128)(2,1)S(1)}, bf16[256,256]{1,0:T(8,128)(2,1)S(1)}, u32[]{:S(2)}, u32[]{:S(2)}) collective-permute-start(bf16[256,256]{1,0:T(8,128)(2,1)S(1)} %collective-permute-done.15.rest_5_), channel_id=1, source_target_pairs={{8,0},{16,8},{24,16},{9,1},{17,9},{25,17},{10,2},{18,10},{26,18},{... | collective-permute-start | bytes 393224 | tf_op jit(solution)/shard_map/ppermute | solution.py:205
  124.5 6.4 %copy-start.10 = (bf16[256,256]{1,0:T(8,128)(2,1)}, bf16[256,256]{1,0:T(8,128)(2,1)S(1)}, u32[]{:S(2)}) copy-start(bf16[256,256]{1,0:T(8,128)(2,1)S(1)} %collective-permute-done.13.rest_3_) | copy-start | bytes 393220
  124.6 6.3 %collective-permute-start.21 = (bf16[256,256]{1,0:T(8,128)(2,1)S(1)}, bf16[256,256]{1,0:T(8,128)(2,1)S(1)}, u32[]{:S(2)}, u32[]{:S(2)}) collective-permute-start(bf16[256,256]{1,0:T(8,128)(2,1)S(1)} %collective-permute-done.13.rest_3_), channel_id=1, source_target_pairs={{8,0},{16,8},{24,16},{9,1},{17,9},{25,17},{10,2},{18,10},{26,18},{... | collective-permute-start | bytes 393224 | tf_op jit(solution)/shard_map/ppermute | solution.py:205
  127.2 3.8 %copy-start.11 = (bf16[256,256]{1,0:T(8,128)(2,1)}, bf16[256,256]{1,0:T(8,128)(2,1)S(1)}, u32[]{:S(2)}) copy-start(bf16[256,256]{1,0:T(8,128)(2,1)S(1)} %collective-permute-done.20.rest_10_) | copy-start | bytes 393220
  127.2 3.8 %copy-start.12 = (bf16[256,256]{1,0:T(8,128)(2,1)}, bf16[256,256]{1,0:T(8,128)(2,1)S(1)}, u32[]{:S(2)}) copy-start(bf16[256,256]{1,0:T(8,128)(2,1)S(1)} %collective-permute-done.19.rest_9_) | copy-start | bytes 393220
  127.2 3.8 %copy-start.13 = (bf16[256,256]{1,0:T(8,128)(2,1)}, bf16[256,256]{1,0:T(8,128)(2,1)S(1)}, u32[]{:S(2)}) copy-start(bf16[256,256]{1,0:T(8,128)(2,1)S(1)} %collective-permute-done.25.rest_15_) | copy-start | bytes 393220
  128.9 2.1 %copy-start.14 = (bf16[256,256]{1,0:T(8,128)(2,1)}, bf16[256,256]{1,0:T(8,128)(2,1)S(1)}, u32[]{:S(2)}) copy-start(bf16[256,256]{1,0:T(8,128)(2,1)S(1)} %collective-permute-done.23.rest_13_) | copy-start | bytes 393220
  130.9 0.7 copy-start.15

commit v2 on v1

v2 whole, which is shorter than its diff:
```python
import functools

import jax
import jax.numpy as jnp
from jax import lax
from jax.experimental import pallas as pl
from jax.experimental.pallas import tpu as pltpu
from jax.sharding import PartitionSpec as P

STEP_X = (-1, -1, -1, 0, 0, 1, 1, 1)
STEP_Y = (-1, 0, 1, -1, 1, -1, 0, 1)
F32 = jnp.float32
BF16 = jnp.bfloat16
DIGIT = 128
VMEM_LIMIT = 56 << 20


def dot(a, b):
    return jnp.dot(a, b, preferred_element_type=F32)


def fine_kernel(
    hosts,
    rows_per_chunk,
    host_ref,
    slot_ref,
    latent_ref,
    low_ref,
    high_ref,
    above_ref,
    below_ref,
    dir_ref,
    mask_ref,
    embed_ref,
    wc_ref,
    wn_ref,
    wm_ref,
    wi_ref,
    wo_ref,
    weight_ref,
    refined_ref,
    *rest,
):
    partial_refs = rest[:hosts]
    proj_ref, center_ref, summed_ref, side_ref, total_ref, count_ref, spread_ref = rest[hosts : hosts + 7]
    cells_ref, result_ref, load_sem, save_sem = rest[hosts + 7 :]
    cells_x, cells_y, width = latent_ref.shape
    me, strip = lax.axis_index("gy"), lax.axis_index("gx")
    flags = (me > 0, me < hosts - 1, strip > 0, strip < lax.axis_size("gx") - 1)
    chunks = cells_x // rows_per_chunk

    def load(chunk):
        part = pl.ds(chunk * rows_per_chunk, rows_per_chunk)
        return pltpu.make_async_copy(latent_ref.at[part], cells_ref.at[part], load_sem.at[chunk])

    def save(chunk):
        part = pl.ds(chunk * rows_per_chunk, rows_per_chunk)
        return pltpu.make_async_copy(result_ref.at[part], refined_ref.at[part], save_sem.at[chunk])

    for chunk in range(chunks):
        load(chunk).start()
    lanes = 128
    size = partial_refs[0].shape[0]
    total_ref[...] = jnp.zeros_like(total_ref)
    place = lax.broadcasted_iota(jnp.int32, (cells_y, width), 0)

    def project(cells):
        return dot(cells, wn_ref[...]).astype(BF16).astype(F32)

    def present(number, proj):
        return jnp.where(flags[number], proj, 0.0)

    def store_row(row, proj):
        low = side_ref[0, pl.ds(row, 1), :]
        high = side_ref[1, pl.ds(row, 1), :]
        proj_ref[1, row] = proj
        proj_ref[0, row] = jnp.where(place == 0, low, pltpu.roll(proj, 1, 0))
        proj_ref[2, row] = jnp.where(
            place == cells_y - 1, high, pltpu.roll(proj, cells_y - 1, 0)
        )

    side_ref[0, 1 : cells_x + 1, :] = present(0, project(low_ref[...]))
    side_ref[1, 1 : cells_x + 1, :] = present(1, project(high_ref[...]))
    for ref, number, row in ((above_ref, 2, 0), (below_ref, 3, cells_x + 1)):
        proj = present(number, project(ref[...]))
        for side in (0, 1):
            corner = proj[cells_y + side : cells_y + side + 1]
            side_ref[side, row : row + 1, :] = present(side, corner)
        store_row(row, proj[:cells_y])

    def prepare(chunk, carry):
        first = chunk * rows_per_chunk
        load(chunk).wait()
        proj = project(cells_ref[pl.ds(first, rows_per_chunk)].reshape(-1, width))
        for row in range(rows_per_chunk):
            store_row(first + row + 1, proj[row * cells_y : (row + 1) * cells_y])
        return carry

    lax.fori_loop(0, chunks, prepare, 0)
    for d in range(8):
        count = None
        for slot in range(dir_ref.shape[0]):
            term = jnp.where(dir_ref[slot] == d, mask_ref[slot].astype(F32), 0.0)
            count = term if count is None else count + term
        count_ref[pl.ds(d, cells_x, stride=8), :] = count

    lowest = -embed_ref[...].astype(F32)
    shape = (8, 8 * lanes)
    own_lanes = lax.broadcasted_iota(jnp.int32, shape, 1) // lanes
    ones = (own_lanes == lax.broadcasted_iota(jnp.int32, shape, 0)).astype(BF16)

    def columns(x, rows):
        count = count_ref[pl.ds(pl.multiple_of(x * 8, 8), 8), :]
        return lax.dot_general(
            count.astype(BF16), rows, (((0,), (0,)), ((), ())), preferred_element_type=F32
        )

    def refine(chunk, carry):
        first = chunk * rows_per_chunk
        cells = cells_ref[pl.ds(first, rows_per_chunk)].reshape(-1, width)
        center_ref[...] = dot(cells, wc_ref[...]).reshape(rows_per_chunk, cells_y, width)
        for row in range(rows_per_chunk):
            spread_ref[row] = columns(first + row, ones)

        def gather(row, inner):
            x = first + row
            for start in range(0, cells_y, 16):
                span = slice(start, start + 16)
                for half in range(0, width, lanes):
                    part = slice(half, half + lanes)
                    center = center_ref[row, span, part]
                    total = None
                    for d in range(8):
                        near = proj_ref[1 + STEP_Y[d], x + 1 + STEP_X[d], span, part]
                        hidden = jnp.maximum(center + near, lowest[d : d + 1, part])
                        term = spread_ref[row, span, d * lanes : (d + 1) * lanes] * hidden
                        total = term if total is None else total + term
                    summed_ref[row, span, part] = total
            return inner

        lax.fori_loop(0, rows_per_chunk, gather, 0)
        rest_sum = jnp.concatenate(
            [columns(first + row, embed_ref[...]) for row in range(rows_per_chunk)]
        )
        summed = (summed_ref[...].reshape(-1, width) + rest_sum).astype(BF16)
        aggregate = dot(summed, wm_ref[...]).astype(BF16)
        hidden = dot(cells, wi_ref[:width]) + dot(aggregate, wi_ref[width:])
        hidden = jnp.maximum(hidden, 0.0).astype(BF16)
        refined = (cells.astype(F32) + dot(hidden, wo_ref[...])).astype(BF16)
        result_ref[pl.ds(first, rows_per_chunk)] = refined.reshape(
            rows_per_chunk, cells_y, width
        )
        save(chunk).start()
        for row in range(rows_per_chunk):
            x = first + row
            rows = weight_ref.shape[1]
            part = dot(weight_ref[x], refined[row * cells_y : (row + 1) * cells_y])
            cluster = (host_ref[x] ^ me) * (size // rows) + slot_ref[x]
            base = pl.multiple_of(cluster * rows, rows)
            total_ref[pl.ds(base, rows), :] += part
        return carry

    lax.fori_loop(0, chunks, refine, 0)
    for host in range(hosts):
        partial_refs[host][...] = total_ref[host * size : (host + 1) * size, :].astype(BF16)
    for chunk in range(chunks):
        save(chunk).wait()


def coarse_kernel(
    hosts,
    degree,
    host_ref,
    slot_ref,
    refined_ref,
    weight_ref,
    as_ref,
    ad_ref,
    am_ref,
    bi_ref,
    bo_ref,
    *rest,
):
    own_refs = rest[:hosts]
    next_refs = rest[hosts : 2 * hosts]
    out_ref, strip_ref, table_ref, rows_ref, dest_ref, summed_ref = rest[2 * hosts : 2 * hosts + 6]
    cells_ref, result_ref, index_ref, lined_ref, source_ref, load_sem, save_sem, index_sem = rest[2 * hosts + 6 :]
    blocks, rows, _ = weight_ref.shape
    size, width = strip_ref.shape[0] // hosts, strip_ref.shape[1]
    lanes = 128
    me = lax.axis_index("gy")
    load = pltpu.make_async_copy(refined_ref, cells_ref, load_sem)
    load.start()

    def cluster_row(block):
        return ((host_ref[block] ^ me) * (size // rows) + slot_ref[block]) * rows

    half = width // 2
    for number, ref in enumerate(own_refs):
        digits = ref[size:, :].astype(F32).astype(jnp.int32)
        local = digits[:degree] * DIGIT + digits[degree : 2 * degree]
        local = 2 * (jnp.clip(local, 0, 2 * hosts * size - 1) ^ (me * size))
        for part in range(size // lanes):
            at = 8 * (number * (size // lanes) + part)
            index_ref[at : at + degree, :] = local[:, part * lanes : (part + 1) * lanes]

    def line_up(block, carry):
        first = cluster_row(block)
        line = pl.multiple_of(8 * (first // lanes), 8)
        turned_by = (lanes - first % lanes) % lanes
        at = pl.ds(pl.multiple_of(8 * block, 8), 8)
        lined_ref[at, :] = pltpu.roll(index_ref[pl.ds(line, 8), :], turned_by, 1)
        return carry

    lax.fori_loop(0, blocks, line_up, 0)
    index_copy = pltpu.make_async_copy(lined_ref, source_ref, index_sem)
    index_copy.start()

    def split_store(ref, first, value):
        count = value.shape[0]
        ref[pl.ds(2 * first, count, stride=2), :] = value[:, :half]
        ref[pl.ds(2 * first + 1, count, stride=2), :] = value[:, half:]

    for number, ref in enumerate(own_refs + next_refs):
        proj = dot(ref[:size, :], as_ref[...]).astype(BF16).astype(F32)
        split_store(table_ref, number * size, proj)
    for number, ref in enumerate(own_refs):
        strip_ref[pl.ds(number * size, size), :] = ref[:size, :]

    def pick(block, carry):
        base = pl.multiple_of(cluster_row(block), rows)
        rows_ref[pl.ds(pl.multiple_of(block * rows, rows), rows), :] = strip_ref[
            pl.ds(base, rows), :
        ]
        return carry

    lax.fori_loop(0, blocks, pick, 0)
    for first in range(0, blocks * rows, 256):
        split_store(dest_ref, first, dot(rows_ref[first : first + 256, :], ad_ref[...]))

    index_copy.wait()

    def gather(block, carry):
        line = 8 * block
        for row in range(rows):
            at = pl.ds(pl.multiple_of(2 * (block * rows + row), 2), 2)
            dest = dest_ref[at, :]
            total = None
            for slot in range(degree):
                source = source_ref[line + slot, row]
                near = table_ref[pl.ds(pl.multiple_of(source, 2), 2), :]
                hidden = jnp.maximum(near + dest, 0.0)
                total = hidden if total is None else total + hidden
            summed_ref[at, :] = total
        return carry

    lax.fori_loop(0, blocks, gather, 0)
    step = 8
    load.wait()

    def save(group):
        part = pl.ds(group * step, step)
        return pltpu.make_async_copy(result_ref.at[part], out_ref.at[part], save_sem.at[group])

    def update(group, carry):
        first = pl.multiple_of(group * step * rows, step * rows)
        base = rows_ref[pl.ds(first, step * rows), :]
        summed = jnp.concatenate(
            [summed_ref[pl.ds(2 * first + part, step * rows, stride=2), :] for part in (0, 1)],
            axis=1,
        ).astype(BF16)
        aggregate = dot(summed, am_ref[...]).astype(BF16)
        hidden = dot(base, bi_ref[:width]) + dot(aggregate, bi_ref[width:])
        hidden = jnp.maximum(hidden, 0.0).astype(BF16)
        result = (base.astype(F32) + dot(hidden, bo_ref[...])).astype(BF16)
        for part in range(step):
            block = group * step + part
            raised = lax.dot_general(
                weight_ref[block],
                result[part * rows : (part + 1) * rows],
                (((0,), (0,)), ((), ())),
                preferred_element_type=F32,
            )
            result_ref[block] = (cells_ref[block].astype(F32) + raised).astype(BF16)
        save(group).start()
        return carry

    lax.fori_loop(0, blocks // step, update, 0)
    for group in range(blocks // step):
        save(group).wait()


def turned(value, axis, step):
    count = lax.axis_size(axis)
    return lax.ppermute(value, axis, [(i, (i + step) % count) for i in range(count)])


def swapped(value, axis, distance):
    count = lax.axis_size(axis)
    return lax.ppermute(value, axis, [(i, i ^ distance) for i in range(count)])


def per_device(
    fine_latent,
    nbr_dir,
    nbr_mask,
    dir_embed,
    w_center,
    w_neighbour,
    w_msg,
    w_node_in,
    w_node_out,
    restrict_weight,
    cluster_host,
    cluster_slot,
    coarse_src,
    a_src,
    a_dst,
    a_msg,
    b_in,
    b_out,
):
    cells_x, cells_y, width = fine_latent.shape
    hosts = lax.axis_size("gy")
    outer = 4
    inner = hosts // outer
    me = lax.axis_index("gy")
    weights = restrict_weight[0]
    blocks, rows, _ = weights.shape
    per_host = blocks // 4
    size = per_host * rows
    degree = coarse_src.shape[1]

    low = turned(fine_latent[:, -1, :], "gy", 1)
    high = turned(fine_latent[:, 0, :], "gy", -1)
    fill = jnp.zeros((14, width), BF16)
    above = turned(jnp.concatenate([fine_latent[-1], low[-1:], high[-1:], fill]), "gx", 1)
    below = turned(jnp.concatenate([fine_latent[0], low[:1], high[:1], fill]), "gx", -1)
    vmem = pl.BlockSpec(memory_space=pltpu.VMEM)
    smem = pl.BlockSpec(memory_space=pltpu.SMEM)
    hbm = pl.BlockSpec(memory_space=pl.ANY)
    block_host, block_slot = cluster_host[0, :, 0], cluster_slot[0]
    chunk = 16
    fine = pl.pallas_call(
        functools.partial(fine_kernel, hosts, chunk),
        out_shape=[jax.ShapeDtypeStruct(fine_latent.shape, BF16)]
        + [jax.ShapeDtypeStruct((size, width), BF16)] * hosts,
        in_specs=[smem] * 2 + [hbm] + [vmem] * 13,
        out_specs=[hbm] + [vmem] * hosts,
        scratch_shapes=[
            pltpu.VMEM((3, cells_x + 2, cells_y, width), F32),
            pltpu.VMEM((chunk, cells_y, width), F32),
            pltpu.VMEM((chunk, cells_y, width), F32),
            pltpu.VMEM((2, cells_x + 8, width), F32),
            pltpu.VMEM((hosts * size, width), F32),
            pltpu.VMEM((cells_x * 8, cells_y), F32),
            pltpu.VMEM((chunk, cells_y, 8 * 128), F32),
            pltpu.VMEM(fine_latent.shape, BF16),
            pltpu.VMEM(fine_latent.shape, BF16),
            pltpu.SemaphoreType.DMA((cells_x // chunk,)),
            pltpu.SemaphoreType.DMA((cells_x // chunk,)),
        ],
        compiler_params=pltpu.CompilerParams(vmem_limit_bytes=VMEM_LIMIT),
        name="fine_cells",
    )(
        block_host,
        block_slot,
        fine_latent,
        low,
        high,
        above,
        below,
        jnp.swapaxes(nbr_dir, 0, 1),
        jnp.swapaxes(nbr_mask, 0, 1),
        dir_embed,
        w_center,
        w_neighbour,
        w_msg,
        w_node_in,
        w_node_out,
        weights,
    )
    refined, partial = fine[0], fine[1:]

    parts = {}
    for far in reversed(range(outer)):
        total = partial[far * inner].astype(F32)
        for near in range(1, inner):
            total = total + swapped(partial[far * inner + near], "gy", near).astype(F32)
        parts[far] = total
    coarse_in = parts[0]
    for far in reversed(range(1, outer)):
        coarse_in = coarse_in + swapped(parts[far].astype(BF16), "gy", far * inner).astype(F32)
    strip_rows = hosts * size
    local = coarse_src.T - lax.axis_index("gx") * strip_rows
    digits = [(local // DIGIT).astype(BF16), (local % DIGIT).astype(BF16)]
    digits = jnp.concatenate(digits + [jnp.zeros((16 - 2 * degree, size), BF16)])
    coarse_in = jnp.concatenate([coarse_in.astype(BF16), digits])

    own = [None] * hosts
    own[0] = coarse_in
    far = outer // 2
    own[far * inner] = swapped(coarse_in, "gy", far * inner)
    for step in range(1, far):
        own[step * inner] = swapped(coarse_in, "gy", step * inner)
        own[(far + step) * inner] = swapped(own[far * inner], "gy", step * inner)
    for far in range(outer):
        for near in range(1, inner):
            own[far * inner + near] = swapped(own[far * inner], "gy", near)
    following = [turned(value, "gx", -1) for value in own]

    return pl.pallas_call(
        functools.partial(coarse_kernel, hosts, degree),
        out_shape=jax.ShapeDtypeStruct(fine_latent.shape, BF16),
        in_specs=[smem] * 2 + [hbm] + [vmem] * (6 + 2 * hosts),
        out_specs=hbm,
        scratch_shapes=[
            pltpu.VMEM((strip_rows, width), BF16),
            pltpu.VMEM((4 * strip_rows, width // 2), F32),
            pltpu.VMEM((blocks * rows, width), BF16),
            pltpu.VMEM((2 * blocks * rows, width // 2), F32),
            pltpu.VMEM((2 * blocks * rows, width // 2), F32),
            pltpu.VMEM(fine_latent.shape, BF16),
            pltpu.VMEM(fine_latent.shape, BF16),
            pltpu.VMEM((8 * strip_rows // 128, 128), jnp.int32),
            pltpu.VMEM((8 * blocks, 128), jnp.int32),
            pltpu.SMEM((8 * blocks, 128), jnp.int32),
            pltpu.SemaphoreType.DMA(()),
            pltpu.SemaphoreType.DMA((4,)),
            pltpu.SemaphoreType.DMA(()),
        ],
        compiler_params=pltpu.CompilerParams(vmem_limit_bytes=VMEM_LIMIT),
        name="coarse_rows",
    )(block_host, block_slot, refined, weights, a_src, a_dst, a_msg, b_in, b_out, *own, *following)


def solution(mesh):
    in_specs = (
        P("gx", "gy", None),
        P("gx", None, "gy"),
        P("gx", None, "gy"),
        P(),
        P(),
        P(),
        P(),
        P(),
        P(),
        P("gy", "gx", None, None),
        P("gy", "gx", None),
        P("gy", "gx"),
        P(("gx", "gy"), None),
        P(),
        P(),
        P(),
        P(),
        P(),
    )
    out_specs = P("gx", "gy", None)
    return jax.shard_map(
        per_device, mesh=mesh, in_specs=in_specs, out_specs=out_specs, check_vma=False
    )
```

time: 147 us -> 97 us (0.66)
  blocking collectives: 24.7 us -> 0 us
  starting transfers between devices: 53.9 us -> 39.3 us
  other arithmetic: 9.48 us -> 4.03 us
  Pallas kernels: 37.6 us -> 33.5 us
    all_gather x1 -> x0, blocking collectives: 24.7 us -> none  [per_device(): strip_src = lax.all_gather(coarse_src.reshape(-1), 'gy', axis=0, tiled=True)]
    ppermute x12, starting transfers between devices: 35.2 us -> 16 us  [turned(): lax.ppermute(value, axis, [(i, (i + step) % count) for i in range(count)])]
    pallas_call x1, Pallas kernels: 22.7 us -> 17.4 us  [per_device(): pl.pallas_call(functools.partial(fine_kernel, hosts, chunk), out_shape=[j...]
    ppermute x14, starting transfers between devices: 18.7 us -> 23.3 us  [swapped(): return lax.ppermute(value, axis, [(i, i ^ distance) for i in range(count)])]
    ppermute x14, waiting for transfers between devices: 11.5 us -> 8.84 us  [swapped(): return lax.ppermute(value, axis, [(i, i ^ distance) for i in range(count)])]
    ppermute x12, waiting for transfers between devices: 5.02 us -> 7.43 us  [turned(): lax.ppermute(value, axis, [(i, (i + step) % count) for i in range(count)])]
  transfers between devices with their start and end apart: 26 -> 26, of which waited for: 8 -> 13; matrix products, arithmetic and copies ran while one was open for 6% -> 4% of each run, Pallas kernels for 0% -> 0%
where the time goes in v2:
time: 97 us; the launch traced here: 96.7 us
  starting transfers between devices  39.3 us (41%)
  Pallas kernels  33.5 us (35%)
  waiting for transfers between devices  16.3 us (17%)
  other arithmetic  4.03 us (4%)
  local copies, waits for them, and re-layouts  3.34 us (3%)
    ppermute x14, starting transfers between devices, swapped(): return lax.ppermute(value, axis, [(i, i ^ distance) for i in range(count)])  23.3 us
    pallas_call x1, Pallas kernels, per_device(): pl.pallas_call(functools.partial(fine_kernel, hosts, chunk), out_shape=[j...  17.4 us
    pallas_call x1, Pallas kernels, per_device(): pl.pallas_call(functools.partial(coarse_kernel, hosts, degree), out_shape...  16.1 us
    ppermute x12, starting transfers between devices, turned(): lax.ppermute(value, axis, [(i, (i + step) % count) for i in range(count)])  16 us
    ppermute x14, waiting for transfers between devices, swapped(): return lax.ppermute(value, axis, [(i, i ^ distance) for i in range(count)])  8.84 us
    ppermute x12, waiting for transfers between devices, turned(): lax.ppermute(value, axis, [(i, (i + step) % count) for i in range(count)])  7.43 us
    convert_element_type x3, other arithmetic, per_device(): parts[far].astype(BF16)  2.82 us
  transfers between devices with their start and end apart: 26, of which 13 were waited for; matrix products, arithmetic and copies ran while one was open for 4% of the time, Pallas kernels for 0%

profile of v2, /device:TPU:1, one launch (start us, length us, event | category | flops | bytes accessed | tf_op | source)
XLA Modules:
  0.0 96.7 jit_solution(706248950813317037)
XLA Ops:
  0.0 1.0 %fusion.5 = (bf16[32,1,256]{2,1,0:T(2,128)(2,1)S(1)}, bf16[32,1,256]{2,1,0:T(2,128)(2,1)S(1)}) fusion(bf16[32,128,256]{2,1,0:T(8,128)(2,1)} %latent_ref.1), kind=kLoop, calls=%fused_computation.23 | loop fusion | bytes 65536 | tf_op jit(solution)/shard_map/slice | solution.py:335
  1.0 2.1 %collective-permute-start = (bf16[32,256]{1,0:T(8,128)(2,1)S(1)}, bf16[32,256]{1,0:T(8,128)(2,1)S(1)}, u32[]{:S(2)}, u32[]{:S(2)}) collective-permute-start(bf16[32,256]{1,0:T(8,128)(2,1)S(1)} %bitcast.45), channel_id=1, source_target_pairs={{0,1},{1,2},{2,3},{3,4},{4,5},{5,6},{6,7},{7,0},{8,9},{9,10},{10,1... | collective-permute-start | bytes 49160 | tf_op jit(solution)/shard_map/ppermute | solution.py:295
  3.2 3.1 %collective-permute-start.1 = (bf16[32,256]{1,0:T(8,128)(2,1)S(1)}, bf16[32,256]{1,0:T(8,128)(2,1)S(1)}, u32[]{:S(2)}, u32[]{:S(2)}) collective-permute-start(bf16[32,256]{1,0:T(8,128)(2,1)S(1)} %bitcast.46), channel_id=1, source_target_pairs={{0,7},{1,0},{2,1},{3,2},{4,3},{5,4},{6,5},{7,6},{8,15},{9,8},{10,9... | collective-permute-start | bytes 49160 | tf_op jit(solution)/shard_map/ppermute | solution.py:295
  6.3 0.9 slice_bitcast_fusion
  7.2 0.1 pad.11.clone
  7.3 0.1 collective-permute-done.low_ref
  7.4 0.0 collective-permute-done.1.high_ref
  7.4 0.1 maximum_maximum_fusion.2
  7.5 1.6 %collective-permute-start.3 = (bf16[144,256]{1,0:T(8,128)(2,1)S(1)}, bf16[144,256]{1,0:T(8,128)(2,1)S(1)}, u32[]{:S(2)}, u32[]{:S(2)}) collective-permute-start(bf16[144,256]{1,0:T(8,128)(2,1)S(1)} %get-tuple-element.33), channel_id=1, source_target_pairs={{0,24},{8,0},{16,8},{24,16},{1,25},{9,1},{17,9},{25,17},{2,26},{10... | collective-permute-start | bytes 221192 | tf_op jit(solution)/shard_map/ppermute | solution.py:295
  9.1 1.3 %collective-permute-start.2 = (bf16[144,256]{1,0:T(8,128)(2,1)S(1)}, bf16[144,256]{1,0:T(8,128)(2,1)S(1)}, u32[]{:S(2)}, u32[]{:S(2)}) collective-permute-start(bf16[144,256]{1,0:T(8,128)(2,1)S(1)} %get-tuple-element.34), channel_id=1, source_target_pairs={{0,8},{8,16},{16,24},{24,0},{1,9},{9,17},{17,25},{25,1},{2,10},{10... | collective-permute-start | bytes 221192 | tf_op jit(solution)/shard_map/ppermute | solution.py:295
  10.4 2.8 %collective-permute-done.3.below_ref = bf16[144,256]{1,0:T(8,128)(2,1)S(1)} collective-permute-done((bf16[144,256]{1,0:T(8,128)(2,1)S(1)}, bf16[144,256]{1,0:T(8,128)(2,1)S(1)}, u32[]{:S(2)}, u32[]{:S(2)}) %collective-permute-start.3) | collective-permute-done | bytes 73760 | tf_op jit(solution)/shard_map/ppermute | solution.py:295
  13.2 0.0 collective-permute-done.2.above_ref
  13.2 0.6 copy-done.16
  13.8 0.0 copy-done.17
  13.8 17.4 %fine_cells.1 = (bf16[32,128,256]{2,1,0:T(8,128)(2,1)}, bf16[256,256]{1,0:T(8,128)(2,1)}, bf16[256,256]{1,0:T(8,128)(2,1)}, bf16[256,256]{1,0:T(8,128)(2,1)}, bf...) custom-call(s32[32]{0:T(128)} %bitcast.47, ...), custom_call_target="tpu_custom_call" | custom-call | tf_op jit(solution)/shard_map/fine_cells/pallas_call | solution.py:344
  31.3 1.2 %collective-permute-start.5 = (bf16[256,256]{1,0:T(8,128)(2,1)}, bf16[256,256]{1,0:T(8,128)(2,1)S(1)}, u32[]{:S(2)}, u32[]{:S(2)}) collective-permute-start(bf16[256,256]{1,0:T(8,128)(2,1)} %get-tuple-element.18), channel_id=1, source_target_pairs={{0,1},{1,0},{2,3},{3,2},{4,5},{5,4},{6,7},{7,6},{8,9},{9,8},{10,11... | collective-permute-start | bytes 393224 | tf_op jit(solution)/shard_map/ppermute | solution.py:300
  32.5 0.1 pad.3.clone
  32.6 0.3 collective-permute-start.4
  32.9 1.2 %collective-permute-start.7 = (bf16[256,256]{1,0:T(8,128)(2,1)}, bf16[256,256]{1,0:T(8,128)(2,1)S(1)}, u32[]{:S(2)}, u32[]{:S(2)}) collective-permute-start(bf16[256,256]{1,0:T(8,128)(2,1)} %get-tuple-element.20), channel_id=1, source_target_pairs={{0,1},{1,0},{2,3},{3,2},{4,5},{5,4},{6,7},{7,6},{8,9},{9,8},{10,11... | collective-permute-start | bytes 393224 | tf_op jit(solution)/shard_map/ppermute | solution.py:300
  34.1 0.3 collective-permute-start.9
  34.4 1.9 %collective-permute-done.5 = bf16[256,256]{1,0:T(8,128)(2,1)S(1)} collective-permute-done((bf16[256,256]{1,0:T(8,128)(2,1)}, bf16[256,256]{1,0:T(8,128)(2,1)S(1)}, u32[]{:S(2)}, u32[]{:S(2)}) %collective-permute-start.5) | collective-permute-done | bytes 131104 | tf_op jit(solution)/shard_map/ppermute | solution.py:300
  36.3 0.9 add_convert_fusion.3
  37.2 3.8 %collective-permute-start.6 = (bf16[256,256]{1,0:T(8,128)(2,1)S(1)}, bf16[256,256]{1,0:T(8,128)(2,1)S(1)}, u32[]{:S(2)}, u32[]{:S(2)}) collective-permute-start(bf16[256,256]{1,0:T(8,128)(2,1)S(1)} %add_convert_fusion.3), channel_id=1, source_target_pairs={{0,6},{1,7},{2,4},{3,5},{4,2},{5,3},{6,0},{7,1},{8,14},{9,15},{10,... | collective-permute-start | bytes 393224 | tf_op jit(solution)/shard_map/ppermute | solution.py:300
  41.0 0.9 collective-permute-done.7
  41.9 0.9 add_convert_fusion.2
  42.8 2.4 %collective-permute-start.8 = (bf16[256,256]{1,0:T(8,128)(2,1)S(1)}, bf16[256,256]{1,0:T(8,128)(2,1)S(1)}, u32[]{:S(2)}, u32[]{:S(2)}) collective-permute-start(bf16[256,256]{1,0:T(8,128)(2,1)S(1)} %add_convert_fusion.2), channel_id=1, source_target_pairs={{0,4},{1,5},{2,6},{3,7},{4,0},{5,1},{6,2},{7,3},{8,12},{9,13},{10,... | collective-permute-start | bytes 393224 | tf_op jit(solution)/shard_map/ppermute | solution.py:300
  45.2 0.0 collective-permute-done.9
  45.2 0.9 add_convert_fusion.1
  46.2 1.7 %collective-permute-start.10 = (bf16[256,256]{1,0:T(8,128)(2,1)S(1)}, bf16[256,256]{1,0:T(8,128)(2,1)S(1)}, u32[]{:S(2)}, u32[]{:S(2)}) collective-permute-start(bf16[256,256]{1,0:T(8,128)(2,1)S(1)} %add_convert_fusion.1), channel_id=1, source_target_pairs={{0,2},{1,3},{2,0},{3,1},{4,6},{5,7},{6,4},{7,5},{8,10},{9,11},{10,... | collective-permute-start | bytes 393224 | tf_op jit(solution)/shard_map/ppermute | solution.py:300
  47.9 0.0 collective-permute-done.4
  47.9 0.0 collective-permute-done.6
  47.9 1.3 %collective-permute-done.8 = bf16[256,256]{1,0:T(8,128)(2,1)S(1)} collective-permute-done((bf16[256,256]{1,0:T(8,128)(2,1)S(1)}, bf16[256,256]{1,0:T(8,128)(2,1)S(1)}, u32[]{:S(2)}, u32[]{:S(2)}) %collective-permute-start.8) | collective-permute-done | bytes 131104 | tf_op jit(solution)/shard_map/ppermute | solution.py:300
  49.2 1.2 %collective-permute-done.10 = bf16[256,256]{1,0:T(8,128)(2,1)S(1)} collective-permute-done((bf16[256,256]{1,0:T(8,128)(2,1)S(1)}, bf16[256,256]{1,0:T(8,128)(2,1)S(1)}, u32[]{:S(2)}, u32[]{:S(2)}) %collective-permute-start.10) | collective-permute-done | bytes 131104 | tf_op jit(solution)/shard_map/ppermute | solution.py:300
  50.4 1.0 %add_convert_fusion = bf16[256,256]{1,0:T(8,128)(2,1)S(1)} fusion(bf16[256,256]{1,0:T(8,128)(2,1)S(1)} %collective-permute-done.10, bf16[256,256]{1,0:T(8,128)(2,1)S(1)} %collective-permute-done.8, bf16[256,256]{1,0:T(8,128)(2,1)S(1)} %collective-permute-done.6, bf16[256,256]{1,0:T(8,128)(2,1)S(1)} %collective-permute-done.4, bf16[256,256]{1,0:T(8,128)(2,1)} %get-tuple-element.15), kind=kLoop, calls=%fused_computation | loop fusion | flops 655360 | bytes 786432 | tf_op jit(solution)/shard_map/convert_element_type | solution.py:398
  51.4 0.1 maximum_maximum_fusion.rest_0_
  51.5 4.1 %collective-permute-start.14 = (bf16[272,256]{1,0:T(8,128)(2,1)S(1)}, bf16[272,256]{1,0:T(8,128)(2,1)S(1)}, u32[]{:S(2)}, u32[]{:S(2)}) collective-permute-start(bf16[272,256]{1,0:T(8,128)(2,1)S(1)} %maximum_maximum_fusion.rest_0_), channel_id=1, source_target_pairs={{0,4},{1,5},{2,6},{3,7},{4,0},{5,1},{6,2},{7,3},{8,12},{9,13},{10,... | collective-permute-start | bytes 417800 | tf_op jit(solution)/shard_map/ppermute | solution.py:300
  55.7 1.5 %collective-permute-start.18 = (bf16[272,256]{1,0:T(8,128)(2,1)S(1)}, bf16[272,256]{1,0:T(8,128)(2,1)S(1)}, u32[]{:S(2)}, u32[]{:S(2)}) collective-permute-start(bf16[272,256]{1,0:T(8,128)(2,1)S(1)} %maximum_maximum_fusion.rest_0_), channel_id=1, source_target_pairs={{0,24},{8,0},{16,8},{24,16},{1,25},{9,1},{17,9},{25,17},{2,26},{10... | collective-permute-start | bytes 417800 | tf_op jit(solution)/shard_map/ppermute | solution.py:295
  57.2 2.2 %collective-permute-start.12 = (bf16[272,256]{1,0:T(8,128)(2,1)S(1)}, bf16[272,256]{1,0:T(8,128)(2,1)S(1)}, u32[]{:S(2)}, u32[]{:S(2)}) collective-permute-start(bf16[272,256]{1,0:T(8,128)(2,1)S(1)} %maximum_maximum_fusion.rest_0_), channel_id=1, source_target_pairs={{0,2},{1,3},{2,0},{3,1},{4,6},{5,7},{6,4},{7,5},{8,10},{9,11},{10,... | collective-permute-start | bytes 417800 | tf_op jit(solution)/shard_map/ppermute | solution.py:300
  59.4 0.6 collective-permute-start.11
  60.0 0.0 collective-permute-done.14.rest_4_
  60.0 3.1 %collective-permute-start.16 = (bf16[272,256]{1,0:T(8,128)(2,1)S(1)}, bf16[272,256]{1,0:T(8,128)(2,1)S(1)}, u32[]{:S(2)}, u32[]{:S(2)}) collective-permute-start(bf16[272,256]{1,0:T(8,128)(2,1)S(1)} %collective-permute-done.14.rest_4_), channel_id=1, source_target_pairs={{0,2},{1,3},{2,0},{3,1},{4,6},{5,7},{6,4},{7,5},{8,10},{9,11},{10,... | collective-permute-start | bytes 417800 | tf_op jit(solution)/shard_map/ppermute | solution.py:300
  63.2 1.1 %collective-permute-start.22 = (bf16[272,256]{1,0:T(8,128)(2,1)S(1)}, bf16[272,256]{1,0:T(8,128)(2,1)S(1)}, u32[]{:S(2)}, u32[]{:S(2)}) collective-permute-start(bf16[272,256]{1,0:T(8,128)(2,1)S(1)} %collective-permute-done.14.rest_4_), channel_id=1, source_target_pairs={{0,24},{8,0},{16,8},{24,16},{1,25},{9,1},{17,9},{25,17},{2,26},{10... | collective-permute-start | bytes 417800 | tf_op jit(solution)/shard_map/ppermute | solution.py:295
  64.2 0.0 collective-permute-done.18.rest_8_
  64.3 0.9 collective-permute-start.15
  65.2 0.0 collective-permute-done.12.rest_2_
  65.2 0.4 collective-permute-start.20
  65.5 0.0 collective-permute-done.11.rest_1_
  65.5 0.6 collective-permute-start.13
  66.1 0.1 collective-permute-done.16.rest_6_
  66.2 0.9 collective-permute-start.17
  67.0 0.9 collective-permute-done.22.rest_12_
  68.0 1.3 %collective-permute-start.19 = (bf16[272,256]{1,0:T(8,128)(2,1)S(1)}, bf16[272,256]{1,0:T(8,128)(2,1)S(1)}, u32[]{:S(2)}, u32[]{:S(2)}) collective-permute-start(bf16[272,256]{1,0:T(8,128)(2,1)S(1)} %collective-permute-done.11.rest_1_), channel_id=1, source_target_pairs={{0,24},{8,0},{16,8},{24,16},{1,25},{9,1},{17,9},{25,17},{2,26},{10... | collective-permute-start | bytes 417800 | tf_op jit(solution)/shard_map/ppermute | solution.py:295
  69.3 0.2 collective-permute-done.15.rest_5_
  69.5 1.3 %collective-permute-start.24 = (bf16[272,256]{1,0:T(8,128)(2,1)S(1)}, bf16[272,256]{1,0:T(8,128)(2,1)S(1)}, u32[]{:S(2)}, u32[]{:S(2)}) collective-permute-start(bf16[272,256]{1,0:T(8,128)(2,1)S(1)} %collective-permute-done.16.rest_6_), channel_id=1, source_target_pairs={{0,24},{8,0},{16,8},{24,16},{1,25},{9,1},{17,9},{25,17},{2,26},{10... | collective-permute-start | bytes 417800 | tf_op jit(solution)/shard_map/ppermute | solution.py:295
  70.8 0.1 collective-permute-start.23
  70.9 1.6 %collective-permute-done.13.rest_3_ = bf16[272,256]{1,0:T(8,128)(2,1)S(1)} collective-permute-done((bf16[272,256]{1,0:T(8,128)(2,1)S(1)}, bf16[272,256]{1,0:T(8,128)(2,1)S(1)}, u32[]{:S(2)}, u32[]{:S(2)}) %collective-permute-start.13) | collective-permute-done | bytes 139296 | tf_op jit(solution)/shard_map/ppermute | solution.py:300
  72.5 1.3 %collective-permute-start.21 = (bf16[272,256]{1,0:T(8,128)(2,1)S(1)}, bf16[272,256]{1,0:T(8,128)(2,1)S(1)}, u32[]{:S(2)}, u32[]{:S(2)}) collective-permute-start(bf16[272,256]{1,0:T(8,128)(2,1)S(1)} %collective-permute-done.13.rest_3_), channel_id=1, source_target_pairs={{0,24},{8,0},{16,8},{24,16},{1,25},{9,1},{17,9},{25,17},{2,26},{10... | collective-permute-start | bytes 417800 | tf_op jit(solution)/shard_map/ppermute | solution.py:295
  73.8 1.7 %collective-permute-done.17.rest_7_ = bf16[272,256]{1,0:T(8,128)(2,1)S(1)} collective-permute-done((bf16[272,256]{1,0:T(8,128)(2,1)S(1)}, bf16[272,256]{1,0:T(8,128)(2,1)S(1)}, u32[]{:S(2)}, u32[]{:S(2)}) %collective-permute-start.17) | collective-permute-done | bytes 139296 | tf_op jit(solution)/shard_map/ppermute | solution.py:300
  75.5 0.9 collective-permute-start.25
  76.3 0.0 collective-permute-done.23.rest_13_
  76.4 0.8 collective-permute-done.21.rest_11_
  77.2 2.7 %collective-permute-done.25.rest_15_ = bf16[272,256]{1,0:T(8,128)(2,1)S(1)} collective-permute-done((bf16[272,256]{1,0:T(8,128)(2,1)S(1)}, bf16[272,256]{1,0:T(8,128)(2,1)S(1)}, u32[]{:S(2)}, u32[]{:S(2)}) %collective-permute-start.25) | collective-permute-done | bytes 139296 | tf_op jit(solution)/shard_map/ppermute | solution.py:295
  80.1 0.5 copy-done.15
  80.6 16.1 %coarse_rows.1 = bf16[32,128,256]{2,1,0:T(8,128)(2,1)} custom-call(s32[32]{0:T(128)} %bitcast.48, s32[32]{0:T(128)} %bitcast.50, bf16[32,128,256]{2,1,0:T(8,128)(2,1)} %get-tuple-element.14.refined_ref, bf16[32,32,128]{2,1,0:T(8,128)(2,1)} %bitcast.42, bf16[256,256]{1,0:T(8,128)(2,1)} %as_ref.1, bf16[256,256]{1,0:T(8,128)(2,1)} %ad_ref.1, ...), custom_call_target="tpu_custom_call" | custom-call | tf_op jit(solution)/shard_map/coarse_rows/pallas_call | solution.py:412
  (49 shorter events, 0.1 us)
Async XLA Ops:
  1.0 6.3 %collective-permute-start = (bf16[32,256]{1,0:T(8,128)(2,1)S(1)}, bf16[32,256]{1,0:T(8,128)(2,1)S(1)}, u32[]{:S(2)}, u32[]{:S(2)}) collective-permute-start(bf16[32,256]{1,0:T(8,128)(2,1)S(1)} %bitcast.45), channel_id=1, source_target_pairs={{0,1},{1,2},{2,3},{3,4},{4,5},{5,6},{6,7},{7,0},{8,9},{9,10},{10,1... | collective-permute-start | bytes 49160 | tf_op jit(solution)/shard_map/ppermute | solution.py:295
  3.2 4.2 %collective-permute-start.1 = (bf16[32,256]{1,0:T(8,128)(2,1)S(1)}, bf16[32,256]{1,0:T(8,128)(2,1)S(1)}, u32[]{:S(2)}, u32[]{:S(2)}) collective-permute-start(bf16[32,256]{1,0:T(8,128)(2,1)S(1)} %bitcast.46), channel_id=1, source_target_pairs={{0,7},{1,0},{2,1},{3,2},{4,3},{5,4},{6,5},{7,6},{8,15},{9,8},{10,9... | collective-permute-start | bytes 49160 | tf_op jit(solution)/shard_map/ppermute | solution.py:295
  7.3 5.9 %copy-start.18 = (bf16[32,256]{1,0:T(8,128)(2,1)}, bf16[32,256]{1,0:T(8,128)(2,1)S(1)}, u32[]{:S(2)}) copy-start(bf16[32,256]{1,0:T(8,128)(2,1)S(1)} %collective-permute-done.low_ref) | copy-start | bytes 49156
  7.4 5.8 %copy-start.19 = (bf16[32,256]{1,0:T(8,128)(2,1)}, bf16[32,256]{1,0:T(8,128)(2,1)S(1)}, u32[]{:S(2)}) copy-start(bf16[32,256]{1,0:T(8,128)(2,1)S(1)} %collective-permute-done.1.high_ref) | copy-start | bytes 49156
  7.5 5.7 %collective-permute-start.3 = (bf16[144,256]{1,0:T(8,128)(2,1)S(1)}, bf16[144,256]{1,0:T(8,128)(2,1)S(1)}, u32[]{:S(2)}, u32[]{:S(2)}) collective-permute-start(bf16[144,256]{1,0:T(8,128)(2,1)S(1)} %get-tuple-element.33), channel_id=1, source_target_pairs={{0,24},{8,0},{16,8},{24,16},{1,25},{9,1},{17,9},{25,17},{2,26},{10... | collective-permute-start | bytes 221192 | tf_op jit(solution)/shard_map/ppermute | solution.py:295
  9.1 4.1 %collective-permute-start.2 = (bf16[144,256]{1,0:T(8,128)(2,1)S(1)}, bf16[144,256]{1,0:T(8,128)(2,1)S(1)}, u32[]{:S(2)}, u32[]{:S(2)}) collective-permute-start(bf16[144,256]{1,0:T(8,128)(2,1)S(1)} %get-tuple-element.34), channel_id=1, source_target_pairs={{0,8},{8,16},{16,24},{24,0},{1,9},{9,17},{17,25},{25,1},{2,10},{10... | collective-permute-start | bytes 221192 | tf_op jit(solution)/shard_map/ppermute | solution.py:295
  13.2 0.6 copy-start.16
  13.2 0.7 copy-start.17
  13.8 34.1 %copy-start.20 = (s32[256,6]{0,1:T(8,128)S(1)}, s32[256,6]{0,1:T(8,128)}, u32[]{:S(2)}) copy-start(s32[256,6]{0,1:T(8,128)} %param.30) | copy-start | bytes 18436
  31.3 5.0 %collective-permute-start.5 = (bf16[256,256]{1,0:T(8,128)(2,1)}, bf16[256,256]{1,0:T(8,128)(2,1)S(1)}, u32[]{:S(2)}, u32[]{:S(2)}) collective-permute-start(bf16[256,256]{1,0:T(8,128)(2,1)} %get-tuple-element.18), channel_id=1, source_target_pairs={{0,1},{1,0},{2,3},{3,2},{4,5},{5,4},{6,7},{7,6},{8,9},{9,8},{10,11... | collective-permute-start | bytes 393224 | tf_op jit(solution)/shard_map/ppermute | solution.py:300
  32.6 15.3 %collective-permute-start.4 = (bf16[256,256]{1,0:T(8,128)(2,1)}, bf16[256,256]{1,0:T(8,128)(2,1)S(1)}, u32[]{:S(2)}, u32[]{:S(2)}) collective-permute-start(bf16[256,256]{1,0:T(8,128)(2,1)} %get-tuple-element.16), channel_id=1, source_target_pairs={{0,1},{1,0},{2,3},{3,2},{4,5},{5,4},{6,7},{7,6},{8,9},{9,8},{10,11... | collective-permute-start | bytes 393224 | tf_op jit(solution)/shard_map/ppermute | solution.py:300
  32.9 9.0 %collective-permute-start.7 = (bf16[256,256]{1,0:T(8,128)(2,1)}, bf16[256,256]{1,0:T(8,128)(2,1)S(1)}, u32[]{:S(2)}, u32[]{:S(2)}) collective-permute-start(bf16[256,256]{1,0:T(8,128)(2,1)} %get-tuple-element.20), channel_id=1, source_target_pairs={{0,1},{1,0},{2,3},{3,2},{4,5},{5,4},{6,7},{7,6},{8,9},{9,8},{10,11... | collective-permute-start | bytes 393224 | tf_op jit(solution)/shard_map/ppermute | solution.py:300
  34.1 11.1 %collective-permute-start.9 = (bf16[256,256]{1,0:T(8,128)(2,1)}, bf16[256,256]{1,0:T(8,128)(2,1)S(1)}, u32[]{:S(2)}, u32[]{:S(2)}) collective-permute-start(bf16[256,256]{1,0:T(8,128)(2,1)} %get-tuple-element.22), channel_id=1, source_target_pairs={{0,1},{1,0},{2,3},{3,2},{4,5},{5,4},{6,7},{7,6},{8,9},{9,8},{10,11... | collective-permute-start | bytes 393224 | tf_op jit(solution)/shard_map/ppermute | solution.py:300
  37.2 10.7 %collective-permute-start.6 = (bf16[256,256]{1,0:T(8,128)(2,1)S(1)}, bf16[256,256]{1,0:T(8,128)(2,1)S(1)}, u32[]{:S(2)}, u32[]{:S(2)}) collective-permute-start(bf16[256,256]{1,0:T(8,128)(2,1)S(1)} %add_convert_fusion.3), channel_id=1, source_target_pairs={{0,6},{1,7},{2,4},{3,5},{4,2},{5,3},{6,0},{7,1},{8,14},{9,15},{10,... | collective-permute-start | bytes 393224 | tf_op jit(solution)/shard_map/ppermute | solution.py:300
  42.8 6.4 %collective-permute-start.8 = (bf16[256,256]{1,0:T(8,128)(2,1)S(1)}, bf16[256,256]{1,0:T(8,128)(2,1)S(1)}, u32[]{:S(2)}, u32[]{:S(2)}) collective-permute-start(bf16[256,256]{1,0:T(8,128)(2,1)S(1)} %add_convert_fusion.2), channel_id=1, source_target_pairs={{0,4},{1,5},{2,6},{3,7},{4,0},{5,1},{6,2},{7,3},{8,12},{9,13},{10,... | collective-permute-start | bytes 393224 | tf_op jit(solution)/shard_map/ppermute | solution.py:300
  46.2 4.3 %collective-permute-start.10 = (bf16[256,256]{1,0:T(8,128)(2,1)S(1)}, bf16[256,256]{1,0:T(8,128)(2,1)S(1)}, u32[]{:S(2)}, u32[]{:S(2)}) collective-permute-start(bf16[256,256]{1,0:T(8,128)(2,1)S(1)} %add_convert_fusion.1), channel_id=1, source_target_pairs={{0,2},{1,3},{2,0},{3,1},{4,6},{5,7},{6,4},{7,5},{8,10},{9,11},{10,... | collective-permute-start | bytes 393224 | tf_op jit(solution)/shard_map/ppermute | solution.py:300
  51.5 28.4 %copy-start = (bf16[272,256]{1,0:T(8,128)(2,1)}, bf16[272,256]{1,0:T(8,128)(2,1)S(1)}, u32[]{:S(2)}) copy-start(bf16[272,256]{1,0:T(8,128)(2,1)S(1)} %maximum_maximum_fusion.rest_0_) | copy-start | bytes 417796
  51.5 8.5 %collective-permute-start.14 = (bf16[272,256]{1,0:T(8,128)(2,1)S(1)}, bf16[272,256]{1,0:T(8,128)(2,1)S(1)}, u32[]{:S(2)}, u32[]{:S(2)}) collective-permute-start(bf16[272,256]{1,0:T(8,128)(2,1)S(1)} %maximum_maximum_fusion.rest_0_), channel_id=1, source_target_pairs={{0,4},{1,5},{2,6},{3,7},{4,0},{5,1},{6,2},{7,3},{8,12},{9,13},{10,... | collective-permute-start | bytes 417800 | tf_op jit(solution)/shard_map/ppermute | solution.py:300
  55.7 8.6 %collective-permute-start.18 = (bf16[272,256]{1,0:T(8,128)(2,1)S(1)}, bf16[272,256]{1,0:T(8,128)(2,1)S(1)}, u32[]{:S(2)}, u32[]{:S(2)}) collective-permute-start(bf16[272,256]{1,0:T(8,128)(2,1)S(1)} %maximum_maximum_fusion.rest_0_), channel_id=1, source_target_pairs={{0,24},{8,0},{16,8},{24,16},{1,25},{9,1},{17,9},{25,17},{2,26},{10... | collective-permute-start | bytes 417800 | tf_op jit(solution)/shard_map/ppermute | solution.py:295
  57.2 8.0 %collective-permute-start.12 = (bf16[272,256]{1,0:T(8,128)(2,1)S(1)}, bf16[272,256]{1,0:T(8,128)(2,1)S(1)}, u32[]{:S(2)}, u32[]{:S(2)}) collective-permute-start(bf16[272,256]{1,0:T(8,128)(2,1)S(1)} %maximum_maximum_fusion.rest_0_), channel_id=1, source_target_pairs={{0,2},{1,3},{2,0},{3,1},{4,6},{5,7},{6,4},{7,5},{8,10},{9,11},{10,... | collective-permute-start | bytes 417800 | tf_op jit(solution)/shard_map/ppermute | solution.py:300
  59.4 6.1 %collective-permute-start.11 = (bf16[272,256]{1,0:T(8,128)(2,1)S(1)}, bf16[272,256]{1,0:T(8,128)(2,1)S(1)}, u32[]{:S(2)}, u32[]{:S(2)}) collective-permute-start(bf16[272,256]{1,0:T(8,128)(2,1)S(1)} %maximum_maximum_fusion.rest_0_), channel_id=1, source_target_pairs={{0,1},{1,0},{2,3},{3,2},{4,5},{5,4},{6,7},{7,6},{8,9},{9,8},{10,11... | collective-permute-start | bytes 417800 | tf_op jit(solution)/shard_map/ppermute | solution.py:300
  60.0 19.9 %copy-start.1 = (bf16[272,256]{1,0:T(8,128)(2,1)}, bf16[272,256]{1,0:T(8,128)(2,1)S(1)}, u32[]{:S(2)}) copy-start(bf16[272,256]{1,0:T(8,128)(2,1)S(1)} %collective-permute-done.14.rest_4_) | copy-start | bytes 417796
  60.0 6.1 %collective-permute-start.16 = (bf16[272,256]{1,0:T(8,128)(2,1)S(1)}, bf16[272,256]{1,0:T(8,128)(2,1)S(1)}, u32[]{:S(2)}, u32[]{:S(2)}) collective-permute-start(bf16[272,256]{1,0:T(8,128)(2,1)S(1)} %collective-permute-done.14.rest_4_), channel_id=1, source_target_pairs={{0,2},{1,3},{2,0},{3,1},{4,6},{5,7},{6,4},{7,5},{8,10},{9,11},{10,... | collective-permute-start | bytes 417800 | tf_op jit(solution)/shard_map/ppermute | solution.py:300
  63.2 4.8 %collective-permute-start.22 = (bf16[272,256]{1,0:T(8,128)(2,1)S(1)}, bf16[272,256]{1,0:T(8,128)(2,1)S(1)}, u32[]{:S(2)}, u32[]{:S(2)}) collective-permute-start(bf16[272,256]{1,0:T(8,128)(2,1)S(1)} %collective-permute-done.14.rest_4_), channel_id=1, source_target_pairs={{0,24},{8,0},{16,8},{24,16},{1,25},{9,1},{17,9},{25,17},{2,26},{10... | collective-permute-start | bytes 417800 | tf_op jit(solution)/shard_map/ppermute | solution.py:295
  64.2 15.7 %copy-start.2 = (bf16[272,256]{1,0:T(8,128)(2,1)}, bf16[272,256]{1,0:T(8,128)(2,1)S(1)}, u32[]{:S(2)}) copy-start(bf16[272,256]{1,0:T(8,128)(2,1)S(1)} %collective-permute-done.18.rest_8_) | copy-start | bytes 417796
  64.3 5.2 %collective-permute-start.15 = (bf16[272,256]{1,0:T(8,128)(2,1)S(1)}, bf16[272,256]{1,0:T(8,128)(2,1)S(1)}, u32[]{:S(2)}, u32[]{:S(2)}) collective-permute-start(bf16[272,256]{1,0:T(8,128)(2,1)S(1)} %collective-permute-done.14.rest_4_), channel_id=1, source_target_pairs={{0,1},{1,0},{2,3},{3,2},{4,5},{5,4},{6,7},{7,6},{8,9},{9,8},{10,11... | collective-permute-start | bytes 417800 | tf_op jit(solution)/shard_map/ppermute | solution.py:300
  65.2 14.8 %copy-start.3 = (bf16[272,256]{1,0:T(8,128)(2,1)}, bf16[272,256]{1,0:T(8,128)(2,1)S(1)}, u32[]{:S(2)}) copy-start(bf16[272,256]{1,0:T(8,128)(2,1)S(1)} %collective-permute-done.12.rest_2_) | copy-start | bytes 417796
  65.2 5.6 %collective-permute-start.20 = (bf16[272,256]{1,0:T(8,128)(2,1)S(1)}, bf16[272,256]{1,0:T(8,128)(2,1)S(1)}, u32[]{:S(2)}, u32[]{:S(2)}) collective-permute-start(bf16[272,256]{1,0:T(8,128)(2,1)S(1)} %collective-permute-done.12.rest_2_), channel_id=1, source_target_pairs={{0,24},{8,0},{16,8},{24,16},{1,25},{9,1},{17,9},{25,17},{2,26},{10... | collective-permute-start | bytes 417800 | tf_op jit(solution)/shard_map/ppermute | solution.py:295
  65.5 14.4 %copy-start.4 = (bf16[272,256]{1,0:T(8,128)(2,1)}, bf16[272,256]{1,0:T(8,128)(2,1)S(1)}, u32[]{:S(2)}) copy-start(bf16[272,256]{1,0:T(8,128)(2,1)S(1)} %collective-permute-done.11.rest_1_) | copy-start | bytes 417796
  65.5 6.9 %collective-permute-start.13 = (bf16[272,256]{1,0:T(8,128)(2,1)S(1)}, bf16[272,256]{1,0:T(8,128)(2,1)S(1)}, u32[]{:S(2)}, u32[]{:S(2)}) collective-permute-start(bf16[272,256]{1,0:T(8,128)(2,1)S(1)} %collective-permute-done.12.rest_2_), channel_id=1, source_target_pairs={{0,1},{1,0},{2,3},{3,2},{4,5},{5,4},{6,7},{7,6},{8,9},{9,8},{10,11... | collective-permute-start | bytes 417800 | tf_op jit(solution)/shard_map/ppermute | solution.py:300
  66.2 13.8 %copy-start.5 = (bf16[272,256]{1,0:T(8,128)(2,1)}, bf16[272,256]{1,0:T(8,128)(2,1)S(1)}, u32[]{:S(2)}) copy-start(bf16[272,256]{1,0:T(8,128)(2,1)S(1)} %collective-permute-done.16.rest_6_) | copy-start | bytes 417796
  66.2 9.3 %collective-permute-start.17 = (bf16[272,256]{1,0:T(8,128)(2,1)S(1)}, bf16[272,256]{1,0:T(8,128)(2,1)S(1)}, u32[]{:S(2)}, u32[]{:S(2)}) collective-permute-start(bf16[272,256]{1,0:T(8,128)(2,1)S(1)} %collective-permute-done.16.rest_6_), channel_id=1, source_target_pairs={{0,1},{1,0},{2,3},{3,2},{4,5},{5,4},{6,7},{7,6},{8,9},{9,8},{10,11... | collective-permute-start | bytes 417800 | tf_op jit(solution)/shard_map/ppermute | solution.py:300
  68.0 12.0 %copy-start.6 = (bf16[272,256]{1,0:T(8,128)(2,1)}, bf16[272,256]{1,0:T(8,128)(2,1)S(1)}, u32[]{:S(2)}) copy-start(bf16[272,256]{1,0:T(8,128)(2,1)S(1)} %collective-permute-done.22.rest_12_) | copy-start | bytes 417796
  68.0 8.4 %collective-permute-start.19 = (bf16[272,256]{1,0:T(8,128)(2,1)S(1)}, bf16[272,256]{1,0:T(8,128)(2,1)S(1)}, u32[]{:S(2)}, u32[]{:S(2)}) collective-permute-start(bf16[272,256]{1,0:T(8,128)(2,1)S(1)} %collective-permute-done.11.rest_1_), channel_id=1, source_target_pairs={{0,24},{8,0},{16,8},{24,16},{1,25},{9,1},{17,9},{25,17},{2,26},{10... | collective-permute-start | bytes 417800 | tf_op jit(solution)/shard_map/ppermute | solution.py:295
  69.5 10.5 %copy-start.7 = (bf16[272,256]{1,0:T(8,128)(2,1)}, bf16[272,256]{1,0:T(8,128)(2,1)S(1)}, u32[]{:S(2)}) copy-start(bf16[272,256]{1,0:T(8,128)(2,1)S(1)} %collective-permute-done.15.rest_5_) | copy-start | bytes 417796
  69.5 6.8 %collective-permute-start.24 = (bf16[272,256]{1,0:T(8,128)(2,1)S(1)}, bf16[272,256]{1,0:T(8,128)(2,1)S(1)}, u32[]{:S(2)}, u32[]{:S(2)}) collective-permute-start(bf16[272,256]{1,0:T(8,128)(2,1)S(1)} %collective-permute-done.16.rest_6_), channel_id=1, source_target_pairs={{0,24},{8,0},{16,8},{24,16},{1,25},{9,1},{17,9},{25,17},{2,26},{10... | collective-permute-start | bytes 417800 | tf_op jit(solution)/shard_map/ppermute | solution.py:295
  70.8 9.2 %copy-start.8 = (bf16[272,256]{1,0:T(8,128)(2,1)}, bf16[272,256]{1,0:T(8,128)(2,1)S(1)}, u32[]{:S(2)}) copy-start(bf16[272,256]{1,0:T(8,128)(2,1)S(1)} %collective-permute-done.20.rest_10_) | copy-start | bytes 417796
  70.8 5.5 %collective-permute-start.23 = (bf16[272,256]{1,0:T(8,128)(2,1)S(1)}, bf16[272,256]{1,0:T(8,128)(2,1)S(1)}, u32[]{:S(2)}, u32[]{:S(2)}) collective-permute-start(bf16[272,256]{1,0:T(8,128)(2,1)S(1)} %collective-permute-done.15.rest_5_), channel_id=1, source_target_pairs={{0,24},{8,0},{16,8},{24,16},{1,25},{9,1},{17,9},{25,17},{2,26},{10... | collective-permute-start | bytes 417800 | tf_op jit(solution)/shard_map/ppermute | solution.py:295
  72.5 7.5 %copy-start.9 = (bf16[272,256]{1,0:T(8,128)(2,1)}, bf16[272,256]{1,0:T(8,128)(2,1)S(1)}, u32[]{:S(2)}) copy-start(bf16[272,256]{1,0:T(8,128)(2,1)S(1)} %collective-permute-done.13.rest_3_) | copy-start | bytes 417796
  72.5 4.7 %collective-permute-start.21 = (bf16[272,256]{1,0:T(8,128)(2,1)S(1)}, bf16[272,256]{1,0:T(8,128)(2,1)S(1)}, u32[]{:S(2)}, u32[]{:S(2)}) collective-permute-start(bf16[272,256]{1,0:T(8,128)(2,1)S(1)} %collective-permute-done.13.rest_3_), channel_id=1, source_target_pairs={{0,24},{8,0},{16,8},{24,16},{1,25},{9,1},{17,9},{25,17},{2,26},{10... | collective-permute-start | bytes 417800 | tf_op jit(solution)/shard_map/ppermute | solution.py:295
  75.4 4.6 %copy-start.10 = (bf16[272,256]{1,0:T(8,128)(2,1)}, bf16[272,256]{1,0:T(8,128)(2,1)S(1)}, u32[]{:S(2)}) copy-start(bf16[272,256]{1,0:T(8,128)(2,1)S(1)} %collective-permute-done.17.rest_7_) | copy-start | bytes 417796
  75.5 4.5 %collective-permute-start.25 = (bf16[272,256]{1,0:T(8,128)(2,1)S(1)}, bf16[272,256]{1,0:T(8,128)(2,1)S(1)}, u32[]{:S(2)}, u32[]{:S(2)}) collective-permute-start(bf16[272,256]{1,0:T(8,128)(2,1)S(1)} %collective-permute-done.17.rest_7_), channel_id=1, source_target_pairs={{0,24},{8,0},{16,8},{24,16},{1,25},{9,1},{17,9},{25,17},{2,26},{10... | collective-permute-start | bytes 417800 | tf_op jit(solution)/shard_map/ppermute | solution.py:295
  76.3 3.7 %copy-start.11 = (bf16[272,256]{1,0:T(8,128)(2,1)}, bf16[272,256]{1,0:T(8,128)(2,1)S(1)}, u32[]{:S(2)}) copy-start(bf16[272,256]{1,0:T(8,128)(2,1)S(1)} %collective-permute-done.19.rest_9_) | copy-start | bytes 417796
  76.3 3.7 %copy-start.12 = (bf16[272,256]{1,0:T(8,128)(2,1)}, bf16[272,256]{1,0:T(8,128)(2,1)S(1)}, u32[]{:S(2)}) copy-start(bf16[272,256]{1,0:T(8,128)(2,1)S(1)} %collective-permute-done.24.rest_14_) | copy-start | bytes 417796
  76.3 3.7 %copy-start.13 = (bf16[272,256]{1,0:T(8,128)(2,1)}, bf16[272,256]{1,0:T(8,128)(2,1)S(1)}, u32[]{:S(2)}) copy-start(bf16[272,256]{1,0:T(8,128)(2,1)S(1)} %collective-permute-done.23.rest_13_) | copy-start | bytes 417796
  77.2 2.9 %copy-start.14 = (bf16[272,256]{1,0:T(8,128)(2,1)}, bf16[272,256]{1,0:T(8,128)(2,1)S(1)}, u32[]{:S(2)}) copy-start(bf16[272,256]{1,0:T(8,128)(2,1)S(1)} %collective-permute-done.21.rest_11_) | copy-start | bytes 417796
  79.9 0.7 copy-start.15

commit v3 on v2

--- a/solution.py
+++ b/solution.py
@@ -25,42 +25,57 @@
     host_ref,
     slot_ref,
     latent_ref,
-    low_ref,
-    high_ref,
-    above_ref,
-    below_ref,
+    low_hbm,
+    high_hbm,
+    above_hbm,
+    below_hbm,
+    wc_hbm,
+    wm_hbm,
+    wi_hbm,
+    wo_hbm,
+    weight_hbm,
     dir_ref,
     mask_ref,
     embed_ref,
-    wc_ref,
     wn_ref,
-    wm_ref,
-    wi_ref,
-    wo_ref,
-    weight_ref,
     refined_ref,
     *rest,
 ):
-    partial_refs = rest[:hosts]
+    partial_hbm = rest[:hosts]
     proj_ref, center_ref, summed_ref, side_ref, total_ref, count_ref, spread_ref = rest[hosts : hosts + 7]
-    cells_ref, result_ref, load_sem, save_sem = rest[hosts + 7 :]
+    cells_ref, result_ref, partial_ref = rest[hosts + 7 : hosts + 10]
+    low_ref, high_ref, above_ref, below_ref = rest[hosts + 10 : hosts + 14]
+    wc_ref, wm_ref, wi_ref, wo_ref, weight_ref = rest[hosts + 14 : hosts + 19]
+    load_sem, save_sem, fetch_sem, partial_sem = rest[hosts + 19 :]
     cells_x, cells_y, width = latent_ref.shape
+    sources = (low_hbm, high_hbm, above_hbm, below_hbm, wc_hbm, wm_hbm, wi_hbm, wo_hbm, weight_hbm)
+    targets = (low_ref, high_ref, above_ref, below_ref, wc_ref, wm_ref, wi_ref, wo_ref, weight_ref)
+    fetches = [
+        pltpu.make_async_copy(source, target, fetch_sem.at[number])
+        for number, (source, target) in enumerate(zip(sources, targets))
+    ]
+    for fetch in fetches[:5]:
+        fetch.start()
     me, strip = lax.axis_index("gy"), lax.axis_index("gx")
     flags = (me > 0, me < hosts - 1, strip > 0, strip < lax.axis_size("gx") - 1)
     chunks = cells_x // rows_per_chunk
+    loaded = 8
+    loads = cells_x // loaded
 
     def load(chunk):
-        part = pl.ds(chunk * rows_per_chunk, rows_per_chunk)
+        part = pl.ds(chunk * loaded, loaded)
         return pltpu.make_async_copy(latent_ref.at[part], cells_ref.at[part], load_sem.at[chunk])
 
     def save(chunk):
         part = pl.ds(chunk * rows_per_chunk, rows_per_chunk)
         return pltpu.make_async_copy(result_ref.at[part], refined_ref.at[part], save_sem.at[chunk])
 
-    for chunk in range(chunks):
+    for chunk in range(loads):
         load(chunk).start()
+    for fetch in fetches[5:]:
+        fetch.start()
     lanes = 128
-    size = partial_refs[0].shape[0]
+    size = partial_hbm[0].shape[0]
     total_ref[...] = jnp.zeros_like(total_ref)
     place = lax.broadcasted_iota(jnp.int32, (cells_y, width), 0)
 
@@ -79,6 +94,8 @@
             place == cells_y - 1, high, pltpu.roll(proj, cells_y - 1, 0)
         )
 
+    for fetch in fetches[:5]:
+        fetch.wait()
     side_ref[0, 1 : cells_x + 1, :] = present(0, project(low_ref[...]))
     side_ref[1, 1 : cells_x + 1, :] = present(1, project(high_ref[...]))
     for ref, number, row in ((above_ref, 2, 0), (below_ref, 3, cells_x + 1)):
@@ -88,15 +105,6 @@
             side_ref[side, row : row + 1, :] = present(side, corner)
         store_row(row, proj[:cells_y])
 
-    def prepare(chunk, carry):
-        first = chunk * rows_per_chunk
-        load(chunk).wait()
-        proj = project(cells_ref[pl.ds(first, rows_per_chunk)].reshape(-1, width))
-        for row in range(rows_per_chunk):
-            store_row(first + row + 1, proj[row * cells_y : (row + 1) * cells_y])
-        return carry
-
-    lax.fori_loop(0, chunks, prepare, 0)
     for d in range(8):
         count = None
         for slot in range(dir_ref.shape[0]):
@@ -115,34 +123,52 @@
             count.astype(BF16), rows, (((0,), (0,)), ((), ())), preferred_element_type=F32
         )
 
+    def prepare(chunk, carry):
+        first = chunk * loaded
+        load(chunk).wait()
+        cells = cells_ref[pl.ds(first, loaded)].reshape(-1, width)
+        proj = project(cells)
+        for row in range(loaded):
+            store_row(first + row + 1, proj[row * cells_y : (row + 1) * cells_y])
+            spread_ref[first + row] = columns(first + row, ones)
+        center_ref[pl.ds(first, loaded)] = dot(cells, wc_ref[...]).reshape(loaded, cells_y, width)
+        return carry
+
+    lax.fori_loop(0, loads, prepare, 0)
+    for fetch in fetches[5:]:
+        fetch.wait()
+
+    parts = [slice(half, half + lanes) for half in range(0, width, lanes)]
+
+    def gather(row, inner):
+        x = row
+        for start in range(0, cells_y, 8):
+            span = slice(start, start + 8)
+            totals = [None] * len(parts)
+            for d in range(8):
+                count = spread_ref[row, span, d * lanes : (d + 1) * lanes]
+                for number, part in enumerate(parts):
+                    near = proj_ref[1 + STEP_Y[d], x + 1 + STEP_X[d], span, part]
+                    hidden = jnp.maximum(
+                        center_ref[row, span, part] + near, lowest[d : d + 1, part]
+                    )
+                    term = count * hidden
+                    total = totals[number]
+                    totals[number] = term if total is None else total + term
+            for number, part in enumerate(parts):
+                summed_ref[row, span, part] = totals[number]
+        return inner
+
+    lax.fori_loop(0, cells_x, gather, 0, unroll=2)
+
     def refine(chunk, carry):
         first = chunk * rows_per_chunk
         cells = cells_ref[pl.ds(first, rows_per_chunk)].reshape(-1, width)
-        center_ref[...] = dot(cells, wc_ref[...]).reshape(rows_per_chunk, cells_y, width)
-        for row in range(rows_per_chunk):
-            spread_ref[row] = columns(first + row, ones)
-
-        def gather(row, inner):
-            x = first + row
-            for start in range(0, cells_y, 16):
-                span = slice(start, start + 16)
-                for half in range(0, width, lanes):
-                    part = slice(half, half + lanes)
-                    center = center_ref[row, span, part]
-                    total = None
-                    for d in range(8):
-                        near = proj_ref[1 + STEP_Y[d], x + 1 + STEP_X[d], span, part]
-                        hidden = jnp.maximum(center + near, lowest[d : d + 1, part])
-                        term = spread_ref[row, span, d * lanes : (d + 1) * lanes] * hidden
-                        total = term if total is None else total + term
-                    summed_ref[row, span, part] = total
-            return inner
-
-        lax.fori_loop(0, rows_per_chunk, gather, 0)
         rest_sum = jnp.concatenate(
             [columns(first + row, embed_ref[...]) for row in range(rows_per_chunk)]
         )
-        summed = (summed_ref[...].reshape(-1, width) + rest_sum).astype(BF16)
+        summed = summed_ref[pl.ds(first, rows_per_chunk)].reshape(-1, width)
+        summed = (summed + rest_sum).astype(BF16)
         aggregate = dot(summed, wm_ref[...]).astype(BF16)
         hidden = dot(cells, wi_ref[:width]) + dot(aggregate, wi_ref[width:])
         hidden = jnp.maximum(hidden, 0.0).astype(BF16)
@@ -161,8 +187,15 @@
         return carry
 
     lax.fori_loop(0, chunks, refine, 0)
+    outs = [
+        pltpu.make_async_copy(partial_ref.at[host], partial_hbm[host], partial_sem.at[host])
+        for host in range(hosts)
+    ]
     for host in range(hosts):
-        partial_refs[host][...] = total_ref[host * size : (host + 1) * size, :].astype(BF16)
+        partial_ref[host] = total_ref[host * size : (host + 1) * size, :].astype(BF16)
+        outs[host].start()
+    for out in outs:
+        out.wait()
     for chunk in range(chunks):
         save(chunk).wait()
 
@@ -184,7 +217,8 @@
     own_refs = rest[:hosts]
     next_refs = rest[hosts : 2 * hosts]
     out_ref, strip_ref, table_ref, rows_ref, dest_ref, summed_ref = rest[2 * hosts : 2 * hosts + 6]
-    cells_ref, result_ref, index_ref, lined_ref, source_ref, load_sem, save_sem, index_sem = rest[2 * hosts + 6 :]
+    cells_ref, result_ref, raise_ref, index_ref, lined_ref, source_ref = rest[2 * hosts + 6 : -3]
+    load_sem, save_sem, index_sem = rest[-3:]
     blocks, rows, _ = weight_ref.shape
     size, width = strip_ref.shape[0] // hosts, strip_ref.shape[1]
     lanes = 128
@@ -204,15 +238,18 @@
             at = 8 * (number * (size // lanes) + part)
             index_ref[at : at + degree, :] = local[:, part * lanes : (part + 1) * lanes]
 
-    def line_up(block, carry):
-        first = cluster_row(block)
-        line = pl.multiple_of(8 * (first // lanes), 8)
-        turned_by = (lanes - first % lanes) % lanes
-        at = pl.ds(pl.multiple_of(8 * block, 8), 8)
-        lined_ref[at, :] = pltpu.roll(index_ref[pl.ds(line, 8), :], turned_by, 1)
-        return carry
-
-    lax.fori_loop(0, blocks, line_up, 0)
+    group = lanes // rows
+    owner = lax.broadcasted_iota(jnp.int32, (8, lanes), 1) // rows
+    for start in range(0, blocks, group):
+        lined = None
+        for part in range(group):
+            first = cluster_row(start + part)
+            line = pl.multiple_of(8 * (first // lanes), 8)
+            turned_by = (lanes + part * rows - first % lanes) % lanes
+            moved = pltpu.roll(index_ref[pl.ds(line, 8), :], turned_by, 1)
+            lined = moved if part == 0 else jnp.where(owner == part, moved, lined)
+        at = 8 * (start // group)
+        lined_ref[at : at + 8, :] = lined
     index_copy = pltpu.make_async_copy(lined_ref, source_ref, index_sem)
     index_copy.start()
 
@@ -240,54 +277,56 @@
 
     index_copy.wait()
 
-    def gather(block, carry):
-        line = 8 * block
-        for row in range(rows):
-            at = pl.ds(pl.multiple_of(2 * (block * rows + row), 2), 2)
-            dest = dest_ref[at, :]
-            total = None
-            for slot in range(degree):
-                source = source_ref[line + slot, row]
-                near = table_ref[pl.ds(pl.multiple_of(source, 2), 2), :]
-                hidden = jnp.maximum(near + dest, 0.0)
-                total = hidden if total is None else total + hidden
-            summed_ref[at, :] = total
+    def gather(number, carry):
+        line = 8 * number
+        for part in range(group):
+            block = number * group + part
+            raise_ref[block] = weight_ref[block].T
+            for row in range(rows):
+                at = pl.ds(pl.multiple_of(2 * (block * rows + row), 2), 2)
+                dest = dest_ref[at, :]
+                total = None
+                for slot in range(degree):
+                    source = source_ref[line + slot, part * rows + row]
+                    near = table_ref[pl.ds(pl.multiple_of(source, 2), 2), :]
+                    hidden = jnp.maximum(near + dest, 0.0)
+                    total = hidden if total is None else total + hidden
+                summed_ref[at, :] = total
         return carry
 
-    lax.fori_loop(0, blocks, gather, 0)
-    step = 8
-    load.wait()
-
-    def save(group):
-        part = pl.ds(group * step, step)
-        return pltpu.make_async_copy(result_ref.at[part], out_ref.at[part], save_sem.at[group])
-
-    def update(group, carry):
-        first = pl.multiple_of(group * step * rows, step * rows)
-        base = rows_ref[pl.ds(first, step * rows), :]
+    lax.fori_loop(0, blocks // group, gather, 0)
+    half_rows = blocks * rows // 2
+    for first in (0, half_rows):
+        base = rows_ref[first : first + half_rows, :]
         summed = jnp.concatenate(
-            [summed_ref[pl.ds(2 * first + part, step * rows, stride=2), :] for part in (0, 1)],
+            [summed_ref[pl.ds(2 * first + part, half_rows, stride=2), :] for part in (0, 1)],
             axis=1,
         ).astype(BF16)
         aggregate = dot(summed, am_ref[...]).astype(BF16)
         hidden = dot(base, bi_ref[:width]) + dot(aggregate, bi_ref[width:])
         hidden = jnp.maximum(hidden, 0.0).astype(BF16)
-        result = (base.astype(F32) + dot(hidden, bo_ref[...])).astype(BF16)
+        rows_ref[first : first + half_rows, :] = (
+            base.astype(F32) + dot(hidden, bo_ref[...])
+        ).astype(BF16)
+    step = 8
+    load.wait()
+
+    def save(number):
+        part = pl.ds(number * step, step)
+        return pltpu.make_async_copy(result_ref.at[part], out_ref.at[part], save_sem.at[number])
+
+    def update(number, carry):
         for part in range(step):
-            block = group * step + part
-            raised = lax.dot_general(
-                weight_ref[block],
-                result[part * rows : (part + 1) * rows],
-                (((0,), (0,)), ((), ())),
-                preferred_element_type=F32,
-            )
+            block = number * step + part
+            at = pl.ds(pl.multiple_of(block * rows, rows), rows)
+            raised = dot(raise_ref[block], rows_ref[at, :])
             result_ref[block] = (cells_ref[block].astype(F32) + raised).astype(BF16)
-        save(group).start()
+        save(number).start()
         return carry
 
     lax.fori_loop(0, blocks // step, update, 0)
-    for group in range(blocks // step):
-        save(group).wait()
+    for number in range(blocks // step):
+        save(number).wait()
 
 
 def turned(value, axis, step):
@@ -341,24 +380,31 @@
     hbm = pl.BlockSpec(memory_space=pl.ANY)
     block_host, block_slot = cluster_host[0, :, 0], cluster_slot[0]
     chunk = 16
+    fetched = (low, high, above, below, w_center, w_msg, w_node_in, w_node_out, weights)
     fine = pl.pallas_call(
         functools.partial(fine_kernel, hosts, chunk),
         out_shape=[jax.ShapeDtypeStruct(fine_latent.shape, BF16)]
         + [jax.ShapeDtypeStruct((size, width), BF16)] * hosts,
-        in_specs=[smem] * 2 + [hbm] + [vmem] * 13,
-        out_specs=[hbm] + [vmem] * hosts,
+        in_specs=[smem] * 2 + [hbm] * 10 + [vmem] * 4,
+        out_specs=[hbm] * (1 + hosts),
         scratch_shapes=[
             pltpu.VMEM((3, cells_x + 2, cells_y, width), F32),
-            pltpu.VMEM((chunk, cells_y, width), F32),
-            pltpu.VMEM((chunk, cells_y, width), F32),
+            pltpu.VMEM((cells_x, cells_y, width), F32),
+            pltpu.VMEM((cells_x, cells_y, width), F32),
             pltpu.VMEM((2, cells_x + 8, width), F32),
             pltpu.VMEM((hosts * size, width), F32),
             pltpu.VMEM((cells_x * 8, cells_y), F32),
-            pltpu.VMEM((chunk, cells_y, 8 * 128), F32),
+            pltpu.VMEM((cells_x, cells_y, 8 * 128), F32),
             pltpu.VMEM(fine_latent.shape, BF16),
             pltpu.VMEM(fine_latent.shape, BF16),
+            pltpu.VMEM((hosts, size, width), BF16),
+        ]
+        + [pltpu.VMEM(value.shape, BF16) for value in fetched]
+        + [
+            pltpu.SemaphoreType.DMA((cells_x // 8,)),
             pltpu.SemaphoreType.DMA((cells_x // chunk,)),
-            pltpu.SemaphoreType.DMA((cells_x // chunk,)),
+            pltpu.SemaphoreType.DMA((len(fetched),)),
+            pltpu.SemaphoreType.DMA((hosts,)),
         ],
         compiler_params=pltpu.CompilerParams(vmem_limit_bytes=VMEM_LIMIT),
         name="fine_cells",
@@ -366,19 +412,11 @@
         block_host,
         block_slot,
         fine_latent,
-        low,
-        high,
-        above,
-        below,
+        *fetched,
         jnp.swapaxes(nbr_dir, 0, 1),
         jnp.swapaxes(nbr_mask, 0, 1),
         dir_embed,
-        w_center,
         w_neighbour,
-        w_msg,
-        w_node_in,
-        w_node_out,
-        weights,
     )
     refined, partial = fine[0], fine[1:]
 
@@ -422,9 +460,10 @@
             pltpu.VMEM((2 * blocks * rows, width // 2), F32),
             pltpu.VMEM(fine_latent.shape, BF16),
             pltpu.VMEM(fine_latent.shape, BF16),
+            pltpu.VMEM((blocks, cells_y, rows), BF16),
             pltpu.VMEM((8 * strip_rows // 128, 128), jnp.int32),
-            pltpu.VMEM((8 * blocks, 128), jnp.int32),
-            pltpu.SMEM((8 * blocks, 128), jnp.int32),
+            pltpu.VMEM((8 * blocks * rows // 128, 128), jnp.int32),
+            pltpu.SMEM((8 * blocks * rows // 128, 128), jnp.int32),
             pltpu.SemaphoreType.DMA(()),
             pltpu.SemaphoreType.DMA((4,)),
             pltpu.SemaphoreType.DMA(()),

time: 97 us -> 91.7 us (0.945)
  Pallas kernels: 33.5 us -> 28.2 us
    pallas_call x1, Pallas kernels: 16.1 us -> 12.2 us  [per_device(): pl.pallas_call(functools.partial(coarse_kernel, hosts, degree), out_shape...]
    pallas_call x1, Pallas kernels: 17.4 us -> 16 us  [per_device(): pl.pallas_call(functools.partial(fine_kernel, hosts, chunk), out_shape=[j...]
  transfers between devices with their start and end apart: 26 -> 26, of which waited for: 13 -> 12; matrix products, arithmetic and copies ran while one was open for 4% -> 4% of each run, Pallas kernels for 0% -> 0%
where the time goes in v3:
time: 91.7 us; the launch traced here: 91.4 us
  starting transfers between devices  38.8 us (42%)
  Pallas kernels  28.2 us (31%)
  waiting for transfers between devices  16.8 us (18%)
  other arithmetic  4.03 us (4%)
  local copies, waits for them, and re-layouts  3.34 us (4%)
    ppermute x14, starting transfers between devices, swapped(): return lax.ppermute(value, axis, [(i, i ^ distance) for i in range(count)])  22.8 us
    ppermute x12, starting transfers between devices, turned(): lax.ppermute(value, axis, [(i, (i + step) % count) for i in range(count)])  16 us
    pallas_call x1, Pallas kernels, per_device(): pl.pallas_call(functools.partial(fine_kernel, hosts, chunk), out_shape=[j...  16 us
    pallas_call x1, Pallas kernels, per_device(): pl.pallas_call(functools.partial(coarse_kernel, hosts, degree), out_shape...  12.2 us
    ppermute x14, waiting for transfers between devices, swapped(): return lax.ppermute(value, axis, [(i, i ^ distance) for i in range(count)])  9.32 us
    ppermute x12, waiting for transfers between devices, turned(): lax.ppermute(value, axis, [(i, (i + step) % count) for i in range(count)])  7.46 us
    convert_element_type x3, other arithmetic, per_device(): parts[far].astype(BF16)  2.82 us
  transfers between devices with their start and end apart: 26, of which 12 were waited for; matrix products, arithmetic and copies ran while one was open for 4% of the time, Pallas kernels for 0%

profile of v3, /device:TPU:1, one launch (start us, length us, event | category | flops | bytes accessed | tf_op | source)
XLA Modules:
  0.0 91.4 jit_solution(2718463723263211682)
XLA Ops:
  0.0 1.0 %fusion.5 = (bf16[32,1,256]{2,1,0:T(2,128)(2,1)S(1)}, bf16[32,1,256]{2,1,0:T(2,128)(2,1)S(1)}) fusion(bf16[32,128,256]{2,1,0:T(8,128)(2,1)} %latent_ref.1), kind=kLoop, calls=%fused_computation.23 | loop fusion | bytes 65536 | tf_op jit(solution)/shard_map/slice | solution.py:374
  1.0 2.1 %collective-permute-start = (bf16[32,256]{1,0:T(8,128)(2,1)S(1)}, bf16[32,256]{1,0:T(8,128)(2,1)S(1)}, u32[]{:S(2)}, u32[]{:S(2)}) collective-permute-start(bf16[32,256]{1,0:T(8,128)(2,1)S(1)} %bitcast.45), channel_id=1, source_target_pairs={{0,1},{1,2},{2,3},{3,4},{4,5},{5,6},{6,7},{7,0},{8,9},{9,10},{10,1... | collective-permute-start | bytes 49160 | tf_op jit(solution)/shard_map/ppermute | solution.py:334
  3.2 3.1 %collective-permute-start.1 = (bf16[32,256]{1,0:T(8,128)(2,1)S(1)}, bf16[32,256]{1,0:T(8,128)(2,1)S(1)}, u32[]{:S(2)}, u32[]{:S(2)}) collective-permute-start(bf16[32,256]{1,0:T(8,128)(2,1)S(1)} %bitcast.46), channel_id=1, source_target_pairs={{0,7},{1,0},{2,1},{3,2},{4,3},{5,4},{6,5},{7,6},{8,15},{9,8},{10,9... | collective-permute-start | bytes 49160 | tf_op jit(solution)/shard_map/ppermute | solution.py:334
  6.3 0.9 slice_bitcast_fusion
  7.2 0.1 pad.11.clone
  7.3 0.1 collective-permute-done.low_hbm
  7.4 0.0 collective-permute-done.1.high_hbm
  7.4 0.1 maximum_maximum_fusion.2
  7.5 1.6 %collective-permute-start.3 = (bf16[144,256]{1,0:T(8,128)(2,1)S(1)}, bf16[144,256]{1,0:T(8,128)(2,1)S(1)}, u32[]{:S(2)}, u32[]{:S(2)}) collective-permute-start(bf16[144,256]{1,0:T(8,128)(2,1)S(1)} %get-tuple-element.33), channel_id=1, source_target_pairs={{0,24},{8,0},{16,8},{24,16},{1,25},{9,1},{17,9},{25,17},{2,26},{10... | collective-permute-start | bytes 221192 | tf_op jit(solution)/shard_map/ppermute | solution.py:334
  9.1 1.3 %collective-permute-start.2 = (bf16[144,256]{1,0:T(8,128)(2,1)S(1)}, bf16[144,256]{1,0:T(8,128)(2,1)S(1)}, u32[]{:S(2)}, u32[]{:S(2)}) collective-permute-start(bf16[144,256]{1,0:T(8,128)(2,1)S(1)} %get-tuple-element.34), channel_id=1, source_target_pairs={{0,8},{8,16},{16,24},{24,0},{1,9},{9,17},{17,25},{25,1},{2,10},{10... | collective-permute-start | bytes 221192 | tf_op jit(solution)/shard_map/ppermute | solution.py:334
  10.4 2.8 %collective-permute-done.3.below_hbm = bf16[144,256]{1,0:T(8,128)(2,1)S(1)} collective-permute-done((bf16[144,256]{1,0:T(8,128)(2,1)S(1)}, bf16[144,256]{1,0:T(8,128)(2,1)S(1)}, u32[]{:S(2)}, u32[]{:S(2)}) %collective-permute-start.3) | collective-permute-done | bytes 73760 | tf_op jit(solution)/shard_map/ppermute | solution.py:334
  13.2 0.0 collective-permute-done.2.above_hbm
  13.2 0.6 copy-done.16
  13.8 0.0 copy-done.17
  13.8 16.0 %fine_cells.1 = (bf16[32,128,256]{2,1,0:T(8,128)(2,1)}, bf16[256,256]{1,0:T(8,128)(2,1)}, bf16[256,256]{1,0:T(8,128)(2,1)}, bf16[256,256]{1,0:T(8,128)(2,1)}, bf...) custom-call(s32[32]{0:T(128)} %bitcast.47, ...), custom_call_target="tpu_custom_call" | custom-call | tf_op jit(solution)/shard_map/fine_cells/pallas_call | solution.py:384
  29.9 1.2 %collective-permute-start.5 = (bf16[256,256]{1,0:T(8,128)(2,1)}, bf16[256,256]{1,0:T(8,128)(2,1)S(1)}, u32[]{:S(2)}, u32[]{:S(2)}) collective-permute-start(bf16[256,256]{1,0:T(8,128)(2,1)} %get-tuple-element.18), channel_id=1, source_target_pairs={{0,1},{1,0},{2,3},{3,2},{4,5},{5,4},{6,7},{7,6},{8,9},{9,8},{10,11... | collective-permute-start | bytes 393224 | tf_op jit(solution)/shard_map/ppermute | solution.py:339
  31.1 0.1 pad.3.clone
  31.2 0.3 collective-permute-start.4
  31.5 1.2 %collective-permute-start.7 = (bf16[256,256]{1,0:T(8,128)(2,1)}, bf16[256,256]{1,0:T(8,128)(2,1)S(1)}, u32[]{:S(2)}, u32[]{:S(2)}) collective-permute-start(bf16[256,256]{1,0:T(8,128)(2,1)} %get-tuple-element.20), channel_id=1, source_target_pairs={{0,1},{1,0},{2,3},{3,2},{4,5},{5,4},{6,7},{7,6},{8,9},{9,8},{10,11... | collective-permute-start | bytes 393224 | tf_op jit(solution)/shard_map/ppermute | solution.py:339
  32.7 0.3 collective-permute-start.9
  33.0 1.9 %collective-permute-done.5 = bf16[256,256]{1,0:T(8,128)(2,1)S(1)} collective-permute-done((bf16[256,256]{1,0:T(8,128)(2,1)}, bf16[256,256]{1,0:T(8,128)(2,1)S(1)}, u32[]{:S(2)}, u32[]{:S(2)}) %collective-permute-start.5) | collective-permute-done | bytes 131104 | tf_op jit(solution)/shard_map/ppermute | solution.py:339
  34.9 0.9 %add_convert_fusion.3 = bf16[256,256]{1,0:T(8,128)(2,1)S(1)} fusion(bf16[256,256]{1,0:T(8,128)(2,1)S(1)} %collective-permute-done.5, bf16[256,256]{1,0:T(8,128)(2,1)} %get-tuple-element.17), kind=kLoop, calls=%fused_computation.3 | loop fusion | flops 262144 | bytes 393216 | tf_op jit(solution)/shard_map/convert_element_type | solution.py:431
  35.8 3.7 %collective-permute-start.6 = (bf16[256,256]{1,0:T(8,128)(2,1)S(1)}, bf16[256,256]{1,0:T(8,128)(2,1)S(1)}, u32[]{:S(2)}, u32[]{:S(2)}) collective-permute-start(bf16[256,256]{1,0:T(8,128)(2,1)S(1)} %add_convert_fusion.3), channel_id=1, source_target_pairs={{0,6},{1,7},{2,4},{3,5},{4,2},{5,3},{6,0},{7,1},{8,14},{9,15},{10,... | collective-permute-start | bytes 393224 | tf_op jit(solution)/shard_map/ppermute | solution.py:339
  39.6 0.9 %collective-permute-done.7 = bf16[256,256]{1,0:T(8,128)(2,1)S(1)} collective-permute-done((bf16[256,256]{1,0:T(8,128)(2,1)}, bf16[256,256]{1,0:T(8,128)(2,1)S(1)}, u32[]{:S(2)}, u32[]{:S(2)}) %collective-permute-start.7) | collective-permute-done | bytes 131104 | tf_op jit(solution)/shard_map/ppermute | solution.py:339
  40.5 0.9 %add_convert_fusion.2 = bf16[256,256]{1,0:T(8,128)(2,1)S(1)} fusion(bf16[256,256]{1,0:T(8,128)(2,1)S(1)} %collective-permute-done.7, bf16[256,256]{1,0:T(8,128)(2,1)} %get-tuple-element.19), kind=kLoop, calls=%fused_computation.2 | loop fusion | flops 262144 | bytes 393216 | tf_op jit(solution)/shard_map/convert_element_type | solution.py:431
  41.4 2.4 %collective-permute-start.8 = (bf16[256,256]{1,0:T(8,128)(2,1)S(1)}, bf16[256,256]{1,0:T(8,128)(2,1)S(1)}, u32[]{:S(2)}, u32[]{:S(2)}) collective-permute-start(bf16[256,256]{1,0:T(8,128)(2,1)S(1)} %add_convert_fusion.2), channel_id=1, source_target_pairs={{0,4},{1,5},{2,6},{3,7},{4,0},{5,1},{6,2},{7,3},{8,12},{9,13},{10,... | collective-permute-start | bytes 393224 | tf_op jit(solution)/shard_map/ppermute | solution.py:339
  43.8 0.0 collective-permute-done.9
  43.8 0.9 %add_convert_fusion.1 = bf16[256,256]{1,0:T(8,128)(2,1)S(1)} fusion(bf16[256,256]{1,0:T(8,128)(2,1)S(1)} %collective-permute-done.9, bf16[256,256]{1,0:T(8,128)(2,1)} %get-tuple-element.21), kind=kLoop, calls=%fused_computation.1 | loop fusion | flops 262144 | bytes 393216 | tf_op jit(solution)/shard_map/convert_element_type | solution.py:431
  44.8 1.7 %collective-permute-start.10 = (bf16[256,256]{1,0:T(8,128)(2,1)S(1)}, bf16[256,256]{1,0:T(8,128)(2,1)S(1)}, u32[]{:S(2)}, u32[]{:S(2)}) collective-permute-start(bf16[256,256]{1,0:T(8,128)(2,1)S(1)} %add_convert_fusion.1), channel_id=1, source_target_pairs={{0,2},{1,3},{2,0},{3,1},{4,6},{5,7},{6,4},{7,5},{8,10},{9,11},{10,... | collective-permute-start | bytes 393224 | tf_op jit(solution)/shard_map/ppermute | solution.py:339
  46.5 0.0 collective-permute-done.4
  46.5 0.0 collective-permute-done.6
  46.5 3.0 %collective-permute-done.8 = bf16[256,256]{1,0:T(8,128)(2,1)S(1)} collective-permute-done((bf16[256,256]{1,0:T(8,128)(2,1)S(1)}, bf16[256,256]{1,0:T(8,128)(2,1)S(1)}, u32[]{:S(2)}, u32[]{:S(2)}) %collective-permute-start.8) | collective-permute-done | bytes 131104 | tf_op jit(solution)/shard_map/ppermute | solution.py:339
  49.5 0.0 collective-permute-done.10
  49.5 1.0 %add_convert_fusion = bf16[256,256]{1,0:T(8,128)(2,1)S(1)} fusion(bf16[256,256]{1,0:T(8,128)(2,1)S(1)} %collective-permute-done.10, bf16[256,256]{1,0:T(8,128)(2,1)S(1)} %collective-permute-done.8, bf16[256,256]{1,0:T(8,128)(2,1)S(1)} %collective-permute-done.6, bf16[256,256]{1,0:T(8,128)(2,1)S(1)} %collective-permute-done.4, bf16[256,256]{1,0:T(8,128)(2,1)} %get-tuple-element.15), kind=kLoop, calls=%fused_computation | loop fusion | flops 655360 | bytes 786432 | tf_op jit(solution)/shard_map/convert_element_type | solution.py:436
  50.5 0.1 maximum_maximum_fusion.rest_0_
  50.6 3.7 %collective-permute-start.14 = (bf16[272,256]{1,0:T(8,128)(2,1)S(1)}, bf16[272,256]{1,0:T(8,128)(2,1)S(1)}, u32[]{:S(2)}, u32[]{:S(2)}) collective-permute-start(bf16[272,256]{1,0:T(8,128)(2,1)S(1)} %maximum_maximum_fusion.rest_0_), channel_id=1, source_target_pairs={{0,4},{1,5},{2,6},{3,7},{4,0},{5,1},{6,2},{7,3},{8,12},{9,13},{10,... | collective-permute-start | bytes 417800 | tf_op jit(solution)/shard_map/ppermute | solution.py:339
  54.3 1.5 %collective-permute-start.18 = (bf16[272,256]{1,0:T(8,128)(2,1)S(1)}, bf16[272,256]{1,0:T(8,128)(2,1)S(1)}, u32[]{:S(2)}, u32[]{:S(2)}) collective-permute-start(bf16[272,256]{1,0:T(8,128)(2,1)S(1)} %maximum_maximum_fusion.rest_0_), channel_id=1, source_target_pairs={{0,24},{8,0},{16,8},{24,16},{1,25},{9,1},{17,9},{25,17},{2,26},{10... | collective-permute-start | bytes 417800 | tf_op jit(solution)/shard_map/ppermute | solution.py:334
  55.8 2.2 %collective-permute-start.12 = (bf16[272,256]{1,0:T(8,128)(2,1)S(1)}, bf16[272,256]{1,0:T(8,128)(2,1)S(1)}, u32[]{:S(2)}, u32[]{:S(2)}) collective-permute-start(bf16[272,256]{1,0:T(8,128)(2,1)S(1)} %maximum_maximum_fusion.rest_0_), channel_id=1, source_target_pairs={{0,2},{1,3},{2,0},{3,1},{4,6},{5,7},{6,4},{7,5},{8,10},{9,11},{10,... | collective-permute-start | bytes 417800 | tf_op jit(solution)/shard_map/ppermute | solution.py:339
  58.0 0.6 collective-permute-start.11
  58.7 0.0 collective-permute-done.14.rest_4_
  58.7 3.1 %collective-permute-start.16 = (bf16[272,256]{1,0:T(8,128)(2,1)S(1)}, bf16[272,256]{1,0:T(8,128)(2,1)S(1)}, u32[]{:S(2)}, u32[]{:S(2)}) collective-permute-start(bf16[272,256]{1,0:T(8,128)(2,1)S(1)} %collective-permute-done.14.rest_4_), channel_id=1, source_target_pairs={{0,2},{1,3},{2,0},{3,1},{4,6},{5,7},{6,4},{7,5},{8,10},{9,11},{10,... | collective-permute-start | bytes 417800 | tf_op jit(solution)/shard_map/ppermute | solution.py:339
  61.8 1.1 %collective-permute-start.22 = (bf16[272,256]{1,0:T(8,128)(2,1)S(1)}, bf16[272,256]{1,0:T(8,128)(2,1)S(1)}, u32[]{:S(2)}, u32[]{:S(2)}) collective-permute-start(bf16[272,256]{1,0:T(8,128)(2,1)S(1)} %collective-permute-done.14.rest_4_), channel_id=1, source_target_pairs={{0,24},{8,0},{16,8},{24,16},{1,25},{9,1},{17,9},{25,17},{2,26},{10... | collective-permute-start | bytes 417800 | tf_op jit(solution)/shard_map/ppermute | solution.py:334
  62.9 0.0 collective-permute-done.18.rest_8_
  62.9 0.9 collective-permute-start.15
  63.8 0.0 collective-permute-done.12.rest_2_
  63.8 0.4 collective-permute-start.20
  64.1 0.0 collective-permute-done.11.rest_1_
  64.1 0.6 collective-permute-start.13
  64.7 0.1 collective-permute-done.16.rest_6_
  64.8 0.8 collective-permute-start.17
  65.6 1.0 %collective-permute-done.22.rest_12_ = bf16[272,256]{1,0:T(8,128)(2,1)S(1)} collective-permute-done((bf16[272,256]{1,0:T(8,128)(2,1)S(1)}, bf16[272,256]{1,0:T(8,128)(2,1)S(1)}, u32[]{:S(2)}, u32[]{:S(2)}) %collective-permute-start.22) | collective-permute-done | bytes 139296 | tf_op jit(solution)/shard_map/ppermute | solution.py:334
  66.6 1.4 %collective-permute-start.19 = (bf16[272,256]{1,0:T(8,128)(2,1)S(1)}, bf16[272,256]{1,0:T(8,128)(2,1)S(1)}, u32[]{:S(2)}, u32[]{:S(2)}) collective-permute-start(bf16[272,256]{1,0:T(8,128)(2,1)S(1)} %collective-permute-done.11.rest_1_), channel_id=1, source_target_pairs={{0,24},{8,0},{16,8},{24,16},{1,25},{9,1},{17,9},{25,17},{2,26},{10... | collective-permute-start | bytes 417800 | tf_op jit(solution)/shard_map/ppermute | solution.py:334
  68.0 0.1 collective-permute-done.15.rest_5_
  68.1 1.3 %collective-permute-start.24 = (bf16[272,256]{1,0:T(8,128)(2,1)S(1)}, bf16[272,256]{1,0:T(8,128)(2,1)S(1)}, u32[]{:S(2)}, u32[]{:S(2)}) collective-permute-start(bf16[272,256]{1,0:T(8,128)(2,1)S(1)} %collective-permute-done.16.rest_6_), channel_id=1, source_target_pairs={{0,24},{8,0},{16,8},{24,16},{1,25},{9,1},{17,9},{25,17},{2,26},{10... | collective-permute-start | bytes 417800 | tf_op jit(solution)/shard_map/ppermute | solution.py:334
  69.4 0.1 collective-permute-start.23
  69.5 1.6 %collective-permute-done.13.rest_3_ = bf16[272,256]{1,0:T(8,128)(2,1)S(1)} collective-permute-done((bf16[272,256]{1,0:T(8,128)(2,1)S(1)}, bf16[272,256]{1,0:T(8,128)(2,1)S(1)}, u32[]{:S(2)}, u32[]{:S(2)}) %collective-permute-start.13) | collective-permute-done | bytes 139296 | tf_op jit(solution)/shard_map/ppermute | solution.py:339
  71.1 1.3 %collective-permute-start.21 = (bf16[272,256]{1,0:T(8,128)(2,1)S(1)}, bf16[272,256]{1,0:T(8,128)(2,1)S(1)}, u32[]{:S(2)}, u32[]{:S(2)}) collective-permute-start(bf16[272,256]{1,0:T(8,128)(2,1)S(1)} %collective-permute-done.13.rest_3_), channel_id=1, source_target_pairs={{0,24},{8,0},{16,8},{24,16},{1,25},{9,1},{17,9},{25,17},{2,26},{10... | collective-permute-start | bytes 417800 | tf_op jit(solution)/shard_map/ppermute | solution.py:334
  72.4 1.7 %collective-permute-done.17.rest_7_ = bf16[272,256]{1,0:T(8,128)(2,1)S(1)} collective-permute-done((bf16[272,256]{1,0:T(8,128)(2,1)S(1)}, bf16[272,256]{1,0:T(8,128)(2,1)S(1)}, u32[]{:S(2)}, u32[]{:S(2)}) %collective-permute-start.17) | collective-permute-done | bytes 139296 | tf_op jit(solution)/shard_map/ppermute | solution.py:339
  74.1 0.9 collective-permute-start.25
  75.0 0.0 collective-permute-done.23.rest_13_
  75.0 0.8 collective-permute-done.21.rest_11_
  75.8 2.7 %collective-permute-done.25.rest_15_ = bf16[272,256]{1,0:T(8,128)(2,1)S(1)} collective-permute-done((bf16[272,256]{1,0:T(8,128)(2,1)S(1)}, bf16[272,256]{1,0:T(8,128)(2,1)S(1)}, u32[]{:S(2)}, u32[]{:S(2)}) %collective-permute-start.25) | collective-permute-done | bytes 139296 | tf_op jit(solution)/shard_map/ppermute | solution.py:334
  78.7 0.5 copy-done.15
  79.2 12.2 %coarse_rows.1 = bf16[32,128,256]{2,1,0:T(8,128)(2,1)} custom-call(s32[32]{0:T(128)} %bitcast.48, s32[32]{0:T(128)} %bitcast.50, bf16[32,128,256]{2,1,0:T(8,128)(2,1)} %get-tuple-element.14.refined_ref, bf16[32,32,128]{2,1,0:T(8,128)(2,1)} %bitcast.42, bf16[256,256]{1,0:T(8,128)(2,1)} %as_ref.1, bf16[256,256]{1,0:T(8,128)(2,1)} %ad_ref.1, ...), custom_call_target="tpu_custom_call" | custom-call | tf_op jit(solution)/shard_map/coarse_rows/pallas_call | solution.py:450
  (49 shorter events, 0.1 us)
Async XLA Ops:
  1.0 6.3 %collective-permute-start = (bf16[32,256]{1,0:T(8,128)(2,1)S(1)}, bf16[32,256]{1,0:T(8,128)(2,1)S(1)}, u32[]{:S(2)}, u32[]{:S(2)}) collective-permute-start(bf16[32,256]{1,0:T(8,128)(2,1)S(1)} %bitcast.45), channel_id=1, source_target_pairs={{0,1},{1,2},{2,3},{3,4},{4,5},{5,6},{6,7},{7,0},{8,9},{9,10},{10,1... | collective-permute-start | bytes 49160 | tf_op jit(solution)/shard_map/ppermute | solution.py:334
  3.2 4.2 %collective-permute-start.1 = (bf16[32,256]{1,0:T(8,128)(2,1)S(1)}, bf16[32,256]{1,0:T(8,128)(2,1)S(1)}, u32[]{:S(2)}, u32[]{:S(2)}) collective-permute-start(bf16[32,256]{1,0:T(8,128)(2,1)S(1)} %bitcast.46), channel_id=1, source_target_pairs={{0,7},{1,0},{2,1},{3,2},{4,3},{5,4},{6,5},{7,6},{8,15},{9,8},{10,9... | collective-permute-start | bytes 49160 | tf_op jit(solution)/shard_map/ppermute | solution.py:334
  7.3 5.9 %copy-start.18 = (bf16[32,256]{1,0:T(8,128)(2,1)}, bf16[32,256]{1,0:T(8,128)(2,1)S(1)}, u32[]{:S(2)}) copy-start(bf16[32,256]{1,0:T(8,128)(2,1)S(1)} %collective-permute-done.low_hbm) | copy-start | bytes 49156
  7.4 5.8 %copy-start.19 = (bf16[32,256]{1,0:T(8,128)(2,1)}, bf16[32,256]{1,0:T(8,128)(2,1)S(1)}, u32[]{:S(2)}) copy-start(bf16[32,256]{1,0:T(8,128)(2,1)S(1)} %collective-permute-done.1.high_hbm) | copy-start | bytes 49156
  7.5 5.7 %collective-permute-start.3 = (bf16[144,256]{1,0:T(8,128)(2,1)S(1)}, bf16[144,256]{1,0:T(8,128)(2,1)S(1)}, u32[]{:S(2)}, u32[]{:S(2)}) collective-permute-start(bf16[144,256]{1,0:T(8,128)(2,1)S(1)} %get-tuple-element.33), channel_id=1, source_target_pairs={{0,24},{8,0},{16,8},{24,16},{1,25},{9,1},{17,9},{25,17},{2,26},{10... | collective-permute-start | bytes 221192 | tf_op jit(solution)/shard_map/ppermute | solution.py:334
  9.1 4.1 %collective-permute-start.2 = (bf16[144,256]{1,0:T(8,128)(2,1)S(1)}, bf16[144,256]{1,0:T(8,128)(2,1)S(1)}, u32[]{:S(2)}, u32[]{:S(2)}) collective-permute-start(bf16[144,256]{1,0:T(8,128)(2,1)S(1)} %get-tuple-element.34), channel_id=1, source_target_pairs={{0,8},{8,16},{16,24},{24,0},{1,9},{9,17},{17,25},{25,1},{2,10},{10... | collective-permute-start | bytes 221192 | tf_op jit(solution)/shard_map/ppermute | solution.py:334
  13.2 0.6 copy-start.16
  13.2 0.7 copy-start.17
  13.8 32.6 %copy-start.20 = (s32[256,6]{0,1:T(8,128)S(1)}, s32[256,6]{0,1:T(8,128)}, u32[]{:S(2)}) copy-start(s32[256,6]{0,1:T(8,128)} %param.30) | copy-start | bytes 18436
  29.9 5.0 %collective-permute-start.5 = (bf16[256,256]{1,0:T(8,128)(2,1)}, bf16[256,256]{1,0:T(8,128)(2,1)S(1)}, u32[]{:S(2)}, u32[]{:S(2)}) collective-permute-start(bf16[256,256]{1,0:T(8,128)(2,1)} %get-tuple-element.18), channel_id=1, source_target_pairs={{0,1},{1,0},{2,3},{3,2},{4,5},{5,4},{6,7},{7,6},{8,9},{9,8},{10,11... | collective-permute-start | bytes 393224 | tf_op jit(solution)/shard_map/ppermute | solution.py:339
  31.2 15.3 %collective-permute-start.4 = (bf16[256,256]{1,0:T(8,128)(2,1)}, bf16[256,256]{1,0:T(8,128)(2,1)S(1)}, u32[]{:S(2)}, u32[]{:S(2)}) collective-permute-start(bf16[256,256]{1,0:T(8,128)(2,1)} %get-tuple-element.16), channel_id=1, source_target_pairs={{0,1},{1,0},{2,3},{3,2},{4,5},{5,4},{6,7},{7,6},{8,9},{9,8},{10,11... | collective-permute-start | bytes 393224 | tf_op jit(solution)/shard_map/ppermute | solution.py:339
  31.5 9.0 %collective-permute-start.7 = (bf16[256,256]{1,0:T(8,128)(2,1)}, bf16[256,256]{1,0:T(8,128)(2,1)S(1)}, u32[]{:S(2)}, u32[]{:S(2)}) collective-permute-start(bf16[256,256]{1,0:T(8,128)(2,1)} %get-tuple-element.20), channel_id=1, source_target_pairs={{0,1},{1,0},{2,3},{3,2},{4,5},{5,4},{6,7},{7,6},{8,9},{9,8},{10,11... | collective-permute-start | bytes 393224 | tf_op jit(solution)/shard_map/ppermute | solution.py:339
  32.7 11.2 %collective-permute-start.9 = (bf16[256,256]{1,0:T(8,128)(2,1)}, bf16[256,256]{1,0:T(8,128)(2,1)S(1)}, u32[]{:S(2)}, u32[]{:S(2)}) collective-permute-start(bf16[256,256]{1,0:T(8,128)(2,1)} %get-tuple-element.22), channel_id=1, source_target_pairs={{0,1},{1,0},{2,3},{3,2},{4,5},{5,4},{6,7},{7,6},{8,9},{9,8},{10,11... | collective-permute-start | bytes 393224 | tf_op jit(solution)/shard_map/ppermute | solution.py:339
  35.8 10.7 %collective-permute-start.6 = (bf16[256,256]{1,0:T(8,128)(2,1)S(1)}, bf16[256,256]{1,0:T(8,128)(2,1)S(1)}, u32[]{:S(2)}, u32[]{:S(2)}) collective-permute-start(bf16[256,256]{1,0:T(8,128)(2,1)S(1)} %add_convert_fusion.3), channel_id=1, source_target_pairs={{0,6},{1,7},{2,4},{3,5},{4,2},{5,3},{6,0},{7,1},{8,14},{9,15},{10,... | collective-permute-start | bytes 393224 | tf_op jit(solution)/shard_map/ppermute | solution.py:339
  41.4 8.1 %collective-permute-start.8 = (bf16[256,256]{1,0:T(8,128)(2,1)S(1)}, bf16[256,256]{1,0:T(8,128)(2,1)S(1)}, u32[]{:S(2)}, u32[]{:S(2)}) collective-permute-start(bf16[256,256]{1,0:T(8,128)(2,1)S(1)} %add_convert_fusion.2), channel_id=1, source_target_pairs={{0,4},{1,5},{2,6},{3,7},{4,0},{5,1},{6,2},{7,3},{8,12},{9,13},{10,... | collective-permute-start | bytes 393224 | tf_op jit(solution)/shard_map/ppermute | solution.py:339
  44.8 4.7 %collective-permute-start.10 = (bf16[256,256]{1,0:T(8,128)(2,1)S(1)}, bf16[256,256]{1,0:T(8,128)(2,1)S(1)}, u32[]{:S(2)}, u32[]{:S(2)}) collective-permute-start(bf16[256,256]{1,0:T(8,128)(2,1)S(1)} %add_convert_fusion.1), channel_id=1, source_target_pairs={{0,2},{1,3},{2,0},{3,1},{4,6},{5,7},{6,4},{7,5},{8,10},{9,11},{10,... | collective-permute-start | bytes 393224 | tf_op jit(solution)/shard_map/ppermute | solution.py:339
  50.6 27.9 %copy-start = (bf16[272,256]{1,0:T(8,128)(2,1)}, bf16[272,256]{1,0:T(8,128)(2,1)S(1)}, u32[]{:S(2)}) copy-start(bf16[272,256]{1,0:T(8,128)(2,1)S(1)} %maximum_maximum_fusion.rest_0_) | copy-start | bytes 417796
  50.6 8.0 %collective-permute-start.14 = (bf16[272,256]{1,0:T(8,128)(2,1)S(1)}, bf16[272,256]{1,0:T(8,128)(2,1)S(1)}, u32[]{:S(2)}, u32[]{:S(2)}) collective-permute-start(bf16[272,256]{1,0:T(8,128)(2,1)S(1)} %maximum_maximum_fusion.rest_0_), channel_id=1, source_target_pairs={{0,4},{1,5},{2,6},{3,7},{4,0},{5,1},{6,2},{7,3},{8,12},{9,13},{10,... | collective-permute-start | bytes 417800 | tf_op jit(solution)/shard_map/ppermute | solution.py:339
  54.3 8.6 %collective-permute-start.18 = (bf16[272,256]{1,0:T(8,128)(2,1)S(1)}, bf16[272,256]{1,0:T(8,128)(2,1)S(1)}, u32[]{:S(2)}, u32[]{:S(2)}) collective-permute-start(bf16[272,256]{1,0:T(8,128)(2,1)S(1)} %maximum_maximum_fusion.rest_0_), channel_id=1, source_target_pairs={{0,24},{8,0},{16,8},{24,16},{1,25},{9,1},{17,9},{25,17},{2,26},{10... | collective-permute-start | bytes 417800 | tf_op jit(solution)/shard_map/ppermute | solution.py:334
  55.8 7.9 %collective-permute-start.12 = (bf16[272,256]{1,0:T(8,128)(2,1)S(1)}, bf16[272,256]{1,0:T(8,128)(2,1)S(1)}, u32[]{:S(2)}, u32[]{:S(2)}) collective-permute-start(bf16[272,256]{1,0:T(8,128)(2,1)S(1)} %maximum_maximum_fusion.rest_0_), channel_id=1, source_target_pairs={{0,2},{1,3},{2,0},{3,1},{4,6},{5,7},{6,4},{7,5},{8,10},{9,11},{10,... | collective-permute-start | bytes 417800 | tf_op jit(solution)/shard_map/ppermute | solution.py:339
  58.0 6.1 %collective-permute-start.11 = (bf16[272,256]{1,0:T(8,128)(2,1)S(1)}, bf16[272,256]{1,0:T(8,128)(2,1)S(1)}, u32[]{:S(2)}, u32[]{:S(2)}) collective-permute-start(bf16[272,256]{1,0:T(8,128)(2,1)S(1)} %maximum_maximum_fusion.rest_0_), channel_id=1, source_target_pairs={{0,1},{1,0},{2,3},{3,2},{4,5},{5,4},{6,7},{7,6},{8,9},{9,8},{10,11... | collective-permute-start | bytes 417800 | tf_op jit(solution)/shard_map/ppermute | solution.py:339
  58.7 19.9 %copy-start.1 = (bf16[272,256]{1,0:T(8,128)(2,1)}, bf16[272,256]{1,0:T(8,128)(2,1)S(1)}, u32[]{:S(2)}) copy-start(bf16[272,256]{1,0:T(8,128)(2,1)S(1)} %collective-permute-done.14.rest_4_) | copy-start | bytes 417796
  58.7 6.1 %collective-permute-start.16 = (bf16[272,256]{1,0:T(8,128)(2,1)S(1)}, bf16[272,256]{1,0:T(8,128)(2,1)S(1)}, u32[]{:S(2)}, u32[]{:S(2)}) collective-permute-start(bf16[272,256]{1,0:T(8,128)(2,1)S(1)} %collective-permute-done.14.rest_4_), channel_id=1, source_target_pairs={{0,2},{1,3},{2,0},{3,1},{4,6},{5,7},{6,4},{7,5},{8,10},{9,11},{10,... | collective-permute-start | bytes 417800 | tf_op jit(solution)/shard_map/ppermute | solution.py:339
  61.8 4.8 %collective-permute-start.22 = (bf16[272,256]{1,0:T(8,128)(2,1)S(1)}, bf16[272,256]{1,0:T(8,128)(2,1)S(1)}, u32[]{:S(2)}, u32[]{:S(2)}) collective-permute-start(bf16[272,256]{1,0:T(8,128)(2,1)S(1)} %collective-permute-done.14.rest_4_), channel_id=1, source_target_pairs={{0,24},{8,0},{16,8},{24,16},{1,25},{9,1},{17,9},{25,17},{2,26},{10... | collective-permute-start | bytes 417800 | tf_op jit(solution)/shard_map/ppermute | solution.py:334
  62.9 15.7 %copy-start.2 = (bf16[272,256]{1,0:T(8,128)(2,1)}, bf16[272,256]{1,0:T(8,128)(2,1)S(1)}, u32[]{:S(2)}) copy-start(bf16[272,256]{1,0:T(8,128)(2,1)S(1)} %collective-permute-done.18.rest_8_) | copy-start | bytes 417796
  62.9 5.2 %collective-permute-start.15 = (bf16[272,256]{1,0:T(8,128)(2,1)S(1)}, bf16[272,256]{1,0:T(8,128)(2,1)S(1)}, u32[]{:S(2)}, u32[]{:S(2)}) collective-permute-start(bf16[272,256]{1,0:T(8,128)(2,1)S(1)} %collective-permute-done.14.rest_4_), channel_id=1, source_target_pairs={{0,1},{1,0},{2,3},{3,2},{4,5},{5,4},{6,7},{7,6},{8,9},{9,8},{10,11... | collective-permute-start | bytes 417800 | tf_op jit(solution)/shard_map/ppermute | solution.py:339
  63.8 14.8 %copy-start.3 = (bf16[272,256]{1,0:T(8,128)(2,1)}, bf16[272,256]{1,0:T(8,128)(2,1)S(1)}, u32[]{:S(2)}) copy-start(bf16[272,256]{1,0:T(8,128)(2,1)S(1)} %collective-permute-done.12.rest_2_) | copy-start | bytes 417796
  63.8 5.7 %collective-permute-start.20 = (bf16[272,256]{1,0:T(8,128)(2,1)S(1)}, bf16[272,256]{1,0:T(8,128)(2,1)S(1)}, u32[]{:S(2)}, u32[]{:S(2)}) collective-permute-start(bf16[272,256]{1,0:T(8,128)(2,1)S(1)} %collective-permute-done.12.rest_2_), channel_id=1, source_target_pairs={{0,24},{8,0},{16,8},{24,16},{1,25},{9,1},{17,9},{25,17},{2,26},{10... | collective-permute-start | bytes 417800 | tf_op jit(solution)/shard_map/ppermute | solution.py:334
  64.1 14.5 %copy-start.4 = (bf16[272,256]{1,0:T(8,128)(2,1)}, bf16[272,256]{1,0:T(8,128)(2,1)S(1)}, u32[]{:S(2)}) copy-start(bf16[272,256]{1,0:T(8,128)(2,1)S(1)} %collective-permute-done.11.rest_1_) | copy-start | bytes 417796
  64.1 7.0 %collective-permute-start.13 = (bf16[272,256]{1,0:T(8,128)(2,1)S(1)}, bf16[272,256]{1,0:T(8,128)(2,1)S(1)}, u32[]{:S(2)}, u32[]{:S(2)}) collective-permute-start(bf16[272,256]{1,0:T(8,128)(2,1)S(1)} %collective-permute-done.12.rest_2_), channel_id=1, source_target_pairs={{0,1},{1,0},{2,3},{3,2},{4,5},{5,4},{6,7},{7,6},{8,9},{9,8},{10,11... | collective-permute-start | bytes 417800 | tf_op jit(solution)/shard_map/ppermute | solution.py:339
  64.8 13.8 %copy-start.5 = (bf16[272,256]{1,0:T(8,128)(2,1)}, bf16[272,256]{1,0:T(8,128)(2,1)S(1)}, u32[]{:S(2)}) copy-start(bf16[272,256]{1,0:T(8,128)(2,1)S(1)} %collective-permute-done.16.rest_6_) | copy-start | bytes 417796
  64.8 9.3 %collective-permute-start.17 = (bf16[272,256]{1,0:T(8,128)(2,1)S(1)}, bf16[272,256]{1,0:T(8,128)(2,1)S(1)}, u32[]{:S(2)}, u32[]{:S(2)}) collective-permute-start(bf16[272,256]{1,0:T(8,128)(2,1)S(1)} %collective-permute-done.16.rest_6_), channel_id=1, source_target_pairs={{0,1},{1,0},{2,3},{3,2},{4,5},{5,4},{6,7},{7,6},{8,9},{9,8},{10,11... | collective-permute-start | bytes 417800 | tf_op jit(solution)/shard_map/ppermute | solution.py:339
  66.6 12.0 %copy-start.6 = (bf16[272,256]{1,0:T(8,128)(2,1)}, bf16[272,256]{1,0:T(8,128)(2,1)S(1)}, u32[]{:S(2)}) copy-start(bf16[272,256]{1,0:T(8,128)(2,1)S(1)} %collective-permute-done.22.rest_12_) | copy-start | bytes 417796
  66.6 8.4 %collective-permute-start.19 = (bf16[272,256]{1,0:T(8,128)(2,1)S(1)}, bf16[272,256]{1,0:T(8,128)(2,1)S(1)}, u32[]{:S(2)}, u32[]{:S(2)}) collective-permute-start(bf16[272,256]{1,0:T(8,128)(2,1)S(1)} %collective-permute-done.11.rest_1_), channel_id=1, source_target_pairs={{0,24},{8,0},{16,8},{24,16},{1,25},{9,1},{17,9},{25,17},{2,26},{10... | collective-permute-start | bytes 417800 | tf_op jit(solution)/shard_map/ppermute | solution.py:334
  68.1 10.5 %copy-start.7 = (bf16[272,256]{1,0:T(8,128)(2,1)}, bf16[272,256]{1,0:T(8,128)(2,1)S(1)}, u32[]{:S(2)}) copy-start(bf16[272,256]{1,0:T(8,128)(2,1)S(1)} %collective-permute-done.15.rest_5_) | copy-start | bytes 417796
  68.1 6.8 %collective-permute-start.24 = (bf16[272,256]{1,0:T(8,128)(2,1)S(1)}, bf16[272,256]{1,0:T(8,128)(2,1)S(1)}, u32[]{:S(2)}, u32[]{:S(2)}) collective-permute-start(bf16[272,256]{1,0:T(8,128)(2,1)S(1)} %collective-permute-done.16.rest_6_), channel_id=1, source_target_pairs={{0,24},{8,0},{16,8},{24,16},{1,25},{9,1},{17,9},{25,17},{2,26},{10... | collective-permute-start | bytes 417800 | tf_op jit(solution)/shard_map/ppermute | solution.py:334
  69.4 9.2 %copy-start.8 = (bf16[272,256]{1,0:T(8,128)(2,1)}, bf16[272,256]{1,0:T(8,128)(2,1)S(1)}, u32[]{:S(2)}) copy-start(bf16[272,256]{1,0:T(8,128)(2,1)S(1)} %collective-permute-done.20.rest_10_) | copy-start | bytes 417796
  69.4 5.5 %collective-permute-start.23 = (bf16[272,256]{1,0:T(8,128)(2,1)S(1)}, bf16[272,256]{1,0:T(8,128)(2,1)S(1)}, u32[]{:S(2)}, u32[]{:S(2)}) collective-permute-start(bf16[272,256]{1,0:T(8,128)(2,1)S(1)} %collective-permute-done.15.rest_5_), channel_id=1, source_target_pairs={{0,24},{8,0},{16,8},{24,16},{1,25},{9,1},{17,9},{25,17},{2,26},{10... | collective-permute-start | bytes 417800 | tf_op jit(solution)/shard_map/ppermute | solution.py:334
  71.1 7.5 %copy-start.9 = (bf16[272,256]{1,0:T(8,128)(2,1)}, bf16[272,256]{1,0:T(8,128)(2,1)S(1)}, u32[]{:S(2)}) copy-start(bf16[272,256]{1,0:T(8,128)(2,1)S(1)} %collective-permute-done.13.rest_3_) | copy-start | bytes 417796
  71.1 4.7 %collective-permute-start.21 = (bf16[272,256]{1,0:T(8,128)(2,1)S(1)}, bf16[272,256]{1,0:T(8,128)(2,1)S(1)}, u32[]{:S(2)}, u32[]{:S(2)}) collective-permute-start(bf16[272,256]{1,0:T(8,128)(2,1)S(1)} %collective-permute-done.13.rest_3_), channel_id=1, source_target_pairs={{0,24},{8,0},{16,8},{24,16},{1,25},{9,1},{17,9},{25,17},{2,26},{10... | collective-permute-start | bytes 417800 | tf_op jit(solution)/shard_map/ppermute | solution.py:334
  74.1 4.6 %copy-start.10 = (bf16[272,256]{1,0:T(8,128)(2,1)}, bf16[272,256]{1,0:T(8,128)(2,1)S(1)}, u32[]{:S(2)}) copy-start(bf16[272,256]{1,0:T(8,128)(2,1)S(1)} %collective-permute-done.17.rest_7_) | copy-start | bytes 417796
  74.1 4.5 %collective-permute-start.25 = (bf16[272,256]{1,0:T(8,128)(2,1)S(1)}, bf16[272,256]{1,0:T(8,128)(2,1)S(1)}, u32[]{:S(2)}, u32[]{:S(2)}) collective-permute-start(bf16[272,256]{1,0:T(8,128)(2,1)S(1)} %collective-permute-done.17.rest_7_), channel_id=1, source_target_pairs={{0,24},{8,0},{16,8},{24,16},{1,25},{9,1},{17,9},{25,17},{2,26},{10... | collective-permute-start | bytes 417800 | tf_op jit(solution)/shard_map/ppermute | solution.py:334
  75.0 3.7 %copy-start.11 = (bf16[272,256]{1,0:T(8,128)(2,1)}, bf16[272,256]{1,0:T(8,128)(2,1)S(1)}, u32[]{:S(2)}) copy-start(bf16[272,256]{1,0:T(8,128)(2,1)S(1)} %collective-permute-done.19.rest_9_) | copy-start | bytes 417796
  75.0 3.7 %copy-start.12 = (bf16[272,256]{1,0:T(8,128)(2,1)}, bf16[272,256]{1,0:T(8,128)(2,1)S(1)}, u32[]{:S(2)}) copy-start(bf16[272,256]{1,0:T(8,128)(2,1)S(1)} %collective-permute-done.24.rest_14_) | copy-start | bytes 417796
  75.0 3.7 %copy-start.13 = (bf16[272,256]{1,0:T(8,128)(2,1)}, bf16[272,256]{1,0:T(8,128)(2,1)S(1)}, u32[]{:S(2)}) copy-start(bf16[272,256]{1,0:T(8,128)(2,1)S(1)} %collective-permute-done.23.rest_13_) | copy-start | bytes 417796
  75.8 2.9 %copy-start.14 = (bf16[272,256]{1,0:T(8,128)(2,1)}, bf16[272,256]{1,0:T(8,128)(2,1)S(1)}, u32[]{:S(2)}) copy-start(bf16[272,256]{1,0:T(8,128)(2,1)S(1)} %collective-permute-done.21.rest_11_) | copy-start | bytes 417796
  78.6 0.7 copy-start.15

commit v4 on v3

--- a/solution.py
+++ b/solution.py
@@ -420,15 +420,23 @@
     )
     refined, partial = fine[0], fine[1:]
 
-    parts = {}
-    for far in reversed(range(outer)):
-        total = partial[far * inner].astype(F32)
+    half = outer // 2
+    parts = [value.astype(F32) for value in partial]
+
+    def arrive(target, number, distance):
+        parts[target] = parts[target] + swapped(partial[number], "gy", distance).astype(F32)
+
+    for far in range(half + 1, outer):
         for near in range(1, inner):
-            total = total + swapped(partial[far * inner + near], "gy", near).astype(F32)
-        parts[far] = total
+            arrive(near, far * inner + near, far * inner)
+        arrive(half * inner, far * inner, (far - half) * inner)
+    for far in range(half, 0, -1):
+        for near in range(1, inner):
+            arrive(far * inner, far * inner + near, near)
     coarse_in = parts[0]
-    for far in reversed(range(1, outer)):
-        coarse_in = coarse_in + swapped(parts[far].astype(BF16), "gy", far * inner).astype(F32)
+    for number in [far * inner for far in range(half, 0, -1)] + list(range(1, inner)):
+        coarse_in = coarse_in + swapped(parts[number].astype(BF16), "gy", number).astype(F32)
+
     strip_rows = hosts * size
     local = coarse_src.T - lax.axis_index("gx") * strip_rows
     digits = [(local // DIGIT).astype(BF16), (local % DIGIT).astype(BF16)]

time: 91.7 us -> 90.8 us (level)
    ppermute x14, starting transfers between devices: 22.8 us -> 16.2 us  [swapped(): return lax.ppermute(value, axis, [(i, i ^ distance) for i in range(count)])]
    ppermute x12, starting transfers between devices: 16 us -> 22 us  [turned(): lax.ppermute(value, axis, [(i, (i + step) % count) for i in range(count)])]
  transfers between devices with their start and end apart: 26 -> 26, of which waited for: 12 -> 9; matrix products, arithmetic and copies ran while one was open for 4% -> 4% of each run, Pallas kernels for 0% -> 0%
where the time goes in v4:
time: 90.8 us; the launch traced here: 90.5 us
  starting transfers between devices  38.1 us (42%)
  Pallas kernels  28.2 us (31%)
  waiting for transfers between devices  16.5 us (18%)
  other arithmetic  4.03 us (4%)
  local copies, waits for them, and re-layouts  3.34 us (4%)
    ppermute x12, starting transfers between devices, turned(): lax.ppermute(value, axis, [(i, (i + step) % count) for i in range(count)])  22 us
    ppermute x14, starting transfers between devices, swapped(): return lax.ppermute(value, axis, [(i, i ^ distance) for i in range(count)])  16.2 us
    pallas_call x1, Pallas kernels, per_device(): pl.pallas_call(functools.partial(fine_kernel, hosts, chunk), out_shape=[j...  16 us
    pallas_call x1, Pallas kernels, per_device(): pl.pallas_call(functools.partial(coarse_kernel, hosts, degree), out_shape...  12.2 us
    ppermute x14, waiting for transfers between devices, swapped(): return lax.ppermute(value, axis, [(i, i ^ distance) for i in range(count)])  9.74 us
    ppermute x12, waiting for transfers between devices, turned(): lax.ppermute(value, axis, [(i, (i + step) % count) for i in range(count)])  6.71 us
    convert_element_type x3, other arithmetic, per_device(): parts[number].astype(BF16)  2.84 us
  transfers between devices with their start and end apart: 26, of which 9 were waited for; matrix products, arithmetic and copies ran while one was open for 4% of the time, Pallas kernels for 0%

profile of v4, /device:TPU:1, one launch (start us, length us, event | category | flops | bytes accessed | tf_op | source)
XLA Modules:
  0.0 90.5 jit_solution(17192771796990216122)
XLA Ops:
  0.0 1.0 %fusion.5 = (bf16[32,1,256]{2,1,0:T(2,128)(2,1)S(1)}, bf16[32,1,256]{2,1,0:T(2,128)(2,1)S(1)}) fusion(bf16[32,128,256]{2,1,0:T(8,128)(2,1)} %latent_ref.1), kind=kLoop, calls=%fused_computation.23 | loop fusion | bytes 65536 | tf_op jit(solution)/shard_map/slice | solution.py:374
  1.0 2.1 %collective-permute-start = (bf16[32,256]{1,0:T(8,128)(2,1)S(1)}, bf16[32,256]{1,0:T(8,128)(2,1)S(1)}, u32[]{:S(2)}, u32[]{:S(2)}) collective-permute-start(bf16[32,256]{1,0:T(8,128)(2,1)S(1)} %bitcast.45), channel_id=1, source_target_pairs={{0,1},{1,2},{2,3},{3,4},{4,5},{5,6},{6,7},{7,0},{8,9},{9,10},{10,1... | collective-permute-start | bytes 49160 | tf_op jit(solution)/shard_map/ppermute | solution.py:334
  3.2 3.1 %collective-permute-start.1 = (bf16[32,256]{1,0:T(8,128)(2,1)S(1)}, bf16[32,256]{1,0:T(8,128)(2,1)S(1)}, u32[]{:S(2)}, u32[]{:S(2)}) collective-permute-start(bf16[32,256]{1,0:T(8,128)(2,1)S(1)} %bitcast.46), channel_id=1, source_target_pairs={{0,7},{1,0},{2,1},{3,2},{4,3},{5,4},{6,5},{7,6},{8,15},{9,8},{10,9... | collective-permute-start | bytes 49160 | tf_op jit(solution)/shard_map/ppermute | solution.py:334
  6.3 0.9 slice_bitcast_fusion
  7.2 0.1 pad.11.clone
  7.3 0.1 collective-permute-done.low_hbm
  7.4 0.0 collective-permute-done.1.high_hbm
  7.4 0.1 maximum_maximum_fusion.2
  7.5 1.6 %collective-permute-start.3 = (bf16[144,256]{1,0:T(8,128)(2,1)S(1)}, bf16[144,256]{1,0:T(8,128)(2,1)S(1)}, u32[]{:S(2)}, u32[]{:S(2)}) collective-permute-start(bf16[144,256]{1,0:T(8,128)(2,1)S(1)} %get-tuple-element.33), channel_id=1, source_target_pairs={{0,24},{8,0},{16,8},{24,16},{1,25},{9,1},{17,9},{25,17},{2,26},{10... | collective-permute-start | bytes 221192 | tf_op jit(solution)/shard_map/ppermute | solution.py:334
  9.1 1.3 %collective-permute-start.2 = (bf16[144,256]{1,0:T(8,128)(2,1)S(1)}, bf16[144,256]{1,0:T(8,128)(2,1)S(1)}, u32[]{:S(2)}, u32[]{:S(2)}) collective-permute-start(bf16[144,256]{1,0:T(8,128)(2,1)S(1)} %get-tuple-element.34), channel_id=1, source_target_pairs={{0,8},{8,16},{16,24},{24,0},{1,9},{9,17},{17,25},{25,1},{2,10},{10... | collective-permute-start | bytes 221192 | tf_op jit(solution)/shard_map/ppermute | solution.py:334
  10.4 2.8 %collective-permute-done.3.below_hbm = bf16[144,256]{1,0:T(8,128)(2,1)S(1)} collective-permute-done((bf16[144,256]{1,0:T(8,128)(2,1)S(1)}, bf16[144,256]{1,0:T(8,128)(2,1)S(1)}, u32[]{:S(2)}, u32[]{:S(2)}) %collective-permute-start.3) | collective-permute-done | bytes 73760 | tf_op jit(solution)/shard_map/ppermute | solution.py:334
  13.2 0.0 collective-permute-done.2.above_hbm
  13.2 0.6 copy-done.16
  13.8 0.0 copy-done.17
  13.8 16.0 %fine_cells.1 = (bf16[32,128,256]{2,1,0:T(8,128)(2,1)}, bf16[256,256]{1,0:T(8,128)(2,1)}, bf16[256,256]{1,0:T(8,128)(2,1)}, bf16[256,256]{1,0:T(8,128)(2,1)}, bf...) custom-call(s32[32]{0:T(128)} %bitcast.47, ...), custom_call_target="tpu_custom_call" | custom-call | tf_op jit(solution)/shard_map/fine_cells/pallas_call | solution.py:384
  29.9 0.4 collective-permute-start.4
  30.3 2.1 %collective-permute-start.5 = (bf16[256,256]{1,0:T(8,128)(2,1)}, bf16[256,256]{1,0:T(8,128)(2,1)S(1)}, u32[]{:S(2)}, u32[]{:S(2)}) collective-permute-start(bf16[256,256]{1,0:T(8,128)(2,1)} %get-tuple-element.18), channel_id=1, source_target_pairs={{0,1},{1,0},{2,3},{3,2},{4,5},{5,4},{6,7},{7,6},{8,9},{9,8},{10,11... | collective-permute-start | bytes 393224 | tf_op jit(solution)/shard_map/ppermute | solution.py:339
  32.4 0.1 pad.3.clone
  32.5 0.0 collective-permute-start.7
  32.5 2.5 %collective-permute-start.9 = (bf16[256,256]{1,0:T(8,128)(2,1)}, bf16[256,256]{1,0:T(8,128)(2,1)S(1)}, u32[]{:S(2)}, u32[]{:S(2)}) collective-permute-start(bf16[256,256]{1,0:T(8,128)(2,1)} %get-tuple-element.22), channel_id=1, source_target_pairs={{0,6},{1,7},{2,4},{3,5},{4,2},{5,3},{6,0},{7,1},{8,14},{9,15},{10,... | collective-permute-start | bytes 393224 | tf_op jit(solution)/shard_map/ppermute | solution.py:339
  35.0 0.0 collective-permute-done.4
  35.0 0.9 collective-permute-done.5
  35.9 1.0 %add_convert_fusion.3 = bf16[256,256]{1,0:T(8,128)(2,1)S(1)} fusion(bf16[256,256]{1,0:T(8,128)(2,1)S(1)} %collective-permute-done.5, bf16[256,256]{1,0:T(8,128)(2,1)S(1)} %collective-permute-done.4, bf16[256,256]{1,0:T(8,128)(2,1)} %get-tuple-element.16), kind=kLoop, calls=%fused_computation.3 | loop fusion | flops 393216 | bytes 524288 | tf_op jit(solution)/shard_map/convert_element_type | solution.py:438
  36.8 2.7 %collective-permute-start.6 = (bf16[256,256]{1,0:T(8,128)(2,1)S(1)}, bf16[256,256]{1,0:T(8,128)(2,1)S(1)}, u32[]{:S(2)}, u32[]{:S(2)}) collective-permute-start(bf16[256,256]{1,0:T(8,128)(2,1)S(1)} %add_convert_fusion.3), channel_id=1, source_target_pairs={{0,4},{1,5},{2,6},{3,7},{4,0},{5,1},{6,2},{7,3},{8,12},{9,13},{10,... | collective-permute-start | bytes 393224 | tf_op jit(solution)/shard_map/ppermute | solution.py:339
  39.5 0.0 collective-permute-done.7
  39.5 0.9 %add_convert_fusion.2 = bf16[256,256]{1,0:T(8,128)(2,1)S(1)} fusion(bf16[256,256]{1,0:T(8,128)(2,1)S(1)} %collective-permute-done.7, bf16[256,256]{1,0:T(8,128)(2,1)} %get-tuple-element.19), kind=kLoop, calls=%fused_computation.2 | loop fusion | flops 262144 | bytes 393216 | tf_op jit(solution)/shard_map/convert_element_type | solution.py:438
  40.5 0.4 collective-permute-start.8
  40.9 0.0 collective-permute-done.9
  40.9 0.9 %add_convert_fusion.1 = bf16[256,256]{1,0:T(8,128)(2,1)S(1)} fusion(bf16[256,256]{1,0:T(8,128)(2,1)S(1)} %collective-permute-done.9, bf16[256,256]{1,0:T(8,128)(2,1)} %get-tuple-element.21), kind=kLoop, calls=%fused_computation.1 | loop fusion | flops 262144 | bytes 393216 | tf_op jit(solution)/shard_map/convert_element_type | solution.py:438
  41.8 1.2 %collective-permute-start.10 = (bf16[256,256]{1,0:T(8,128)(2,1)S(1)}, bf16[256,256]{1,0:T(8,128)(2,1)S(1)}, u32[]{:S(2)}, u32[]{:S(2)}) collective-permute-start(bf16[256,256]{1,0:T(8,128)(2,1)S(1)} %add_convert_fusion.1), channel_id=1, source_target_pairs={{0,1},{1,0},{2,3},{3,2},{4,5},{5,4},{6,7},{7,6},{8,9},{9,8},{10,11... | collective-permute-start | bytes 393224 | tf_op jit(solution)/shard_map/ppermute | solution.py:339
  43.1 4.1 %collective-permute-done.6 = bf16[256,256]{1,0:T(8,128)(2,1)S(1)} collective-permute-done((bf16[256,256]{1,0:T(8,128)(2,1)S(1)}, bf16[256,256]{1,0:T(8,128)(2,1)S(1)}, u32[]{:S(2)}, u32[]{:S(2)}) %collective-permute-start.6) | collective-permute-done | bytes 131104 | tf_op jit(solution)/shard_map/ppermute | solution.py:339
  47.2 0.0 collective-permute-done.8
  47.2 0.0 collective-permute-done.10
  47.2 1.0 %add_convert_fusion = bf16[256,256]{1,0:T(8,128)(2,1)S(1)} fusion(bf16[256,256]{1,0:T(8,128)(2,1)S(1)} %collective-permute-done.10, bf16[256,256]{1,0:T(8,128)(2,1)S(1)} %collective-permute-done.8, bf16[256,256]{1,0:T(8,128)(2,1)S(1)} %collective-permute-done.6, bf16[256,256]{1,0:T(8,128)(2,1)} %get-tuple-element.15), kind=kLoop, calls=%fused_computation | loop fusion | flops 524288 | bytes 655360 | tf_op jit(solution)/shard_map/convert_element_type | solution.py:444
  48.2 0.1 maximum_maximum_fusion.rest_0_
  48.3 0.9 %collective-permute-start.14 = (bf16[272,256]{1,0:T(8,128)(2,1)S(1)}, bf16[272,256]{1,0:T(8,128)(2,1)S(1)}, u32[]{:S(2)}, u32[]{:S(2)}) collective-permute-start(bf16[272,256]{1,0:T(8,128)(2,1)S(1)} %maximum_maximum_fusion.rest_0_), channel_id=1, source_target_pairs={{0,4},{1,5},{2,6},{3,7},{4,0},{5,1},{6,2},{7,3},{8,12},{9,13},{10,... | collective-permute-start | bytes 417800 | tf_op jit(solution)/shard_map/ppermute | solution.py:339
  49.2 5.0 %collective-permute-start.18 = (bf16[272,256]{1,0:T(8,128)(2,1)S(1)}, bf16[272,256]{1,0:T(8,128)(2,1)S(1)}, u32[]{:S(2)}, u32[]{:S(2)}) collective-permute-start(bf16[272,256]{1,0:T(8,128)(2,1)S(1)} %maximum_maximum_fusion.rest_0_), channel_id=1, source_target_pairs={{0,24},{8,0},{16,8},{24,16},{1,25},{9,1},{17,9},{25,17},{2,26},{10... | collective-permute-start | bytes 417800 | tf_op jit(solution)/shard_map/ppermute | solution.py:334
  54.2 0.0 collective-permute-start.12
  54.2 1.4 %collective-permute-start.11 = (bf16[272,256]{1,0:T(8,128)(2,1)S(1)}, bf16[272,256]{1,0:T(8,128)(2,1)S(1)}, u32[]{:S(2)}, u32[]{:S(2)}) collective-permute-start(bf16[272,256]{1,0:T(8,128)(2,1)S(1)} %maximum_maximum_fusion.rest_0_), channel_id=1, source_target_pairs={{0,1},{1,0},{2,3},{3,2},{4,5},{5,4},{6,7},{7,6},{8,9},{9,8},{10,11... | collective-permute-start | bytes 417800 | tf_op jit(solution)/shard_map/ppermute | solution.py:339
  55.5 1.2 %collective-permute-start.16 = (bf16[272,256]{1,0:T(8,128)(2,1)S(1)}, bf16[272,256]{1,0:T(8,128)(2,1)S(1)}, u32[]{:S(2)}, u32[]{:S(2)}) collective-permute-start(bf16[272,256]{1,0:T(8,128)(2,1)S(1)} %collective-permute-done.14.rest_4_), channel_id=1, source_target_pairs={{0,2},{1,3},{2,0},{3,1},{4,6},{5,7},{6,4},{7,5},{8,10},{9,11},{10,... | collective-permute-start | bytes 417800 | tf_op jit(solution)/shard_map/ppermute | solution.py:339
  56.7 4.5 %collective-permute-start.22 = (bf16[272,256]{1,0:T(8,128)(2,1)S(1)}, bf16[272,256]{1,0:T(8,128)(2,1)S(1)}, u32[]{:S(2)}, u32[]{:S(2)}) collective-permute-start(bf16[272,256]{1,0:T(8,128)(2,1)S(1)} %collective-permute-done.14.rest_4_), channel_id=1, source_target_pairs={{0,24},{8,0},{16,8},{24,16},{1,25},{9,1},{17,9},{25,17},{2,26},{10... | collective-permute-start | bytes 417800 | tf_op jit(solution)/shard_map/ppermute | solution.py:334
  61.3 0.0 collective-permute-done.18.rest_8_
  61.3 1.9 %collective-permute-start.15 = (bf16[272,256]{1,0:T(8,128)(2,1)S(1)}, bf16[272,256]{1,0:T(8,128)(2,1)S(1)}, u32[]{:S(2)}, u32[]{:S(2)}) collective-permute-start(bf16[272,256]{1,0:T(8,128)(2,1)S(1)} %collective-permute-done.14.rest_4_), channel_id=1, source_target_pairs={{0,1},{1,0},{2,3},{3,2},{4,5},{5,4},{6,7},{7,6},{8,9},{9,8},{10,11... | collective-permute-start | bytes 417800 | tf_op jit(solution)/shard_map/ppermute | solution.py:339
  63.2 0.0 collective-permute-done.12.rest_2_
  63.2 0.4 collective-permute-start.20
  63.5 0.0 collective-permute-start.13
  63.5 0.0 collective-permute-done.16.rest_6_
  63.6 1.5 %collective-permute-start.17 = (bf16[272,256]{1,0:T(8,128)(2,1)S(1)}, bf16[272,256]{1,0:T(8,128)(2,1)S(1)}, u32[]{:S(2)}, u32[]{:S(2)}) collective-permute-start(bf16[272,256]{1,0:T(8,128)(2,1)S(1)} %collective-permute-done.16.rest_6_), channel_id=1, source_target_pairs={{0,1},{1,0},{2,3},{3,2},{4,5},{5,4},{6,7},{7,6},{8,9},{9,8},{10,11... | collective-permute-start | bytes 417800 | tf_op jit(solution)/shard_map/ppermute | solution.py:339
  65.0 0.0 collective-permute-done.22.rest_12_
  65.0 1.5 %collective-permute-start.19 = (bf16[272,256]{1,0:T(8,128)(2,1)S(1)}, bf16[272,256]{1,0:T(8,128)(2,1)S(1)}, u32[]{:S(2)}, u32[]{:S(2)}) collective-permute-start(bf16[272,256]{1,0:T(8,128)(2,1)S(1)} %collective-permute-done.11.rest_1_), channel_id=1, source_target_pairs={{0,24},{8,0},{16,8},{24,16},{1,25},{9,1},{17,9},{25,17},{2,26},{10... | collective-permute-start | bytes 417800 | tf_op jit(solution)/shard_map/ppermute | solution.py:334
  66.5 0.7 collective-permute-done.15.rest_5_
  67.2 0.9 %collective-permute-start.24 = (bf16[272,256]{1,0:T(8,128)(2,1)S(1)}, bf16[272,256]{1,0:T(8,128)(2,1)S(1)}, u32[]{:S(2)}, u32[]{:S(2)}) collective-permute-start(bf16[272,256]{1,0:T(8,128)(2,1)S(1)} %collective-permute-done.16.rest_6_), channel_id=1, source_target_pairs={{0,24},{8,0},{16,8},{24,16},{1,25},{9,1},{17,9},{25,17},{2,26},{10... | collective-permute-start | bytes 417800 | tf_op jit(solution)/shard_map/ppermute | solution.py:334
  68.1 0.0 collective-permute-done.20.rest_10_
  68.1 0.1 collective-permute-start.23
  68.1 2.0 %collective-permute-done.13.rest_3_ = bf16[272,256]{1,0:T(8,128)(2,1)S(1)} collective-permute-done((bf16[272,256]{1,0:T(8,128)(2,1)S(1)}, bf16[272,256]{1,0:T(8,128)(2,1)S(1)}, u32[]{:S(2)}, u32[]{:S(2)}) %collective-permute-start.13) | collective-permute-done | bytes 139296 | tf_op jit(solution)/shard_map/ppermute | solution.py:339
  70.1 0.9 %collective-permute-start.21 = (bf16[272,256]{1,0:T(8,128)(2,1)S(1)}, bf16[272,256]{1,0:T(8,128)(2,1)S(1)}, u32[]{:S(2)}, u32[]{:S(2)}) collective-permute-start(bf16[272,256]{1,0:T(8,128)(2,1)S(1)} %collective-permute-done.13.rest_3_), channel_id=1, source_target_pairs={{0,24},{8,0},{16,8},{24,16},{1,25},{9,1},{17,9},{25,17},{2,26},{10... | collective-permute-start | bytes 417800 | tf_op jit(solution)/shard_map/ppermute | solution.py:334
  71.0 2.1 %collective-permute-done.17.rest_7_ = bf16[272,256]{1,0:T(8,128)(2,1)S(1)} collective-permute-done((bf16[272,256]{1,0:T(8,128)(2,1)S(1)}, bf16[272,256]{1,0:T(8,128)(2,1)S(1)}, u32[]{:S(2)}, u32[]{:S(2)}) %collective-permute-start.17) | collective-permute-done | bytes 139296 | tf_op jit(solution)/shard_map/ppermute | solution.py:339
  73.1 0.7 collective-permute-start.25
  73.8 0.0 collective-permute-done.19.rest_9_
  73.8 0.0 collective-permute-done.24.rest_14_
  73.8 0.8 collective-permute-done.21.rest_11_
  74.6 3.0 %collective-permute-done.25.rest_15_ = bf16[272,256]{1,0:T(8,128)(2,1)S(1)} collective-permute-done((bf16[272,256]{1,0:T(8,128)(2,1)S(1)}, bf16[272,256]{1,0:T(8,128)(2,1)S(1)}, u32[]{:S(2)}, u32[]{:S(2)}) %collective-permute-start.25) | collective-permute-done | bytes 139296 | tf_op jit(solution)/shard_map/ppermute | solution.py:334
  77.7 0.5 copy-done.15
  78.3 12.2 %coarse_rows.1 = bf16[32,128,256]{2,1,0:T(8,128)(2,1)} custom-call(s32[32]{0:T(128)} %bitcast.48, s32[32]{0:T(128)} %bitcast.50, bf16[32,128,256]{2,1,0:T(8,128)(2,1)} %get-tuple-element.14.refined_ref, bf16[32,32,128]{2,1,0:T(8,128)(2,1)} %bitcast.42, bf16[256,256]{1,0:T(8,128)(2,1)} %as_ref.1, bf16[256,256]{1,0:T(8,128)(2,1)} %ad_ref.1, ...), custom_call_target="tpu_custom_call" | custom-call | tf_op jit(solution)/shard_map/coarse_rows/pallas_call | solution.py:458
  (49 shorter events, 0.1 us)
Async XLA Ops:
  1.0 6.3 %collective-permute-start = (bf16[32,256]{1,0:T(8,128)(2,1)S(1)}, bf16[32,256]{1,0:T(8,128)(2,1)S(1)}, u32[]{:S(2)}, u32[]{:S(2)}) collective-permute-start(bf16[32,256]{1,0:T(8,128)(2,1)S(1)} %bitcast.45), channel_id=1, source_target_pairs={{0,1},{1,2},{2,3},{3,4},{4,5},{5,6},{6,7},{7,0},{8,9},{9,10},{10,1... | collective-permute-start | bytes 49160 | tf_op jit(solution)/shard_map/ppermute | solution.py:334
  3.2 4.2 %collective-permute-start.1 = (bf16[32,256]{1,0:T(8,128)(2,1)S(1)}, bf16[32,256]{1,0:T(8,128)(2,1)S(1)}, u32[]{:S(2)}, u32[]{:S(2)}) collective-permute-start(bf16[32,256]{1,0:T(8,128)(2,1)S(1)} %bitcast.46), channel_id=1, source_target_pairs={{0,7},{1,0},{2,1},{3,2},{4,3},{5,4},{6,5},{7,6},{8,15},{9,8},{10,9... | collective-permute-start | bytes 49160 | tf_op jit(solution)/shard_map/ppermute | solution.py:334
  7.3 5.9 %copy-start.18 = (bf16[32,256]{1,0:T(8,128)(2,1)}, bf16[32,256]{1,0:T(8,128)(2,1)S(1)}, u32[]{:S(2)}) copy-start(bf16[32,256]{1,0:T(8,128)(2,1)S(1)} %collective-permute-done.low_hbm) | copy-start | bytes 49156
  7.4 5.8 %copy-start.19 = (bf16[32,256]{1,0:T(8,128)(2,1)}, bf16[32,256]{1,0:T(8,128)(2,1)S(1)}, u32[]{:S(2)}) copy-start(bf16[32,256]{1,0:T(8,128)(2,1)S(1)} %collective-permute-done.1.high_hbm) | copy-start | bytes 49156
  7.5 5.7 %collective-permute-start.3 = (bf16[144,256]{1,0:T(8,128)(2,1)S(1)}, bf16[144,256]{1,0:T(8,128)(2,1)S(1)}, u32[]{:S(2)}, u32[]{:S(2)}) collective-permute-start(bf16[144,256]{1,0:T(8,128)(2,1)S(1)} %get-tuple-element.33), channel_id=1, source_target_pairs={{0,24},{8,0},{16,8},{24,16},{1,25},{9,1},{17,9},{25,17},{2,26},{10... | collective-permute-start | bytes 221192 | tf_op jit(solution)/shard_map/ppermute | solution.py:334
  9.1 4.1 %collective-permute-start.2 = (bf16[144,256]{1,0:T(8,128)(2,1)S(1)}, bf16[144,256]{1,0:T(8,128)(2,1)S(1)}, u32[]{:S(2)}, u32[]{:S(2)}) collective-permute-start(bf16[144,256]{1,0:T(8,128)(2,1)S(1)} %get-tuple-element.34), channel_id=1, source_target_pairs={{0,8},{8,16},{16,24},{24,0},{1,9},{9,17},{17,25},{25,1},{2,10},{10... | collective-permute-start | bytes 221192 | tf_op jit(solution)/shard_map/ppermute | solution.py:334
  13.2 0.6 copy-start.16
  13.2 0.7 copy-start.17
  13.8 29.2 %copy-start.20 = (s32[256,6]{0,1:T(8,128)S(1)}, s32[256,6]{0,1:T(8,128)}, u32[]{:S(2)}) copy-start(s32[256,6]{0,1:T(8,128)} %param.30) | copy-start | bytes 18436
  29.9 5.1 %collective-permute-start.4 = (bf16[256,256]{1,0:T(8,128)(2,1)}, bf16[256,256]{1,0:T(8,128)(2,1)S(1)}, u32[]{:S(2)}, u32[]{:S(2)}) collective-permute-start(bf16[256,256]{1,0:T(8,128)(2,1)} %get-tuple-element.17), channel_id=1, source_target_pairs={{0,2},{1,3},{2,0},{3,1},{4,6},{5,7},{6,4},{7,5},{8,10},{9,11},{10,... | collective-permute-start | bytes 393224 | tf_op jit(solution)/shard_map/ppermute | solution.py:339
  30.3 5.6 %collective-permute-start.5 = (bf16[256,256]{1,0:T(8,128)(2,1)}, bf16[256,256]{1,0:T(8,128)(2,1)S(1)}, u32[]{:S(2)}, u32[]{:S(2)}) collective-permute-start(bf16[256,256]{1,0:T(8,128)(2,1)} %get-tuple-element.18), channel_id=1, source_target_pairs={{0,1},{1,0},{2,3},{3,2},{4,5},{5,4},{6,7},{7,6},{8,9},{9,8},{10,11... | collective-permute-start | bytes 393224 | tf_op jit(solution)/shard_map/ppermute | solution.py:339
  32.5 7.0 %collective-permute-start.7 = (bf16[256,256]{1,0:T(8,128)(2,1)}, bf16[256,256]{1,0:T(8,128)(2,1)S(1)}, u32[]{:S(2)}, u32[]{:S(2)}) collective-permute-start(bf16[256,256]{1,0:T(8,128)(2,1)} %get-tuple-element.20), channel_id=1, source_target_pairs={{0,1},{1,0},{2,3},{3,2},{4,5},{5,4},{6,7},{7,6},{8,9},{9,8},{10,11... | collective-permute-start | bytes 393224 | tf_op jit(solution)/shard_map/ppermute | solution.py:339
  32.5 8.3 %collective-permute-start.9 = (bf16[256,256]{1,0:T(8,128)(2,1)}, bf16[256,256]{1,0:T(8,128)(2,1)S(1)}, u32[]{:S(2)}, u32[]{:S(2)}) collective-permute-start(bf16[256,256]{1,0:T(8,128)(2,1)} %get-tuple-element.22), channel_id=1, source_target_pairs={{0,6},{1,7},{2,4},{3,5},{4,2},{5,3},{6,0},{7,1},{8,14},{9,15},{10,... | collective-permute-start | bytes 393224 | tf_op jit(solution)/shard_map/ppermute | solution.py:339
  36.8 10.3 %collective-permute-start.6 = (bf16[256,256]{1,0:T(8,128)(2,1)S(1)}, bf16[256,256]{1,0:T(8,128)(2,1)S(1)}, u32[]{:S(2)}, u32[]{:S(2)}) collective-permute-start(bf16[256,256]{1,0:T(8,128)(2,1)S(1)} %add_convert_fusion.3), channel_id=1, source_target_pairs={{0,4},{1,5},{2,6},{3,7},{4,0},{5,1},{6,2},{7,3},{8,12},{9,13},{10,... | collective-permute-start | bytes 393224 | tf_op jit(solution)/shard_map/ppermute | solution.py:339
  40.5 6.7 %collective-permute-start.8 = (bf16[256,256]{1,0:T(8,128)(2,1)S(1)}, bf16[256,256]{1,0:T(8,128)(2,1)S(1)}, u32[]{:S(2)}, u32[]{:S(2)}) collective-permute-start(bf16[256,256]{1,0:T(8,128)(2,1)S(1)} %add_convert_fusion.2), channel_id=1, source_target_pairs={{0,2},{1,3},{2,0},{3,1},{4,6},{5,7},{6,4},{7,5},{8,10},{9,11},{10,... | collective-permute-start | bytes 393224 | tf_op jit(solution)/shard_map/ppermute | solution.py:339
  41.8 5.3 %collective-permute-start.10 = (bf16[256,256]{1,0:T(8,128)(2,1)S(1)}, bf16[256,256]{1,0:T(8,128)(2,1)S(1)}, u32[]{:S(2)}, u32[]{:S(2)}) collective-permute-start(bf16[256,256]{1,0:T(8,128)(2,1)S(1)} %add_convert_fusion.1), channel_id=1, source_target_pairs={{0,1},{1,0},{2,3},{3,2},{4,5},{5,4},{6,7},{7,6},{8,9},{9,8},{10,11... | collective-permute-start | bytes 393224 | tf_op jit(solution)/shard_map/ppermute | solution.py:339
  48.3 29.3 %copy-start = (bf16[272,256]{1,0:T(8,128)(2,1)}, bf16[272,256]{1,0:T(8,128)(2,1)S(1)}, u32[]{:S(2)}) copy-start(bf16[272,256]{1,0:T(8,128)(2,1)S(1)} %maximum_maximum_fusion.rest_0_) | copy-start | bytes 417796
  48.3 7.3 %collective-permute-start.14 = (bf16[272,256]{1,0:T(8,128)(2,1)S(1)}, bf16[272,256]{1,0:T(8,128)(2,1)S(1)}, u32[]{:S(2)}, u32[]{:S(2)}) collective-permute-start(bf16[272,256]{1,0:T(8,128)(2,1)S(1)} %maximum_maximum_fusion.rest_0_), channel_id=1, source_target_pairs={{0,4},{1,5},{2,6},{3,7},{4,0},{5,1},{6,2},{7,3},{8,12},{9,13},{10,... | collective-permute-start | bytes 417800 | tf_op jit(solution)/shard_map/ppermute | solution.py:339
  49.2 12.1 %collective-permute-start.18 = (bf16[272,256]{1,0:T(8,128)(2,1)S(1)}, bf16[272,256]{1,0:T(8,128)(2,1)S(1)}, u32[]{:S(2)}, u32[]{:S(2)}) collective-permute-start(bf16[272,256]{1,0:T(8,128)(2,1)S(1)} %maximum_maximum_fusion.rest_0_), channel_id=1, source_target_pairs={{0,24},{8,0},{16,8},{24,16},{1,25},{9,1},{17,9},{25,17},{2,26},{10... | collective-permute-start | bytes 417800 | tf_op jit(solution)/shard_map/ppermute | solution.py:334
  54.2 9.0 %collective-permute-start.12 = (bf16[272,256]{1,0:T(8,128)(2,1)S(1)}, bf16[272,256]{1,0:T(8,128)(2,1)S(1)}, u32[]{:S(2)}, u32[]{:S(2)}) collective-permute-start(bf16[272,256]{1,0:T(8,128)(2,1)S(1)} %maximum_maximum_fusion.rest_0_), channel_id=1, source_target_pairs={{0,2},{1,3},{2,0},{3,1},{4,6},{5,7},{6,4},{7,5},{8,10},{9,11},{10,... | collective-permute-start | bytes 417800 | tf_op jit(solution)/shard_map/ppermute | solution.py:339
  54.2 9.4 %collective-permute-start.11 = (bf16[272,256]{1,0:T(8,128)(2,1)S(1)}, bf16[272,256]{1,0:T(8,128)(2,1)S(1)}, u32[]{:S(2)}, u32[]{:S(2)}) collective-permute-start(bf16[272,256]{1,0:T(8,128)(2,1)S(1)} %maximum_maximum_fusion.rest_0_), channel_id=1, source_target_pairs={{0,1},{1,0},{2,3},{3,2},{4,5},{5,4},{6,7},{7,6},{8,9},{9,8},{10,11... | collective-permute-start | bytes 417800 | tf_op jit(solution)/shard_map/ppermute | solution.py:339
  55.5 22.1 %copy-start.1 = (bf16[272,256]{1,0:T(8,128)(2,1)}, bf16[272,256]{1,0:T(8,128)(2,1)S(1)}, u32[]{:S(2)}) copy-start(bf16[272,256]{1,0:T(8,128)(2,1)S(1)} %collective-permute-done.14.rest_4_) | copy-start | bytes 417796
  55.5 8.0 %collective-permute-start.16 = (bf16[272,256]{1,0:T(8,128)(2,1)S(1)}, bf16[272,256]{1,0:T(8,128)(2,1)S(1)}, u32[]{:S(2)}, u32[]{:S(2)}) collective-permute-start(bf16[272,256]{1,0:T(8,128)(2,1)S(1)} %collective-permute-done.14.rest_4_), channel_id=1, source_target_pairs={{0,2},{1,3},{2,0},{3,1},{4,6},{5,7},{6,4},{7,5},{8,10},{9,11},{10,... | collective-permute-start | bytes 417800 | tf_op jit(solution)/shard_map/ppermute | solution.py:339
  56.7 8.3 %collective-permute-start.22 = (bf16[272,256]{1,0:T(8,128)(2,1)S(1)}, bf16[272,256]{1,0:T(8,128)(2,1)S(1)}, u32[]{:S(2)}, u32[]{:S(2)}) collective-permute-start(bf16[272,256]{1,0:T(8,128)(2,1)S(1)} %collective-permute-done.14.rest_4_), channel_id=1, source_target_pairs={{0,24},{8,0},{16,8},{24,16},{1,25},{9,1},{17,9},{25,17},{2,26},{10... | collective-permute-start | bytes 417800 | tf_op jit(solution)/shard_map/ppermute | solution.py:334
  61.3 16.4 %copy-start.2 = (bf16[272,256]{1,0:T(8,128)(2,1)}, bf16[272,256]{1,0:T(8,128)(2,1)S(1)}, u32[]{:S(2)}) copy-start(bf16[272,256]{1,0:T(8,128)(2,1)S(1)} %collective-permute-done.18.rest_8_) | copy-start | bytes 417796
  61.3 5.9 %collective-permute-start.15 = (bf16[272,256]{1,0:T(8,128)(2,1)S(1)}, bf16[272,256]{1,0:T(8,128)(2,1)S(1)}, u32[]{:S(2)}, u32[]{:S(2)}) collective-permute-start(bf16[272,256]{1,0:T(8,128)(2,1)S(1)} %collective-permute-done.14.rest_4_), channel_id=1, source_target_pairs={{0,1},{1,0},{2,3},{3,2},{4,5},{5,4},{6,7},{7,6},{8,9},{9,8},{10,11... | collective-permute-start | bytes 417800 | tf_op jit(solution)/shard_map/ppermute | solution.py:339
  63.2 14.4 %copy-start.3 = (bf16[272,256]{1,0:T(8,128)(2,1)}, bf16[272,256]{1,0:T(8,128)(2,1)S(1)}, u32[]{:S(2)}) copy-start(bf16[272,256]{1,0:T(8,128)(2,1)S(1)} %collective-permute-done.12.rest_2_) | copy-start | bytes 417796
  63.2 4.9 %collective-permute-start.20 = (bf16[272,256]{1,0:T(8,128)(2,1)S(1)}, bf16[272,256]{1,0:T(8,128)(2,1)S(1)}, u32[]{:S(2)}, u32[]{:S(2)}) collective-permute-start(bf16[272,256]{1,0:T(8,128)(2,1)S(1)} %collective-permute-done.12.rest_2_), channel_id=1, source_target_pairs={{0,24},{8,0},{16,8},{24,16},{1,25},{9,1},{17,9},{25,17},{2,26},{10... | collective-permute-start | bytes 417800 | tf_op jit(solution)/shard_map/ppermute | solution.py:334
  63.5 14.1 %copy-start.4 = (bf16[272,256]{1,0:T(8,128)(2,1)}, bf16[272,256]{1,0:T(8,128)(2,1)S(1)}, u32[]{:S(2)}) copy-start(bf16[272,256]{1,0:T(8,128)(2,1)S(1)} %collective-permute-done.11.rest_1_) | copy-start | bytes 417796
  63.5 6.6 %collective-permute-start.13 = (bf16[272,256]{1,0:T(8,128)(2,1)S(1)}, bf16[272,256]{1,0:T(8,128)(2,1)S(1)}, u32[]{:S(2)}, u32[]{:S(2)}) collective-permute-start(bf16[272,256]{1,0:T(8,128)(2,1)S(1)} %collective-permute-done.12.rest_2_), channel_id=1, source_target_pairs={{0,1},{1,0},{2,3},{3,2},{4,5},{5,4},{6,7},{7,6},{8,9},{9,8},{10,11... | collective-permute-start | bytes 417800 | tf_op jit(solution)/shard_map/ppermute | solution.py:339
  63.6 14.1 %copy-start.5 = (bf16[272,256]{1,0:T(8,128)(2,1)}, bf16[272,256]{1,0:T(8,128)(2,1)S(1)}, u32[]{:S(2)}) copy-start(bf16[272,256]{1,0:T(8,128)(2,1)S(1)} %collective-permute-done.16.rest_6_) | copy-start | bytes 417796
  63.6 9.6 %collective-permute-start.17 = (bf16[272,256]{1,0:T(8,128)(2,1)S(1)}, bf16[272,256]{1,0:T(8,128)(2,1)S(1)}, u32[]{:S(2)}, u32[]{:S(2)}) collective-permute-start(bf16[272,256]{1,0:T(8,128)(2,1)S(1)} %collective-permute-done.16.rest_6_), channel_id=1, source_target_pairs={{0,1},{1,0},{2,3},{3,2},{4,5},{5,4},{6,7},{7,6},{8,9},{9,8},{10,11... | collective-permute-start | bytes 417800 | tf_op jit(solution)/shard_map/ppermute | solution.py:339
  65.0 12.6 %copy-start.6 = (bf16[272,256]{1,0:T(8,128)(2,1)}, bf16[272,256]{1,0:T(8,128)(2,1)S(1)}, u32[]{:S(2)}) copy-start(bf16[272,256]{1,0:T(8,128)(2,1)S(1)} %collective-permute-done.22.rest_12_) | copy-start | bytes 417796
  65.0 8.7 %collective-permute-start.19 = (bf16[272,256]{1,0:T(8,128)(2,1)S(1)}, bf16[272,256]{1,0:T(8,128)(2,1)S(1)}, u32[]{:S(2)}, u32[]{:S(2)}) collective-permute-start(bf16[272,256]{1,0:T(8,128)(2,1)S(1)} %collective-permute-done.11.rest_1_), channel_id=1, source_target_pairs={{0,24},{8,0},{16,8},{24,16},{1,25},{9,1},{17,9},{25,17},{2,26},{10... | collective-permute-start | bytes 417800 | tf_op jit(solution)/shard_map/ppermute | solution.py:334
  67.1 10.5 %copy-start.7 = (bf16[272,256]{1,0:T(8,128)(2,1)}, bf16[272,256]{1,0:T(8,128)(2,1)S(1)}, u32[]{:S(2)}) copy-start(bf16[272,256]{1,0:T(8,128)(2,1)S(1)} %collective-permute-done.15.rest_5_) | copy-start | bytes 417796
  67.2 6.6 %collective-permute-start.24 = (bf16[272,256]{1,0:T(8,128)(2,1)S(1)}, bf16[272,256]{1,0:T(8,128)(2,1)S(1)}, u32[]{:S(2)}, u32[]{:S(2)}) collective-permute-start(bf16[272,256]{1,0:T(8,128)(2,1)S(1)} %collective-permute-done.16.rest_6_), channel_id=1, source_target_pairs={{0,24},{8,0},{16,8},{24,16},{1,25},{9,1},{17,9},{25,17},{2,26},{10... | collective-permute-start | bytes 417800 | tf_op jit(solution)/shard_map/ppermute | solution.py:334
  68.1 9.6 %copy-start.8 = (bf16[272,256]{1,0:T(8,128)(2,1)}, bf16[272,256]{1,0:T(8,128)(2,1)S(1)}, u32[]{:S(2)}) copy-start(bf16[272,256]{1,0:T(8,128)(2,1)S(1)} %collective-permute-done.20.rest_10_) | copy-start | bytes 417796
  68.1 5.7 %collective-permute-start.23 = (bf16[272,256]{1,0:T(8,128)(2,1)S(1)}, bf16[272,256]{1,0:T(8,128)(2,1)S(1)}, u32[]{:S(2)}, u32[]{:S(2)}) collective-permute-start(bf16[272,256]{1,0:T(8,128)(2,1)S(1)} %collective-permute-done.15.rest_5_), channel_id=1, source_target_pairs={{0,24},{8,0},{16,8},{24,16},{1,25},{9,1},{17,9},{25,17},{2,26},{10... | collective-permute-start | bytes 417800 | tf_op jit(solution)/shard_map/ppermute | solution.py:334
  70.1 7.5 %copy-start.9 = (bf16[272,256]{1,0:T(8,128)(2,1)}, bf16[272,256]{1,0:T(8,128)(2,1)S(1)}, u32[]{:S(2)}) copy-start(bf16[272,256]{1,0:T(8,128)(2,1)S(1)} %collective-permute-done.13.rest_3_) | copy-start | bytes 417796
  70.1 4.5 %collective-permute-start.21 = (bf16[272,256]{1,0:T(8,128)(2,1)S(1)}, bf16[272,256]{1,0:T(8,128)(2,1)S(1)}, u32[]{:S(2)}, u32[]{:S(2)}) collective-permute-start(bf16[272,256]{1,0:T(8,128)(2,1)S(1)} %collective-permute-done.13.rest_3_), channel_id=1, source_target_pairs={{0,24},{8,0},{16,8},{24,16},{1,25},{9,1},{17,9},{25,17},{2,26},{10... | collective-permute-start | bytes 417800 | tf_op jit(solution)/shard_map/ppermute | solution.py:334
  73.1 4.6 %copy-start.10 = (bf16[272,256]{1,0:T(8,128)(2,1)}, bf16[272,256]{1,0:T(8,128)(2,1)S(1)}, u32[]{:S(2)}) copy-start(bf16[272,256]{1,0:T(8,128)(2,1)S(1)} %collective-permute-done.17.rest_7_) | copy-start | bytes 417796
  73.1 4.5 %collective-permute-start.25 = (bf16[272,256]{1,0:T(8,128)(2,1)S(1)}, bf16[272,256]{1,0:T(8,128)(2,1)S(1)}, u32[]{:S(2)}, u32[]{:S(2)}) collective-permute-start(bf16[272,256]{1,0:T(8,128)(2,1)S(1)} %collective-permute-done.17.rest_7_), channel_id=1, source_target_pairs={{0,24},{8,0},{16,8},{24,16},{1,25},{9,1},{17,9},{25,17},{2,26},{10... | collective-permute-start | bytes 417800 | tf_op jit(solution)/shard_map/ppermute | solution.py:334
  73.8 3.9 %copy-start.11 = (bf16[272,256]{1,0:T(8,128)(2,1)}, bf16[272,256]{1,0:T(8,128)(2,1)S(1)}, u32[]{:S(2)}) copy-start(bf16[272,256]{1,0:T(8,128)(2,1)S(1)} %collective-permute-done.19.rest_9_) | copy-start | bytes 417796
  73.8 3.9 %copy-start.12 = (bf16[272,256]{1,0:T(8,128)(2,1)}, bf16[272,256]{1,0:T(8,128)(2,1)S(1)}, u32[]{:S(2)}) copy-start(bf16[272,256]{1,0:T(8,128)(2,1)S(1)} %collective-permute-done.24.rest_14_) | copy-start | bytes 417796
  73.8 3.9 %copy-start.13 = (bf16[272,256]{1,0:T(8,128)(2,1)}, bf16[272,256]{1,0:T(8,128)(2,1)S(1)}, u32[]{:S(2)}) copy-start(bf16[272,256]{1,0:T(8,128)(2,1)S(1)} %collective-permute-done.23.rest_13_) | copy-start | bytes 417796
  74.6 3.1 %copy-start.14 = (bf16[272,256]{1,0:T(8,128)(2,1)}, bf16[272,256]{1,0:T(8,128)(2,1)S(1)}, u32[]{:S(2)}) copy-start(bf16[272,256]{1,0:T(8,128)(2,1)S(1)} %collective-permute-done.21.rest_11_) | copy-start | bytes 417796
  77.6 0.7 copy-start.15

commit v5 on v4

--- a/solution.py
+++ b/solution.py
@@ -450,9 +450,14 @@
     for step in range(1, far):
         own[step * inner] = swapped(coarse_in, "gy", step * inner)
         own[(far + step) * inner] = swapped(own[far * inner], "gy", step * inner)
-    for far in range(outer):
+    for near in range(1, inner):
+        own[near] = swapped(coarse_in, "gy", near)
+    for far in range(1, outer):
         for near in range(1, inner):
-            own[far * inner + near] = swapped(own[far * inner], "gy", near)
+            if far > outer // 2:
+                own[far * inner + near] = swapped(own[near], "gy", far * inner)
+            else:
+                own[far * inner + near] = swapped(own[far * inner], "gy", near)
     following = [turned(value, "gx", -1) for value in own]
 
     return pl.pallas_call(

time: 90.8 us -> 88.7 us (0.977)
  waiting for transfers between devices: 16.5 us -> 15.3 us
    ppermute x12, starting transfers between devices: 22 us -> 19.9 us  [turned(): lax.ppermute(value, axis, [(i, (i + step) % count) for i in range(count)])]
    ppermute x14, waiting for transfers between devices: 9.74 us -> 8.26 us  [swapped(): return lax.ppermute(value, axis, [(i, i ^ distance) for i in range(count)])]
    ppermute x14, starting transfers between devices: 16.2 us -> 17.3 us  [swapped(): return lax.ppermute(value, axis, [(i, i ^ distance) for i in range(count)])]
  transfers between devices with their start and end apart: 26 -> 26, of which waited for: 9 -> 11; matrix products, arithmetic and copies ran while one was open for 4% -> 4% of each run, Pallas kernels for 0% -> 0%
where the time goes in v5:
time: 88.7 us; the launch traced here: 88.4 us
  starting transfers between devices  37.3 us (42%)
  Pallas kernels  28.2 us (32%)
  waiting for transfers between devices  15.3 us (17%)
  other arithmetic  4.03 us (5%)
  local copies, waits for them, and re-layouts  3.34 us (4%)
    ppermute x12, starting transfers between devices, turned(): lax.ppermute(value, axis, [(i, (i + step) % count) for i in range(count)])  19.9 us
    ppermute x14, starting transfers between devices, swapped(): return lax.ppermute(value, axis, [(i, i ^ distance) for i in range(count)])  17.3 us
    pallas_call x1, Pallas kernels, per_device(): pl.pallas_call(functools.partial(fine_kernel, hosts, chunk), out_shape=[j...  16 us
    pallas_call x1, Pallas kernels, per_device(): pl.pallas_call(functools.partial(coarse_kernel, hosts, degree), out_shape...  12.2 us
    ppermute x14, waiting for transfers between devices, swapped(): return lax.ppermute(value, axis, [(i, i ^ distance) for i in range(count)])  8.26 us
    ppermute x12, waiting for transfers between devices, turned(): lax.ppermute(value, axis, [(i, (i + step) % count) for i in range(count)])  7.02 us
    convert_element_type x3, other arithmetic, per_device(): parts[number].astype(BF16)  2.84 us
  transfers between devices with their start and end apart: 26, of which 11 were waited for; matrix products, arithmetic and copies ran while one was open for 4% of the time, Pallas kernels for 0%

profile of v5, /device:TPU:1, one launch (start us, length us, event | category | flops | bytes accessed | tf_op | source)
XLA Modules:
  0.0 88.4 jit_solution(12026137638413208700)
XLA Ops:
  0.0 1.0 %fusion.5 = (bf16[32,1,256]{2,1,0:T(2,128)(2,1)S(1)}, bf16[32,1,256]{2,1,0:T(2,128)(2,1)S(1)}) fusion(bf16[32,128,256]{2,1,0:T(8,128)(2,1)} %latent_ref.1), kind=kLoop, calls=%fused_computation.23 | loop fusion | bytes 65536 | tf_op jit(solution)/shard_map/slice | solution.py:374
  1.0 2.1 %collective-permute-start = (bf16[32,256]{1,0:T(8,128)(2,1)S(1)}, bf16[32,256]{1,0:T(8,128)(2,1)S(1)}, u32[]{:S(2)}, u32[]{:S(2)}) collective-permute-start(bf16[32,256]{1,0:T(8,128)(2,1)S(1)} %bitcast.45), channel_id=1, source_target_pairs={{0,1},{1,2},{2,3},{3,4},{4,5},{5,6},{6,7},{7,0},{8,9},{9,10},{10,1... | collective-permute-start | bytes 49160 | tf_op jit(solution)/shard_map/ppermute | solution.py:334
  3.2 3.1 %collective-permute-start.1 = (bf16[32,256]{1,0:T(8,128)(2,1)S(1)}, bf16[32,256]{1,0:T(8,128)(2,1)S(1)}, u32[]{:S(2)}, u32[]{:S(2)}) collective-permute-start(bf16[32,256]{1,0:T(8,128)(2,1)S(1)} %bitcast.46), channel_id=1, source_target_pairs={{0,7},{1,0},{2,1},{3,2},{4,3},{5,4},{6,5},{7,6},{8,15},{9,8},{10,9... | collective-permute-start | bytes 49160 | tf_op jit(solution)/shard_map/ppermute | solution.py:334
  6.3 0.9 slice_bitcast_fusion
  7.2 0.1 pad.11.clone
  7.3 0.1 collective-permute-done.low_hbm
  7.4 0.0 collective-permute-done.1.high_hbm
  7.4 0.1 maximum_maximum_fusion.2
  7.5 1.6 %collective-permute-start.3 = (bf16[144,256]{1,0:T(8,128)(2,1)S(1)}, bf16[144,256]{1,0:T(8,128)(2,1)S(1)}, u32[]{:S(2)}, u32[]{:S(2)}) collective-permute-start(bf16[144,256]{1,0:T(8,128)(2,1)S(1)} %get-tuple-element.33), channel_id=1, source_target_pairs={{0,24},{8,0},{16,8},{24,16},{1,25},{9,1},{17,9},{25,17},{2,26},{10... | collective-permute-start | bytes 221192 | tf_op jit(solution)/shard_map/ppermute | solution.py:334
  9.1 1.3 %collective-permute-start.2 = (bf16[144,256]{1,0:T(8,128)(2,1)S(1)}, bf16[144,256]{1,0:T(8,128)(2,1)S(1)}, u32[]{:S(2)}, u32[]{:S(2)}) collective-permute-start(bf16[144,256]{1,0:T(8,128)(2,1)S(1)} %get-tuple-element.34), channel_id=1, source_target_pairs={{0,8},{8,16},{16,24},{24,0},{1,9},{9,17},{17,25},{25,1},{2,10},{10... | collective-permute-start | bytes 221192 | tf_op jit(solution)/shard_map/ppermute | solution.py:334
  10.4 2.8 %collective-permute-done.3.below_hbm = bf16[144,256]{1,0:T(8,128)(2,1)S(1)} collective-permute-done((bf16[144,256]{1,0:T(8,128)(2,1)S(1)}, bf16[144,256]{1,0:T(8,128)(2,1)S(1)}, u32[]{:S(2)}, u32[]{:S(2)}) %collective-permute-start.3) | collective-permute-done | bytes 73760 | tf_op jit(solution)/shard_map/ppermute | solution.py:334
  13.2 0.0 collective-permute-done.2.above_hbm
  13.2 0.6 copy-done.16
  13.8 0.0 copy-done.17
  13.8 16.0 %fine_cells.1 = (bf16[32,128,256]{2,1,0:T(8,128)(2,1)}, bf16[256,256]{1,0:T(8,128)(2,1)}, bf16[256,256]{1,0:T(8,128)(2,1)}, bf16[256,256]{1,0:T(8,128)(2,1)}, bf...) custom-call(s32[32]{0:T(128)} %bitcast.47, ...), custom_call_target="tpu_custom_call" | custom-call | tf_op jit(solution)/shard_map/fine_cells/pallas_call | solution.py:384
  29.9 0.4 collective-permute-start.4
  30.3 2.1 %collective-permute-start.5 = (bf16[256,256]{1,0:T(8,128)(2,1)}, bf16[256,256]{1,0:T(8,128)(2,1)S(1)}, u32[]{:S(2)}, u32[]{:S(2)}) collective-permute-start(bf16[256,256]{1,0:T(8,128)(2,1)} %get-tuple-element.18), channel_id=1, source_target_pairs={{0,1},{1,0},{2,3},{3,2},{4,5},{5,4},{6,7},{7,6},{8,9},{9,8},{10,11... | collective-permute-start | bytes 393224 | tf_op jit(solution)/shard_map/ppermute | solution.py:339
  32.4 0.1 pad.3.clone
  32.5 0.0 collective-permute-start.7
  32.5 2.5 %collective-permute-start.9 = (bf16[256,256]{1,0:T(8,128)(2,1)}, bf16[256,256]{1,0:T(8,128)(2,1)S(1)}, u32[]{:S(2)}, u32[]{:S(2)}) collective-permute-start(bf16[256,256]{1,0:T(8,128)(2,1)} %get-tuple-element.22), channel_id=1, source_target_pairs={{0,6},{1,7},{2,4},{3,5},{4,2},{5,3},{6,0},{7,1},{8,14},{9,15},{10,... | collective-permute-start | bytes 393224 | tf_op jit(solution)/shard_map/ppermute | solution.py:339
  35.0 0.0 collective-permute-done.4
  35.0 0.9 collective-permute-done.5
  35.9 1.0 %add_convert_fusion.3 = bf16[256,256]{1,0:T(8,128)(2,1)S(1)} fusion(bf16[256,256]{1,0:T(8,128)(2,1)S(1)} %collective-permute-done.5, bf16[256,256]{1,0:T(8,128)(2,1)S(1)} %collective-permute-done.4, bf16[256,256]{1,0:T(8,128)(2,1)} %get-tuple-element.16), kind=kLoop, calls=%fused_computation.3 | loop fusion | flops 393216 | bytes 524288 | tf_op jit(solution)/shard_map/convert_element_type | solution.py:438
  36.8 2.7 %collective-permute-start.6 = (bf16[256,256]{1,0:T(8,128)(2,1)S(1)}, bf16[256,256]{1,0:T(8,128)(2,1)S(1)}, u32[]{:S(2)}, u32[]{:S(2)}) collective-permute-start(bf16[256,256]{1,0:T(8,128)(2,1)S(1)} %add_convert_fusion.3), channel_id=1, source_target_pairs={{0,4},{1,5},{2,6},{3,7},{4,0},{5,1},{6,2},{7,3},{8,12},{9,13},{10,... | collective-permute-start | bytes 393224 | tf_op jit(solution)/shard_map/ppermute | solution.py:339
  39.5 0.0 collective-permute-done.7
  39.5 0.9 %add_convert_fusion.2 = bf16[256,256]{1,0:T(8,128)(2,1)S(1)} fusion(bf16[256,256]{1,0:T(8,128)(2,1)S(1)} %collective-permute-done.7, bf16[256,256]{1,0:T(8,128)(2,1)} %get-tuple-element.19), kind=kLoop, calls=%fused_computation.2 | loop fusion | flops 262144 | bytes 393216 | tf_op jit(solution)/shard_map/convert_element_type | solution.py:438
  40.5 0.4 collective-permute-start.8
  40.9 0.0 collective-permute-done.9
  40.9 0.9 %add_convert_fusion.1 = bf16[256,256]{1,0:T(8,128)(2,1)S(1)} fusion(bf16[256,256]{1,0:T(8,128)(2,1)S(1)} %collective-permute-done.9, bf16[256,256]{1,0:T(8,128)(2,1)} %get-tuple-element.21), kind=kLoop, calls=%fused_computation.1 | loop fusion | flops 262144 | bytes 393216 | tf_op jit(solution)/shard_map/convert_element_type | solution.py:438
  41.8 1.2 %collective-permute-start.10 = (bf16[256,256]{1,0:T(8,128)(2,1)S(1)}, bf16[256,256]{1,0:T(8,128)(2,1)S(1)}, u32[]{:S(2)}, u32[]{:S(2)}) collective-permute-start(bf16[256,256]{1,0:T(8,128)(2,1)S(1)} %add_convert_fusion.1), channel_id=1, source_target_pairs={{0,1},{1,0},{2,3},{3,2},{4,5},{5,4},{6,7},{7,6},{8,9},{9,8},{10,11... | collective-permute-start | bytes 393224 | tf_op jit(solution)/shard_map/ppermute | solution.py:339
  43.1 4.1 %collective-permute-done.6 = bf16[256,256]{1,0:T(8,128)(2,1)S(1)} collective-permute-done((bf16[256,256]{1,0:T(8,128)(2,1)S(1)}, bf16[256,256]{1,0:T(8,128)(2,1)S(1)}, u32[]{:S(2)}, u32[]{:S(2)}) %collective-permute-start.6) | collective-permute-done | bytes 131104 | tf_op jit(solution)/shard_map/ppermute | solution.py:339
  47.2 0.0 collective-permute-done.8
  47.2 0.0 collective-permute-done.10
  47.2 1.0 %add_convert_fusion = bf16[256,256]{1,0:T(8,128)(2,1)S(1)} fusion(bf16[256,256]{1,0:T(8,128)(2,1)S(1)} %collective-permute-done.10, bf16[256,256]{1,0:T(8,128)(2,1)S(1)} %collective-permute-done.8, bf16[256,256]{1,0:T(8,128)(2,1)S(1)} %collective-permute-done.6, bf16[256,256]{1,0:T(8,128)(2,1)} %get-tuple-element.15), kind=kLoop, calls=%fused_computation | loop fusion | flops 524288 | bytes 655360 | tf_op jit(solution)/shard_map/convert_element_type | solution.py:444
  48.2 0.1 maximum_maximum_fusion.rest_0_
  48.3 0.9 %collective-permute-start.14 = (bf16[272,256]{1,0:T(8,128)(2,1)S(1)}, bf16[272,256]{1,0:T(8,128)(2,1)S(1)}, u32[]{:S(2)}, u32[]{:S(2)}) collective-permute-start(bf16[272,256]{1,0:T(8,128)(2,1)S(1)} %maximum_maximum_fusion.rest_0_), channel_id=1, source_target_pairs={{0,4},{1,5},{2,6},{3,7},{4,0},{5,1},{6,2},{7,3},{8,12},{9,13},{10,... | collective-permute-start | bytes 417800 | tf_op jit(solution)/shard_map/ppermute | solution.py:339
  49.2 5.0 %collective-permute-start.18 = (bf16[272,256]{1,0:T(8,128)(2,1)S(1)}, bf16[272,256]{1,0:T(8,128)(2,1)S(1)}, u32[]{:S(2)}, u32[]{:S(2)}) collective-permute-start(bf16[272,256]{1,0:T(8,128)(2,1)S(1)} %maximum_maximum_fusion.rest_0_), channel_id=1, source_target_pairs={{0,24},{8,0},{16,8},{24,16},{1,25},{9,1},{17,9},{25,17},{2,26},{10... | collective-permute-start | bytes 417800 | tf_op jit(solution)/shard_map/ppermute | solution.py:334
  54.2 0.0 collective-permute-start.12
  54.2 1.4 %collective-permute-start.11 = (bf16[272,256]{1,0:T(8,128)(2,1)S(1)}, bf16[272,256]{1,0:T(8,128)(2,1)S(1)}, u32[]{:S(2)}, u32[]{:S(2)}) collective-permute-start(bf16[272,256]{1,0:T(8,128)(2,1)S(1)} %maximum_maximum_fusion.rest_0_), channel_id=1, source_target_pairs={{0,1},{1,0},{2,3},{3,2},{4,5},{5,4},{6,7},{7,6},{8,9},{9,8},{10,11... | collective-permute-start | bytes 417800 | tf_op jit(solution)/shard_map/ppermute | solution.py:339
  55.5 0.0 collective-permute-done.14.rest_4_
  55.5 2.5 %collective-permute-start.22 = (bf16[272,256]{1,0:T(8,128)(2,1)S(1)}, bf16[272,256]{1,0:T(8,128)(2,1)S(1)}, u32[]{:S(2)}, u32[]{:S(2)}) collective-permute-start(bf16[272,256]{1,0:T(8,128)(2,1)S(1)} %collective-permute-done.14.rest_4_), channel_id=1, source_target_pairs={{0,24},{8,0},{16,8},{24,16},{1,25},{9,1},{17,9},{25,17},{2,26},{10... | collective-permute-start | bytes 417800 | tf_op jit(solution)/shard_map/ppermute | solution.py:334
  58.1 2.9 %collective-permute-start.16 = (bf16[272,256]{1,0:T(8,128)(2,1)S(1)}, bf16[272,256]{1,0:T(8,128)(2,1)S(1)}, u32[]{:S(2)}, u32[]{:S(2)}) collective-permute-start(bf16[272,256]{1,0:T(8,128)(2,1)S(1)} %collective-permute-done.14.rest_4_), channel_id=1, source_target_pairs={{0,2},{1,3},{2,0},{3,1},{4,6},{5,7},{6,4},{7,5},{8,10},{9,11},{10,... | collective-permute-start | bytes 417800 | tf_op jit(solution)/shard_map/ppermute | solution.py:339
  61.0 1.7 %collective-permute-start.15 = (bf16[272,256]{1,0:T(8,128)(2,1)S(1)}, bf16[272,256]{1,0:T(8,128)(2,1)S(1)}, u32[]{:S(2)}, u32[]{:S(2)}) collective-permute-start(bf16[272,256]{1,0:T(8,128)(2,1)S(1)} %collective-permute-done.14.rest_4_), channel_id=1, source_target_pairs={{0,1},{1,0},{2,3},{3,2},{4,5},{5,4},{6,7},{7,6},{8,9},{9,8},{10,11... | collective-permute-start | bytes 417800 | tf_op jit(solution)/shard_map/ppermute | solution.py:339
  62.7 0.6 collective-permute-start.20
  63.3 0.0 collective-permute-done.11.rest_1_
  63.3 0.0 collective-permute-start.13
  63.3 0.0 collective-permute-done.22.rest_12_
  63.3 1.1 %collective-permute-start.17 = (bf16[272,256]{1,0:T(8,128)(2,1)S(1)}, bf16[272,256]{1,0:T(8,128)(2,1)S(1)}, u32[]{:S(2)}, u32[]{:S(2)}) collective-permute-start(bf16[272,256]{1,0:T(8,128)(2,1)S(1)} %collective-permute-done.11.rest_1_), channel_id=1, source_target_pairs={{0,6},{1,7},{2,4},{3,5},{4,2},{5,3},{6,0},{7,1},{8,14},{9,15},{10,... | collective-permute-start | bytes 417800 | tf_op jit(solution)/shard_map/ppermute | solution.py:339
  64.4 0.6 collective-permute-done.16.rest_6_
  65.0 0.8 collective-permute-start.19
  65.8 0.8 collective-permute-done.15.rest_5_
  66.6 1.2 %collective-permute-start.24 = (bf16[272,256]{1,0:T(8,128)(2,1)S(1)}, bf16[272,256]{1,0:T(8,128)(2,1)S(1)}, u32[]{:S(2)}, u32[]{:S(2)}) collective-permute-start(bf16[272,256]{1,0:T(8,128)(2,1)S(1)} %collective-permute-done.16.rest_6_), channel_id=1, source_target_pairs={{0,24},{8,0},{16,8},{24,16},{1,25},{9,1},{17,9},{25,17},{2,26},{10... | collective-permute-start | bytes 417800 | tf_op jit(solution)/shard_map/ppermute | solution.py:334
  67.7 0.1 collective-permute-start.23
  67.8 1.7 %collective-permute-done.13.rest_3_ = bf16[272,256]{1,0:T(8,128)(2,1)S(1)} collective-permute-done((bf16[272,256]{1,0:T(8,128)(2,1)S(1)}, bf16[272,256]{1,0:T(8,128)(2,1)S(1)}, u32[]{:S(2)}, u32[]{:S(2)}) %collective-permute-start.13) | collective-permute-done | bytes 139296 | tf_op jit(solution)/shard_map/ppermute | solution.py:339
  69.5 0.8 collective-permute-start.21
  70.3 0.1 collective-permute-done.17.rest_7_
  70.5 0.9 %collective-permute-start.25 = (bf16[272,256]{1,0:T(8,128)(2,1)S(1)}, bf16[272,256]{1,0:T(8,128)(2,1)S(1)}, u32[]{:S(2)}, u32[]{:S(2)}) collective-permute-start(bf16[272,256]{1,0:T(8,128)(2,1)S(1)} %collective-permute-done.17.rest_7_), channel_id=1, source_target_pairs={{0,24},{8,0},{16,8},{24,16},{1,25},{9,1},{17,9},{25,17},{2,26},{10... | collective-permute-start | bytes 417800 | tf_op jit(solution)/shard_map/ppermute | solution.py:334
  71.4 0.0 collective-permute-done.19.rest_9_
  71.4 0.0 collective-permute-done.24.rest_14_
  71.4 1.1 %collective-permute-done.23.rest_13_ = bf16[272,256]{1,0:T(8,128)(2,1)S(1)} collective-permute-done((bf16[272,256]{1,0:T(8,128)(2,1)S(1)}, bf16[272,256]{1,0:T(8,128)(2,1)S(1)}, u32[]{:S(2)}, u32[]{:S(2)}) %collective-permute-start.23) | collective-permute-done | bytes 139296 | tf_op jit(solution)/shard_map/ppermute | solution.py:334
  72.5 1.5 %collective-permute-done.21.rest_11_ = bf16[272,256]{1,0:T(8,128)(2,1)S(1)} collective-permute-done((bf16[272,256]{1,0:T(8,128)(2,1)S(1)}, bf16[272,256]{1,0:T(8,128)(2,1)S(1)}, u32[]{:S(2)}, u32[]{:S(2)}) %collective-permute-start.21) | collective-permute-done | bytes 139296 | tf_op jit(solution)/shard_map/ppermute | solution.py:334
  74.0 1.5 %collective-permute-done.25.rest_15_ = bf16[272,256]{1,0:T(8,128)(2,1)S(1)} collective-permute-done((bf16[272,256]{1,0:T(8,128)(2,1)S(1)}, bf16[272,256]{1,0:T(8,128)(2,1)S(1)}, u32[]{:S(2)}, u32[]{:S(2)}) %collective-permute-start.25) | collective-permute-done | bytes 139296 | tf_op jit(solution)/shard_map/ppermute | solution.py:334
  75.7 0.5 copy-done.15
  76.2 12.2 %coarse_rows.1 = bf16[32,128,256]{2,1,0:T(8,128)(2,1)} custom-call(s32[32]{0:T(128)} %bitcast.48, s32[32]{0:T(128)} %bitcast.50, bf16[32,128,256]{2,1,0:T(8,128)(2,1)} %get-tuple-element.14.refined_ref, bf16[32,32,128]{2,1,0:T(8,128)(2,1)} %bitcast.42, bf16[256,256]{1,0:T(8,128)(2,1)} %as_ref.1, bf16[256,256]{1,0:T(8,128)(2,1)} %ad_ref.1, ...), custom_call_target="tpu_custom_call" | custom-call | tf_op jit(solution)/shard_map/coarse_rows/pallas_call | solution.py:463
  (49 shorter events, 0.1 us)
Async XLA Ops:
  1.0 6.3 %collective-permute-start = (bf16[32,256]{1,0:T(8,128)(2,1)S(1)}, bf16[32,256]{1,0:T(8,128)(2,1)S(1)}, u32[]{:S(2)}, u32[]{:S(2)}) collective-permute-start(bf16[32,256]{1,0:T(8,128)(2,1)S(1)} %bitcast.45), channel_id=1, source_target_pairs={{0,1},{1,2},{2,3},{3,4},{4,5},{5,6},{6,7},{7,0},{8,9},{9,10},{10,1... | collective-permute-start | bytes 49160 | tf_op jit(solution)/shard_map/ppermute | solution.py:334
  3.2 4.2 %collective-permute-start.1 = (bf16[32,256]{1,0:T(8,128)(2,1)S(1)}, bf16[32,256]{1,0:T(8,128)(2,1)S(1)}, u32[]{:S(2)}, u32[]{:S(2)}) collective-permute-start(bf16[32,256]{1,0:T(8,128)(2,1)S(1)} %bitcast.46), channel_id=1, source_target_pairs={{0,7},{1,0},{2,1},{3,2},{4,3},{5,4},{6,5},{7,6},{8,15},{9,8},{10,9... | collective-permute-start | bytes 49160 | tf_op jit(solution)/shard_map/ppermute | solution.py:334
  7.3 5.9 %copy-start.18 = (bf16[32,256]{1,0:T(8,128)(2,1)}, bf16[32,256]{1,0:T(8,128)(2,1)S(1)}, u32[]{:S(2)}) copy-start(bf16[32,256]{1,0:T(8,128)(2,1)S(1)} %collective-permute-done.low_hbm) | copy-start | bytes 49156
  7.4 5.8 %copy-start.19 = (bf16[32,256]{1,0:T(8,128)(2,1)}, bf16[32,256]{1,0:T(8,128)(2,1)S(1)}, u32[]{:S(2)}) copy-start(bf16[32,256]{1,0:T(8,128)(2,1)S(1)} %collective-permute-done.1.high_hbm) | copy-start | bytes 49156
  7.5 5.7 %collective-permute-start.3 = (bf16[144,256]{1,0:T(8,128)(2,1)S(1)}, bf16[144,256]{1,0:T(8,128)(2,1)S(1)}, u32[]{:S(2)}, u32[]{:S(2)}) collective-permute-start(bf16[144,256]{1,0:T(8,128)(2,1)S(1)} %get-tuple-element.33), channel_id=1, source_target_pairs={{0,24},{8,0},{16,8},{24,16},{1,25},{9,1},{17,9},{25,17},{2,26},{10... | collective-permute-start | bytes 221192 | tf_op jit(solution)/shard_map/ppermute | solution.py:334
  9.1 4.1 %collective-permute-start.2 = (bf16[144,256]{1,0:T(8,128)(2,1)S(1)}, bf16[144,256]{1,0:T(8,128)(2,1)S(1)}, u32[]{:S(2)}, u32[]{:S(2)}) collective-permute-start(bf16[144,256]{1,0:T(8,128)(2,1)S(1)} %get-tuple-element.34), channel_id=1, source_target_pairs={{0,8},{8,16},{16,24},{24,0},{1,9},{9,17},{17,25},{25,1},{2,10},{10... | collective-permute-start | bytes 221192 | tf_op jit(solution)/shard_map/ppermute | solution.py:334
  13.2 0.6 copy-start.16
  13.2 0.7 copy-start.17
  13.8 29.2 %copy-start.20 = (s32[256,6]{0,1:T(8,128)S(1)}, s32[256,6]{0,1:T(8,128)}, u32[]{:S(2)}) copy-start(s32[256,6]{0,1:T(8,128)} %param.30) | copy-start | bytes 18436
  29.9 5.1 %collective-permute-start.4 = (bf16[256,256]{1,0:T(8,128)(2,1)}, bf16[256,256]{1,0:T(8,128)(2,1)S(1)}, u32[]{:S(2)}, u32[]{:S(2)}) collective-permute-start(bf16[256,256]{1,0:T(8,128)(2,1)} %get-tuple-element.17), channel_id=1, source_target_pairs={{0,2},{1,3},{2,0},{3,1},{4,6},{5,7},{6,4},{7,5},{8,10},{9,11},{10,... | collective-permute-start | bytes 393224 | tf_op jit(solution)/shard_map/ppermute | solution.py:339
  30.3 5.6 %collective-permute-start.5 = (bf16[256,256]{1,0:T(8,128)(2,1)}, bf16[256,256]{1,0:T(8,128)(2,1)S(1)}, u32[]{:S(2)}, u32[]{:S(2)}) collective-permute-start(bf16[256,256]{1,0:T(8,128)(2,1)} %get-tuple-element.18), channel_id=1, source_target_pairs={{0,1},{1,0},{2,3},{3,2},{4,5},{5,4},{6,7},{7,6},{8,9},{9,8},{10,11... | collective-permute-start | bytes 393224 | tf_op jit(solution)/shard_map/ppermute | solution.py:339
  32.5 7.0 %collective-permute-start.7 = (bf16[256,256]{1,0:T(8,128)(2,1)}, bf16[256,256]{1,0:T(8,128)(2,1)S(1)}, u32[]{:S(2)}, u32[]{:S(2)}) collective-permute-start(bf16[256,256]{1,0:T(8,128)(2,1)} %get-tuple-element.20), channel_id=1, source_target_pairs={{0,1},{1,0},{2,3},{3,2},{4,5},{5,4},{6,7},{7,6},{8,9},{9,8},{10,11... | collective-permute-start | bytes 393224 | tf_op jit(solution)/shard_map/ppermute | solution.py:339
  32.5 8.3 %collective-permute-start.9 = (bf16[256,256]{1,0:T(8,128)(2,1)}, bf16[256,256]{1,0:T(8,128)(2,1)S(1)}, u32[]{:S(2)}, u32[]{:S(2)}) collective-permute-start(bf16[256,256]{1,0:T(8,128)(2,1)} %get-tuple-element.22), channel_id=1, source_target_pairs={{0,6},{1,7},{2,4},{3,5},{4,2},{5,3},{6,0},{7,1},{8,14},{9,15},{10,... | collective-permute-start | bytes 393224 | tf_op jit(solution)/shard_map/ppermute | solution.py:339
  36.8 10.3 %collective-permute-start.6 = (bf16[256,256]{1,0:T(8,128)(2,1)S(1)}, bf16[256,256]{1,0:T(8,128)(2,1)S(1)}, u32[]{:S(2)}, u32[]{:S(2)}) collective-permute-start(bf16[256,256]{1,0:T(8,128)(2,1)S(1)} %add_convert_fusion.3), channel_id=1, source_target_pairs={{0,4},{1,5},{2,6},{3,7},{4,0},{5,1},{6,2},{7,3},{8,12},{9,13},{10,... | collective-permute-start | bytes 393224 | tf_op jit(solution)/shard_map/ppermute | solution.py:339
  40.5 6.7 %collective-permute-start.8 = (bf16[256,256]{1,0:T(8,128)(2,1)S(1)}, bf16[256,256]{1,0:T(8,128)(2,1)S(1)}, u32[]{:S(2)}, u32[]{:S(2)}) collective-permute-start(bf16[256,256]{1,0:T(8,128)(2,1)S(1)} %add_convert_fusion.2), channel_id=1, source_target_pairs={{0,2},{1,3},{2,0},{3,1},{4,6},{5,7},{6,4},{7,5},{8,10},{9,11},{10,... | collective-permute-start | bytes 393224 | tf_op jit(solution)/shard_map/ppermute | solution.py:339
  41.8 5.3 %collective-permute-start.10 = (bf16[256,256]{1,0:T(8,128)(2,1)S(1)}, bf16[256,256]{1,0:T(8,128)(2,1)S(1)}, u32[]{:S(2)}, u32[]{:S(2)}) collective-permute-start(bf16[256,256]{1,0:T(8,128)(2,1)S(1)} %add_convert_fusion.1), channel_id=1, source_target_pairs={{0,1},{1,0},{2,3},{3,2},{4,5},{5,4},{6,7},{7,6},{8,9},{9,8},{10,11... | collective-permute-start | bytes 393224 | tf_op jit(solution)/shard_map/ppermute | solution.py:339
  48.3 27.3 %copy-start = (bf16[272,256]{1,0:T(8,128)(2,1)}, bf16[272,256]{1,0:T(8,128)(2,1)S(1)}, u32[]{:S(2)}) copy-start(bf16[272,256]{1,0:T(8,128)(2,1)S(1)} %maximum_maximum_fusion.rest_0_) | copy-start | bytes 417796
  48.3 7.3 %collective-permute-start.14 = (bf16[272,256]{1,0:T(8,128)(2,1)S(1)}, bf16[272,256]{1,0:T(8,128)(2,1)S(1)}, u32[]{:S(2)}, u32[]{:S(2)}) collective-permute-start(bf16[272,256]{1,0:T(8,128)(2,1)S(1)} %maximum_maximum_fusion.rest_0_), channel_id=1, source_target_pairs={{0,4},{1,5},{2,6},{3,7},{4,0},{5,1},{6,2},{7,3},{8,12},{9,13},{10,... | collective-permute-start | bytes 417800 | tf_op jit(solution)/shard_map/ppermute | solution.py:339
  49.2 11.8 %collective-permute-start.18 = (bf16[272,256]{1,0:T(8,128)(2,1)S(1)}, bf16[272,256]{1,0:T(8,128)(2,1)S(1)}, u32[]{:S(2)}, u32[]{:S(2)}) collective-permute-start(bf16[272,256]{1,0:T(8,128)(2,1)S(1)} %maximum_maximum_fusion.rest_0_), channel_id=1, source_target_pairs={{0,24},{8,0},{16,8},{24,16},{1,25},{9,1},{17,9},{25,17},{2,26},{10... | collective-permute-start | bytes 417800 | tf_op jit(solution)/shard_map/ppermute | solution.py:334
  54.2 8.6 %collective-permute-start.12 = (bf16[272,256]{1,0:T(8,128)(2,1)S(1)}, bf16[272,256]{1,0:T(8,128)(2,1)S(1)}, u32[]{:S(2)}, u32[]{:S(2)}) collective-permute-start(bf16[272,256]{1,0:T(8,128)(2,1)S(1)} %maximum_maximum_fusion.rest_0_), channel_id=1, source_target_pairs={{0,2},{1,3},{2,0},{3,1},{4,6},{5,7},{6,4},{7,5},{8,10},{9,11},{10,... | collective-permute-start | bytes 417800 | tf_op jit(solution)/shard_map/ppermute | solution.py:339
  54.2 9.1 %collective-permute-start.11 = (bf16[272,256]{1,0:T(8,128)(2,1)S(1)}, bf16[272,256]{1,0:T(8,128)(2,1)S(1)}, u32[]{:S(2)}, u32[]{:S(2)}) collective-permute-start(bf16[272,256]{1,0:T(8,128)(2,1)S(1)} %maximum_maximum_fusion.rest_0_), channel_id=1, source_target_pairs={{0,1},{1,0},{2,3},{3,2},{4,5},{5,4},{6,7},{7,6},{8,9},{9,8},{10,11... | collective-permute-start | bytes 417800 | tf_op jit(solution)/shard_map/ppermute | solution.py:339
  55.5 20.0 %copy-start.1 = (bf16[272,256]{1,0:T(8,128)(2,1)}, bf16[272,256]{1,0:T(8,128)(2,1)S(1)}, u32[]{:S(2)}) copy-start(bf16[272,256]{1,0:T(8,128)(2,1)S(1)} %collective-permute-done.14.rest_4_) | copy-start | bytes 417796
  55.5 7.8 %collective-permute-start.22 = (bf16[272,256]{1,0:T(8,128)(2,1)S(1)}, bf16[272,256]{1,0:T(8,128)(2,1)S(1)}, u32[]{:S(2)}, u32[]{:S(2)}) collective-permute-start(bf16[272,256]{1,0:T(8,128)(2,1)S(1)} %collective-permute-done.14.rest_4_), channel_id=1, source_target_pairs={{0,24},{8,0},{16,8},{24,16},{1,25},{9,1},{17,9},{25,17},{2,26},{10... | collective-permute-start | bytes 417800 | tf_op jit(solution)/shard_map/ppermute | solution.py:334
  58.1 7.0 %collective-permute-start.16 = (bf16[272,256]{1,0:T(8,128)(2,1)S(1)}, bf16[272,256]{1,0:T(8,128)(2,1)S(1)}, u32[]{:S(2)}, u32[]{:S(2)}) collective-permute-start(bf16[272,256]{1,0:T(8,128)(2,1)S(1)} %collective-permute-done.14.rest_4_), channel_id=1, source_target_pairs={{0,2},{1,3},{2,0},{3,1},{4,6},{5,7},{6,4},{7,5},{8,10},{9,11},{10,... | collective-permute-start | bytes 417800 | tf_op jit(solution)/shard_map/ppermute | solution.py:339
  61.0 14.6 %copy-start.2 = (bf16[272,256]{1,0:T(8,128)(2,1)}, bf16[272,256]{1,0:T(8,128)(2,1)S(1)}, u32[]{:S(2)}) copy-start(bf16[272,256]{1,0:T(8,128)(2,1)S(1)} %collective-permute-done.18.rest_8_) | copy-start | bytes 417796
  61.0 5.6 %collective-permute-start.15 = (bf16[272,256]{1,0:T(8,128)(2,1)S(1)}, bf16[272,256]{1,0:T(8,128)(2,1)S(1)}, u32[]{:S(2)}, u32[]{:S(2)}) collective-permute-start(bf16[272,256]{1,0:T(8,128)(2,1)S(1)} %collective-permute-done.14.rest_4_), channel_id=1, source_target_pairs={{0,1},{1,0},{2,3},{3,2},{4,5},{5,4},{6,7},{7,6},{8,9},{9,8},{10,11... | collective-permute-start | bytes 417800 | tf_op jit(solution)/shard_map/ppermute | solution.py:339
  62.7 12.8 %copy-start.3 = (bf16[272,256]{1,0:T(8,128)(2,1)}, bf16[272,256]{1,0:T(8,128)(2,1)S(1)}, u32[]{:S(2)}) copy-start(bf16[272,256]{1,0:T(8,128)(2,1)S(1)} %collective-permute-done.12.rest_2_) | copy-start | bytes 417796
  62.7 5.0 %collective-permute-start.20 = (bf16[272,256]{1,0:T(8,128)(2,1)S(1)}, bf16[272,256]{1,0:T(8,128)(2,1)S(1)}, u32[]{:S(2)}, u32[]{:S(2)}) collective-permute-start(bf16[272,256]{1,0:T(8,128)(2,1)S(1)} %collective-permute-done.12.rest_2_), channel_id=1, source_target_pairs={{0,24},{8,0},{16,8},{24,16},{1,25},{9,1},{17,9},{25,17},{2,26},{10... | collective-permute-start | bytes 417800 | tf_op jit(solution)/shard_map/ppermute | solution.py:334
  63.3 12.3 %copy-start.4 = (bf16[272,256]{1,0:T(8,128)(2,1)}, bf16[272,256]{1,0:T(8,128)(2,1)S(1)}, u32[]{:S(2)}) copy-start(bf16[272,256]{1,0:T(8,128)(2,1)S(1)} %collective-permute-done.11.rest_1_) | copy-start | bytes 417796
  63.3 6.2 %collective-permute-start.13 = (bf16[272,256]{1,0:T(8,128)(2,1)S(1)}, bf16[272,256]{1,0:T(8,128)(2,1)S(1)}, u32[]{:S(2)}, u32[]{:S(2)}) collective-permute-start(bf16[272,256]{1,0:T(8,128)(2,1)S(1)} %collective-permute-done.12.rest_2_), channel_id=1, source_target_pairs={{0,1},{1,0},{2,3},{3,2},{4,5},{5,4},{6,7},{7,6},{8,9},{9,8},{10,11... | collective-permute-start | bytes 417800 | tf_op jit(solution)/shard_map/ppermute | solution.py:339
  63.3 12.2 %copy-start.5 = (bf16[272,256]{1,0:T(8,128)(2,1)}, bf16[272,256]{1,0:T(8,128)(2,1)S(1)}, u32[]{:S(2)}) copy-start(bf16[272,256]{1,0:T(8,128)(2,1)S(1)} %collective-permute-done.22.rest_12_) | copy-start | bytes 417796
  63.3 7.1 %collective-permute-start.17 = (bf16[272,256]{1,0:T(8,128)(2,1)S(1)}, bf16[272,256]{1,0:T(8,128)(2,1)S(1)}, u32[]{:S(2)}, u32[]{:S(2)}) collective-permute-start(bf16[272,256]{1,0:T(8,128)(2,1)S(1)} %collective-permute-done.11.rest_1_), channel_id=1, source_target_pairs={{0,6},{1,7},{2,4},{3,5},{4,2},{5,3},{6,0},{7,1},{8,14},{9,15},{10,... | collective-permute-start | bytes 417800 | tf_op jit(solution)/shard_map/ppermute | solution.py:339
  65.0 10.5 %copy-start.6 = (bf16[272,256]{1,0:T(8,128)(2,1)}, bf16[272,256]{1,0:T(8,128)(2,1)S(1)}, u32[]{:S(2)}) copy-start(bf16[272,256]{1,0:T(8,128)(2,1)S(1)} %collective-permute-done.16.rest_6_) | copy-start | bytes 417796
  65.0 6.4 %collective-permute-start.19 = (bf16[272,256]{1,0:T(8,128)(2,1)S(1)}, bf16[272,256]{1,0:T(8,128)(2,1)S(1)}, u32[]{:S(2)}, u32[]{:S(2)}) collective-permute-start(bf16[272,256]{1,0:T(8,128)(2,1)S(1)} %collective-permute-done.11.rest_1_), channel_id=1, source_target_pairs={{0,24},{8,0},{16,8},{24,16},{1,25},{9,1},{17,9},{25,17},{2,26},{10... | collective-permute-start | bytes 417800 | tf_op jit(solution)/shard_map/ppermute | solution.py:334
  66.6 9.0 %copy-start.7 = (bf16[272,256]{1,0:T(8,128)(2,1)}, bf16[272,256]{1,0:T(8,128)(2,1)S(1)}, u32[]{:S(2)}) copy-start(bf16[272,256]{1,0:T(8,128)(2,1)S(1)} %collective-permute-done.15.rest_5_) | copy-start | bytes 417796
  66.6 4.8 %collective-permute-start.24 = (bf16[272,256]{1,0:T(8,128)(2,1)S(1)}, bf16[272,256]{1,0:T(8,128)(2,1)S(1)}, u32[]{:S(2)}, u32[]{:S(2)}) collective-permute-start(bf16[272,256]{1,0:T(8,128)(2,1)S(1)} %collective-permute-done.16.rest_6_), channel_id=1, source_target_pairs={{0,24},{8,0},{16,8},{24,16},{1,25},{9,1},{17,9},{25,17},{2,26},{10... | collective-permute-start | bytes 417800 | tf_op jit(solution)/shard_map/ppermute | solution.py:334
  67.7 7.9 %copy-start.8 = (bf16[272,256]{1,0:T(8,128)(2,1)}, bf16[272,256]{1,0:T(8,128)(2,1)S(1)}, u32[]{:S(2)}) copy-start(bf16[272,256]{1,0:T(8,128)(2,1)S(1)} %collective-permute-done.20.rest_10_) | copy-start | bytes 417796
  67.7 4.8 %collective-permute-start.23 = (bf16[272,256]{1,0:T(8,128)(2,1)S(1)}, bf16[272,256]{1,0:T(8,128)(2,1)S(1)}, u32[]{:S(2)}, u32[]{:S(2)}) collective-permute-start(bf16[272,256]{1,0:T(8,128)(2,1)S(1)} %collective-permute-done.15.rest_5_), channel_id=1, source_target_pairs={{0,24},{8,0},{16,8},{24,16},{1,25},{9,1},{17,9},{25,17},{2,26},{10... | collective-permute-start | bytes 417800 | tf_op jit(solution)/shard_map/ppermute | solution.py:334
  69.5 6.1 %copy-start.9 = (bf16[272,256]{1,0:T(8,128)(2,1)}, bf16[272,256]{1,0:T(8,128)(2,1)S(1)}, u32[]{:S(2)}) copy-start(bf16[272,256]{1,0:T(8,128)(2,1)S(1)} %collective-permute-done.13.rest_3_) | copy-start | bytes 417796
  69.5 4.5 %collective-permute-start.21 = (bf16[272,256]{1,0:T(8,128)(2,1)S(1)}, bf16[272,256]{1,0:T(8,128)(2,1)S(1)}, u32[]{:S(2)}, u32[]{:S(2)}) collective-permute-start(bf16[272,256]{1,0:T(8,128)(2,1)S(1)} %collective-permute-done.13.rest_3_), channel_id=1, source_target_pairs={{0,24},{8,0},{16,8},{24,16},{1,25},{9,1},{17,9},{25,17},{2,26},{10... | collective-permute-start | bytes 417800 | tf_op jit(solution)/shard_map/ppermute | solution.py:334
  70.5 5.1 %copy-start.10 = (bf16[272,256]{1,0:T(8,128)(2,1)}, bf16[272,256]{1,0:T(8,128)(2,1)S(1)}, u32[]{:S(2)}) copy-start(bf16[272,256]{1,0:T(8,128)(2,1)S(1)} %collective-permute-done.17.rest_7_) | copy-start | bytes 417796
  70.5 5.1 %collective-permute-start.25 = (bf16[272,256]{1,0:T(8,128)(2,1)S(1)}, bf16[272,256]{1,0:T(8,128)(2,1)S(1)}, u32[]{:S(2)}, u32[]{:S(2)}) collective-permute-start(bf16[272,256]{1,0:T(8,128)(2,1)S(1)} %collective-permute-done.17.rest_7_), channel_id=1, source_target_pairs={{0,24},{8,0},{16,8},{24,16},{1,25},{9,1},{17,9},{25,17},{2,26},{10... | collective-permute-start | bytes 417800 | tf_op jit(solution)/shard_map/ppermute | solution.py:334
  71.4 4.2 %copy-start.11 = (bf16[272,256]{1,0:T(8,128)(2,1)}, bf16[272,256]{1,0:T(8,128)(2,1)S(1)}, u32[]{:S(2)}) copy-start(bf16[272,256]{1,0:T(8,128)(2,1)S(1)} %collective-permute-done.19.rest_9_) | copy-start | bytes 417796
  71.4 4.2 %copy-start.12 = (bf16[272,256]{1,0:T(8,128)(2,1)}, bf16[272,256]{1,0:T(8,128)(2,1)S(1)}, u32[]{:S(2)}) copy-start(bf16[272,256]{1,0:T(8,128)(2,1)S(1)} %collective-permute-done.24.rest_14_) | copy-start | bytes 417796
  72.5 3.1 %copy-start.13 = (bf16[272,256]{1,0:T(8,128)(2,1)}, bf16[272,256]{1,0:T(8,128)(2,1)S(1)}, u32[]{:S(2)}) copy-start(bf16[272,256]{1,0:T(8,128)(2,1)S(1)} %collective-permute-done.23.rest_13_) | copy-start | bytes 417796
  74.0 1.6 %copy-start.14 = (bf16[272,256]{1,0:T(8,128)(2,1)}, bf16[272,256]{1,0:T(8,128)(2,1)S(1)}, u32[]{:S(2)}) copy-start(bf16[272,256]{1,0:T(8,128)(2,1)S(1)} %collective-permute-done.21.rest_11_) | copy-start | bytes 417796
  75.5 0.7 copy-start.15
